TPU v7x, 32 devices: a whole 2x2x4 slice. The times are simulated.
32 devices in a mesh: wide: 8 (over z, y), narrow: 4 (over x, core).
Axes of the slice: x: 2, y: 2, z: 4, core: 2. Of those that a mesh axis runs over, the one named last changes fastest.
Arguments:
- tokens: bfloat16 [8192, 2048], P('wide'), may hold values from -6 to 6
- seq_lengths: int32 [8, 4], P('wide'), may hold values from 1 to 768, 1024 in all within a row
- attn_gain: float32 [2048], replicated, may hold values from 0.1 to 1.9
- w_query: bfloat16 [2048, 2048], P(None, 'narrow'), may hold values from -0.125 to 0.125
- key_weight: bfloat16 [2048, 1024], P(None, 'narrow'), may hold values from -0.125 to 0.125
- value_weight: bfloat16 [2048, 1024], P(None, 'narrow'), may hold values from -0.125 to 0.125
- query_gain: float32 [128], replicated, may hold values from 0.1 to 1.9
- key_norm_gain: float32 [128], replicated, may hold values from 0.1 to 1.9
- w_output: bfloat16 [2048, 2048], P('narrow'), may hold values from -0.5 to 0.5
- mlp_gain: float32 [2048], replicated, may hold values from 0.1 to 1.9
- w_gate: bfloat16 [2048, 6144], P(None, 'narrow'), may hold values from -0.125 to 0.125
- w_up: bfloat16 [2048, 6144], P(None, 'narrow'), may hold values from -0.125 to 0.125
- w_down: bfloat16 [6144, 2048], P('narrow'), may hold values from -0.078125 to 0.078125
- cotangent: bfloat16 [8192, 2048], P('wide'), may hold values from -6 to 6
Outputs:
- output: bfloat16 [8192, 2048], P('wide')
- grad_tokens: bfloat16 [8192, 2048], P('wide')
- grad_attn_gain: float32 [2048], P('wide')
- grad_w_query: float32 [2048, 2048], P('wide', 'narrow')
- grad_w_key: float32 [2048, 1024], P('wide', 'narrow')
- grad_w_value: float32 [2048, 1024], P('wide', 'narrow')
- grad_query_gain: float32 [128], P('wide')
- grad_key_gain: float32 [128], P('wide')
- grad_w_output: float32 [2048, 2048], P('narrow', 'wide')
- grad_mlp_gain: float32 [2048], P('wide')
- grad_w_gate: float32 [2048, 6144], P('wide', 'narrow')
- grad_w_up: float32 [2048, 6144], P('wide', 'narrow')
- grad_w_down: float32 [6144, 2048], P('narrow', 'wide')
Inputs may be any that keep to these rules, and one draw needn't show every extreme that they name: `seq_lengths`: each row's 4 lengths sum to 1024, and the longest of each row is 768.
All inputs are finite; a program needn't handle non-finite values.
Results may differ from a plain program's by a relative error of at most 0.015.
Values sent between devices are 32-bit elements; how exact they have to be, the bound alone decides.
A program may use at most 256 MiB of HBM per device.

v0:
```python
import jax
import jax.numpy as jnp
from jax import lax
from jax.sharding import PartitionSpec as P

norm_eps = 1e-06
rope_base = 1000000.0
masked_score = -1e30


def root_mean_scale(values, gain):
    return values * lax.rsqrt(jnp.mean(values * values, axis=-1, keepdims=True) + norm_eps) * gain


def rotate_pairs(values, cosine_table, sine_table):
    half_width = values.shape[-1] // 2
    turned = jnp.concatenate([-values[..., half_width:], values[..., :half_width]], axis=-1)
    return values * cosine_table + turned * sine_table


def layout(seq_lengths, row_len):
    seq_ends = jnp.cumsum(seq_lengths, axis=-1)
    starts = seq_ends - seq_lengths
    places = jnp.arange(row_len, dtype=jnp.int32)
    segment_index = jnp.sum(
        (places[None, :, None] >= seq_ends[:, None, :]).astype(jnp.int32), axis=-1
    )
    belongs = (
        segment_index[:, :, None]
        == jnp.arange(seq_lengths.shape[-1], dtype=jnp.int32)[None, None, :]
    )
    seq_start = jnp.sum(jnp.where(belongs, starts[:, None, :], 0), axis=-1)
    return (segment_index, places[None, :] - seq_start)


def tables(token_positions, head_dim):
    half_width = head_dim // 2
    frequency = rope_base ** (-2.0 * jnp.arange(half_width, dtype=jnp.float32) / head_dim)
    angles = token_positions.astype(jnp.float32)[:, None] * frequency[None, :]
    angles = jnp.concatenate([angles, angles], axis=-1)
    return (jnp.cos(angles)[:, None, :], jnp.sin(angles)[:, None, :])


def swiglu(gate_act, up_act):
    return jax.nn.silu(gate_act) * up_act


def forward_dot(left_side, right_side):
    return jnp.dot(left_side, right_side, preferred_element_type=jnp.float32)


def outer_sum(left_side, right_side):
    return lax.dot_general(
        left_side, right_side, (((0,), (0,)), ((), ())), preferred_element_type=jnp.float32
    )


def back_dot(left_side, right_side):
    return lax.dot_general(
        left_side, right_side, (((1,), (1,)), ((), ())), preferred_element_type=jnp.float32
    )


def score_block(query_low, key_low, allowed, score_scale):
    scores = (
        jnp.einsum("tkgd,skd->kgts", query_low, key_low, preferred_element_type=jnp.float32)
        * score_scale
    )
    return jnp.where(allowed[None, None], scores, masked_score)


def per_device(
    tokens,
    seq_lengths,
    attn_gain,
    w_query,
    key_weight,
    value_weight,
    query_gain,
    key_norm_gain,
    w_output,
    mlp_gain,
    w_gate,
    w_up,
    w_down,
    cotangent,
):
    token_count = tokens.shape[0]
    head_dim = query_gain.shape[0]
    kv_heads = key_weight.shape[1] // head_dim
    q_heads = w_query.shape[1] // head_dim
    group_width = q_heads // kv_heads
    score_scale = head_dim ** (-0.5)
    segment_index, token_positions = layout(seq_lengths, token_count)
    segment_index = segment_index.reshape(-1)
    token_positions = token_positions.reshape(-1)
    allowed = (segment_index[:, None] == segment_index[None, :]) & (
        token_positions[:, None] >= token_positions[None, :]
    )
    cosine_table, sine_table = tables(token_positions, head_dim)

    def prepare(raw_heads, gain):
        return rotate_pairs(root_mean_scale(raw_heads, gain), cosine_table, sine_table)

    tokens32 = tokens.astype(jnp.float32)
    normed32, norm_pull = jax.vjp(root_mean_scale, tokens32, attn_gain)
    normed = normed32.astype(jnp.bfloat16)
    query_proj = forward_dot(normed, w_query)
    key_projected = forward_dot(normed, key_weight)
    value_low = (
        forward_dot(normed, value_weight)
        .astype(jnp.bfloat16)
        .reshape(token_count, kv_heads, head_dim)
    )
    query32, query_pull = jax.vjp(
        prepare, query_proj.reshape(token_count, q_heads, head_dim), query_gain
    )
    key32, key_pull = jax.vjp(
        prepare, key_projected.reshape(token_count, kv_heads, head_dim), key_norm_gain
    )
    query_low = query32.astype(jnp.bfloat16).reshape(token_count, kv_heads, group_width, head_dim)
    key_low = key32.astype(jnp.bfloat16)
    scores = score_block(query_low, key_low, allowed, score_scale)
    top_score = jnp.max(scores, axis=-1, keepdims=True)
    expd = jnp.exp(scores - top_score)
    row_total = jnp.sum(expd, axis=-1, keepdims=True)
    probs_low = (expd / row_total).astype(jnp.bfloat16)
    log_total = top_score + jnp.log(row_total)
    mixed_heads = jnp.einsum(
        "kgts,skd->tkgd", probs_low, value_low, preferred_element_type=jnp.float32
    )
    context = mixed_heads.reshape(token_count, q_heads * head_dim).astype(jnp.bfloat16)
    attn_branch = lax.psum(forward_dot(context, w_output), "narrow")
    hidden = tokens32 + attn_branch
    mlp32, mlp_pull = jax.vjp(root_mean_scale, hidden, mlp_gain)
    mlp_in = mlp32.astype(jnp.bfloat16)
    gate_act = forward_dot(mlp_in, w_gate)
    up_act = forward_dot(mlp_in, w_up)
    inner32, swiglu_pull = jax.vjp(swiglu, gate_act, up_act)
    inner_act = inner32.astype(jnp.bfloat16)
    mlp_branch = lax.psum(forward_dot(inner_act, w_down), "narrow")
    output = (hidden + mlp_branch).astype(jnp.bfloat16)
    grad_y = cotangent.astype(jnp.float32)
    grad_w_down = outer_sum(inner_act, cotangent)
    grad_inner = back_dot(cotangent, w_down)
    grad_gate32, grad_up32 = swiglu_pull(grad_inner)
    grad_gate = grad_gate32.astype(jnp.bfloat16)
    grad_up = grad_up32.astype(jnp.bfloat16)
    grad_w_gate = outer_sum(mlp_in, grad_gate)
    grad_w_up = outer_sum(mlp_in, grad_up)
    mlp_part = back_dot(grad_gate, w_gate) + back_dot(grad_up, w_up)
    grad_mlp_in = lax.psum(mlp_part, "narrow")
    grad_hidden_norm, grad_mlp_gain = mlp_pull(grad_mlp_in)
    grad_hidden = grad_y + grad_hidden_norm
    attn_low = grad_hidden.astype(jnp.bfloat16)
    grad_w_output = outer_sum(context, attn_low)
    grad_context = (
        back_dot(attn_low, w_output)
        .astype(jnp.bfloat16)
        .reshape(token_count, kv_heads, group_width, head_dim)
    )
    again = score_block(query_low, key_low, allowed, score_scale)
    probs = jnp.exp(again - log_total)
    again_low = probs.astype(jnp.bfloat16)
    grad_value = jnp.einsum(
        "kgts,tkgd->skd", again_low, grad_context, preferred_element_type=jnp.float32
    )
    grad_probs = jnp.einsum(
        "tkgd,skd->kgts", grad_context, value_low, preferred_element_type=jnp.float32
    )
    grad_scores = probs * (grad_probs - jnp.sum(probs * grad_probs, axis=-1, keepdims=True))
    scores_low = grad_scores.astype(jnp.bfloat16)
    grad_query_heads = (
        jnp.einsum("kgts,skd->tkgd", scores_low, key_low, preferred_element_type=jnp.float32)
        * score_scale
    )
    grad_key_heads = (
        jnp.einsum("kgts,tkgd->skd", scores_low, query_low, preferred_element_type=jnp.float32)
        * score_scale
    )
    grad_query32, query_gain_part = query_pull(
        grad_query_heads.reshape(token_count, q_heads, head_dim)
    )
    grad_key32, key_gain_part = key_pull(grad_key_heads)
    grad_query_proj = grad_query32.reshape(token_count, q_heads * head_dim).astype(jnp.bfloat16)
    grad_key_proj = grad_key32.reshape(token_count, kv_heads * head_dim).astype(jnp.bfloat16)
    grad_value_low = grad_value.reshape(token_count, kv_heads * head_dim).astype(jnp.bfloat16)
    grad_w_query = outer_sum(normed, grad_query_proj)
    grad_w_key = outer_sum(normed, grad_key_proj)
    grad_w_value = outer_sum(normed, grad_value_low)
    attn_part = (
        back_dot(grad_query_proj, w_query)
        + back_dot(grad_key_proj, key_weight)
        + back_dot(grad_value_low, value_weight)
    )
    grad_normed, query_gain_sum, key_gain_sum = lax.psum(
        (attn_part, query_gain_part, key_gain_part), "narrow"
    )
    grad_tokens_norm, grad_attn_gain = norm_pull(grad_normed)
    grad_tokens = (grad_hidden + grad_tokens_norm).astype(jnp.bfloat16)
    (
        grad_tokens,
        grad_attn_gain,
        grad_w_query,
        grad_w_key,
        grad_w_value,
        query_gain_sum,
        key_gain_sum,
        grad_w_output,
    ) = (
        grad_tokens,
        grad_attn_gain,
        grad_w_query,
        grad_w_key,
        grad_w_value,
        query_gain_sum,
        key_gain_sum,
        grad_w_output,
    )
    (
        shard_attn_gain,
        shard_query,
        shard_key,
        shard_value,
        shard_query_gain,
        shard_key_gain,
        shard_output,
        shard_mlp_gain,
        shard_gate,
        shard_up,
        shard_down,
    ) = (
        lax.psum_scatter(grad_attn_gain, "wide", scatter_dimension=0, tiled=True),
        lax.psum_scatter(grad_w_query, "wide", scatter_dimension=0, tiled=True),
        lax.psum_scatter(grad_w_key, "wide", scatter_dimension=0, tiled=True),
        lax.psum_scatter(grad_w_value, "wide", scatter_dimension=0, tiled=True),
        lax.psum_scatter(query_gain_sum, "wide", scatter_dimension=0, tiled=True),
        lax.psum_scatter(key_gain_sum, "wide", scatter_dimension=0, tiled=True),
        lax.psum_scatter(grad_w_output, "wide", scatter_dimension=1, tiled=True),
        lax.psum_scatter(grad_mlp_gain, "wide", scatter_dimension=0, tiled=True),
        lax.psum_scatter(grad_w_gate, "wide", scatter_dimension=0, tiled=True),
        lax.psum_scatter(grad_w_up, "wide", scatter_dimension=0, tiled=True),
        lax.psum_scatter(grad_w_down, "wide", scatter_dimension=1, tiled=True),
    )
    return (
        output,
        grad_tokens,
        shard_attn_gain,
        shard_query,
        shard_key,
        shard_value,
        shard_query_gain,
        shard_key_gain,
        shard_output,
        shard_mlp_gain,
        shard_gate,
        shard_up,
        shard_down,
    )


def solution(mesh):
    return jax.shard_map(
        per_device,
        mesh=mesh,
        in_specs=(
            P("wide", None),
            P("wide", None),
            P(),
            P(None, "narrow"),
            P(None, "narrow"),
            P(None, "narrow"),
            P(),
            P(),
            P("narrow", None),
            P(),
            P(None, "narrow"),
            P(None, "narrow"),
            P("narrow", None),
            P("wide", None),
        ),
        out_specs=(
            P("wide", None),
            P("wide", None),
            P("wide"),
            P("wide", "narrow"),
            P("wide", "narrow"),
            P("wide", "narrow"),
            P("wide"),
            P("wide"),
            P("narrow", "wide"),
            P("wide"),
            P("wide", "narrow"),
            P("wide", "narrow"),
            P("narrow", "wide"),
        ),
        check_vma=False,
    )
```

profile of v0, /device:TPU:0, one launch (start us, length us, event | category | flops | bytes accessed | tf_op | source)
XLA Modules:
  0.0 1767.0 jit_solution(1844320383201942213)
XLA Ops:
  32.2 7.7 fusion.55
  40.0 8.0 fusion.3
  48.0 7.8 fusion.31
  62.5 155.7 %all-reduce.15.cloned.1.call-done = f32[1024,2048]{1,0:T(8,128)} async-done(((f32[1024,2048]{1,0:T(8,128)}), f32[1024,2048]{1,0:T(8,128)}) %all-reduce.15.cloned.1.call-update) | async-done | bytes 8388624 | tf_op jit(solution)/shard_map/psum | solution.py:133
  227.1 12.0 fusion.58
  239.1 10.7 fusion.57
  249.8 15.3 multiply_convert_fusion.1
  265.1 10.0 fusion.60
  275.1 10.9 convolution_add_fusion
  286.2 11.9 fusion.59
  298.1 141.2 %all-reduce.17.cloned.1.call-done = f32[1024,2048]{1,0:T(8,128)} async-done(((f32[1024,2048]{1,0:T(8,128)}), f32[1024,2048]{1,0:T(8,128)}) %all-reduce.17.cloned.1.call-update) | async-done | bytes 8388624 | tf_op jit(solution)/shard_map/psum | solution.py:152
  439.3 7.1 multiply_reduce_fusion
  446.5 9.8 fusion.9
  456.2 7.6 fusion.32
  468.3 11.2 fusion
  479.6 8.5 fusion.2
  492.8 6.4 broadcast_multiply_fusion
  522.2 8.2 fusion.27
  530.5 6.7 fusion.63
  537.3 12.2 fusion.68
  549.7 12.4 fusion.67
  562.3 12.6 fusion.66
  577.4 223.2 %all-reduce.19.cloned.1.call-done = (f32[1024,2048]{1,0:T(8,128)}, f32[1024,2048]{1,0:T(8,128)}) async-done(((f32[1024,2048]{1,0:T(8,128)}, f32[1024,2048]{1,0:T(8,128)}), (f32[1024,2048]{1,0:T(8,128)}, f32[1024,2048]{1,0:T(8,128)})) %all-reduce.19.cloned.1.call-update) | async-done | bytes 16777232 | tf_op jit(solution)/shard_map/psum | solution.py:141
  806.7 37.6 %all-reduce.8 = (f32[2048]{0:T(1024)S(1)}, f32[128]{0:T(128)S(1)}, f32[128]{0:T(128)S(1)}, f32[2048]{0:T(1024)S(1)}) all-reduce(f32[2048]{0:T(1024)S(1)} %get-tuple-element.15, f32[128]{0:T(128)S(1)} %get-tuple-element.17, f32[128]{0:T(128)S(1)} %copy-done.51, ...), channel_id=2, replica_groups=mesh['wide'=8,'narrow'=4] {'wide'}, use_global_device_ids=true, to_apply=%region_19.20.clone | all-reduce | flops 4352 | bytes 34816
  845.8 6.4 all-reduce.9
  852.2 18.3 %fusion.11 = (bf16[1024,2048]{1,0:T(8,128)(2,1)}, bf16[1024,2048]{1,0:T(8,128)(2,1)}) fusion(f32[1024,2048]{1,0:T(8,128)} %fusion.9, bf16[1024,2048]{1,0:T(8,128)(2,1)} %param.14, f32[1024,2048]{1,0:T(8,128)} %get-tuple-element.28, f32[1024]{0:T(1024)S(1)} %multiply_multiply_fusion.4, f32[2048]{0:T(1024)S(1)} %copy-done.38, f32[1024]{0:T(1024)S(1)} %copy-done.42, ...), kind=kLoop, calls=%fused_computation.25 | loop fusion | flops 20971520 | bytes 46153728 | tf_op jit(solution)/shard_map/convert_element_type | solution.py:200
  872.4 70.9 %reduce-scatter.10.cloned.1.call-done = f32[256,256]{1,0:T(8,128)} async-done(((f32[2048,256]{1,0:T(8,128)}), f32[256,256]{1,0:T(8,128)}) %reduce-scatter.10.cloned.1.call-update) | async-done | bytes 262160 | tf_op jit(solution)/shard_map/reduce_scatter | solution.py:235
  943.2 91.4 %reduce-scatter.14.cloned.1.call-done = f32[512,256]{1,0:T(8,128)} async-done(((f32[512,2048]{1,0:T(8,128)}), f32[512,256]{1,0:T(8,128)}) %reduce-scatter.14.cloned.1.call-update) | async-done | bytes 524304 | tf_op jit(solution)/shard_map/reduce_scatter | solution.py:239
  1034.6 92.5 %reduce-scatter.8.cloned.1.call-done = f32[256,512]{1,0:T(8,128)} async-done(((f32[2048,512]{1,0:T(8,128)}), f32[256,512]{1,0:T(8,128)}) %reduce-scatter.8.cloned.1.call-update) | async-done | bytes 524304 | tf_op jit(solution)/shard_map/reduce_scatter | solution.py:234
  1127.1 211.7 %reduce-scatter.20.cloned.1.call-done = f32[1536,256]{1,0:T(8,128)} async-done(((f32[1536,2048]{1,0:T(8,128)}), f32[1536,256]{1,0:T(8,128)}) %reduce-scatter.20.cloned.1.call-update) | async-done | bytes 1572880 | tf_op jit(solution)/shard_map/reduce_scatter | solution.py:243
  1338.9 210.6 %reduce-scatter.18.cloned.1.call-done = f32[256,1536]{1,0:T(8,128)} async-done(((f32[2048,1536]{1,0:T(8,128)}), f32[256,1536]{1,0:T(8,128)}) %reduce-scatter.18.cloned.1.call-update) | async-done | bytes 1572880 | tf_op jit(solution)/shard_map/reduce_scatter | solution.py:242
  1549.5 210.5 %reduce-scatter.16.cloned.1.call-done = f32[256,1536]{1,0:T(8,128)} async-done(((f32[2048,1536]{1,0:T(8,128)}), f32[256,1536]{1,0:T(8,128)}) %reduce-scatter.16.cloned.1.call-update) | async-done | bytes 1572880 | tf_op jit(solution)/shard_map/reduce_scatter | solution.py:241
  (199 shorter events, 83.3 us)
Async XLA Ops:
  7.2 16.9 copy-start
  7.2 10.9 copy-start.37
  7.2 211.0 %all-reduce.15.cloned.1.call-start = ((), (), s32[]{:S(2)}) async-start(), calls=%async_computation.7 | async-start | bytes 16777216 | tf_op jit(solution)/shard_map/psum | solution.py:133
  8.2 9.9 copy-start.2
  13.0 8.4 copy-start.41
  22.7 8.2 copy-start.6
  22.7 8.1 copy-start.34
  31.4 8.6 copy-start.22
  48.0 8.8 copy-start.52
  62.5 161.5 %copy-start.36 = (f32[2048]{0:T(1024)S(1)}, f32[2048]{0:T(1024)}, u32[]{:S(2)}) copy-start(f32[2048]{0:T(1024)} %param.23) | copy-start | bytes 24580
  62.5 376.8 %all-reduce.17.cloned.1.call-start = ((), (), s32[]{:S(2)}) async-start(), calls=%async_computation.8 | async-start | bytes 16777216 | tf_op jit(solution)/shard_map/psum | solution.py:152
  227.1 12.0 copy-start.15
  239.1 10.7 copy-start.13
  265.1 10.0 copy-start.56
  265.1 10.0 copy-start.57
  286.1 514.5 %all-reduce.19.cloned.1.call-start = ((), (), s32[]{:S(2)}) async-start(), calls=%async_computation.16 | async-start | bytes 33554432 | tf_op jit(solution)/shard_map/psum | solution.py:141
  446.4 9.8 copy-start.53
  446.4 17.4 slice-start
  446.4 17.4 slice-start.1
  446.4 17.4 slice-start.2
  479.5 11.8 copy-start.23
  511.4 360.9 %reduce-scatter.12.cloned.1.call-start = ((), (), s32[]{:S(2)}) async-start(), calls=%async_computation.11 | async-start | bytes 2359296 | tf_op jit(solution)/shard_map/reduce_scatter | solution.py:236
  516.8 426.5 %reduce-scatter.10.cloned.1.call-start = ((), (), s32[]{:S(2)}) async-start(), calls=%async_computation.10 | async-start | bytes 2359296 | tf_op jit(solution)/shard_map/reduce_scatter | solution.py:235
  522.2 8.4 copy-start.30
  522.2 512.4 %reduce-scatter.14.cloned.1.call-start = ((), (), s32[]{:S(2)}) async-start(), calls=%async_computation.12 | async-start | bytes 4718592 | tf_op jit(solution)/shard_map/reduce_scatter | solution.py:239
  530.5 596.6 %reduce-scatter.8.cloned.1.call-start = ((), (), s32[]{:S(2)}) async-start(), calls=%async_computation.9 | async-start | bytes 4718592 | tf_op jit(solution)/shard_map/reduce_scatter | solution.py:234
  537.2 801.7 %reduce-scatter.20.cloned.1.call-start = ((), (), s32[]{:S(2)}) async-start(), calls=%async_computation.15 | async-start | bytes 14155776 | tf_op jit(solution)/shard_map/reduce_scatter | solution.py:243
  549.5 999.9 %reduce-scatter.18.cloned.1.call-start = ((), (), s32[]{:S(2)}) async-start(), calls=%async_computation.14 | async-start | bytes 14155776 | tf_op jit(solution)/shard_map/reduce_scatter | solution.py:242
  562.2 1197.7 %reduce-scatter.16.cloned.1.call-start = ((), (), s32[]{:S(2)}) async-start(), calls=%async_computation.13 | async-start | bytes 14155776 | tf_op jit(solution)/shard_map/reduce_scatter | solution.py:241
  574.8 225.7 %copy-start.38 = (f32[2048]{0:T(1024)S(1)}, f32[2048]{0:T(1024)}, u32[]{:S(2)}) copy-start(f32[2048]{0:T(1024)} %param.16) | copy-start | bytes 24580
  574.9 225.7 %copy-start.42 = (f32[1024]{0:T(1024)S(1)}, f32[1024]{0:T(1024)}, u32[]{:S(2)}) copy-start(f32[1024]{0:T(1024)} %copy-done.41) | copy-start | bytes 12292
  800.6 51.6 %copy-start.44 = (f32[1024]{0:T(1024)S(1)}, f32[1024]{0:T(1024)}, u32[]{:S(2)}) copy-start(f32[1024]{0:T(1024)} %copy-done.43) | copy-start | bytes 12292
  (40 other events, 134.6 us)
Sparse Core Ops, SparseCore 0:
  62.6 155.5 all-reduce.14
  286.2 153.0 all-reduce.16
  511.6 288.9 all-reduce.18
  804.5 67.7 reduce-scatter.11
  876.3 66.8 reduce-scatter.9
  947.3 87.2 reduce-scatter.13
  1039.2 87.8 reduce-scatter.7
  1131.3 207.5 reduce-scatter.19
  1343.0 206.3 reduce-scatter.17
  1553.5 206.4 reduce-scatter.15
where the time goes:
time: 1780 us; the launch traced here: 1770 us
  waiting for transfers between devices  1410 us (79%)
  matrix products  201 us (11%)
  other arithmetic  84.1 us (5%)
  blocking collectives  44.1 us (2%)
    psum x1, waiting for transfers between devices, per_device(): mlp_branch = lax.psum(forward_dot(inner_act, w_down), 'narrow')  223 us
    reduce_scatter x1, waiting for transfers between devices, per_device(): lax.psum_scatter(grad_w_down, 'wide', scatter_dimension=1, tiled=True)  212 us
    reduce_scatter x1, waiting for transfers between devices, per_device(): lax.psum_scatter(grad_w_up, 'wide', scatter_dimension=0, tiled=True)  211 us
    reduce_scatter x1, waiting for transfers between devices, per_device(): lax.psum_scatter(grad_w_gate, 'wide', scatter_dimension=0, tiled=True)  210 us
    psum x1, waiting for transfers between devices, per_device(): attn_branch = lax.psum(forward_dot(context, w_output), 'narrow')  156 us
    psum x1, waiting for transfers between devices, per_device(): grad_mlp_in = lax.psum(mlp_part, 'narrow')  141 us
    reduce_scatter x1, waiting for transfers between devices, per_device(): lax.psum_scatter(grad_w_query, 'wide', scatter_dimension=0, tiled=True)  92.5 us
    reduce_scatter x1, waiting for transfers between devices, per_device(): lax.psum_scatter(grad_w_output, 'wide', scatter_dimension=1, tiled=True)  91.4 us
  transfers between devices with their start and end apart: 10, of which 10 were waited for; matrix products, arithmetic and copies ran while one was open for 6% of the time, Pallas kernels for 0%

commit v1 on v0

v1 whole, which is shorter than its diff:
```python
import jax
import jax.numpy as jnp
from jax import lax
from jax.experimental import pallas as pl
from jax.experimental.pallas import tpu as pltpu
from jax.sharding import PartitionSpec as P

norm_eps = 1e-06
rope_base = 1000000.0
masked_score = -1e30
bf16 = jnp.bfloat16
f32 = jnp.float32


def inverse_rms(values):
    return lax.rsqrt(jnp.mean(values * values, axis=-1, keepdims=True) + norm_eps)


def root_mean_scale(values, gain):
    return values * inverse_rms(values) * gain


def rotate_pairs(values, cosine_table, sine_table):
    half_width = values.shape[-1] // 2
    turned = jnp.concatenate([-values[..., half_width:], values[..., :half_width]], axis=-1)
    return values * cosine_table + turned * sine_table


def layout(seq_lengths, row_len):
    seq_ends = jnp.cumsum(seq_lengths, axis=-1)
    starts = seq_ends - seq_lengths
    places = jnp.arange(row_len, dtype=jnp.int32)
    segment_index = jnp.sum(
        (places[None, :, None] >= seq_ends[:, None, :]).astype(jnp.int32), axis=-1
    )
    belongs = (
        segment_index[:, :, None]
        == jnp.arange(seq_lengths.shape[-1], dtype=jnp.int32)[None, None, :]
    )
    seq_start = jnp.sum(jnp.where(belongs, starts[:, None, :], 0), axis=-1)
    return (segment_index, places[None, :] - seq_start)


def tables(token_positions, head_dim):
    half_width = head_dim // 2
    frequency = rope_base ** (-2.0 * jnp.arange(half_width, dtype=f32) / head_dim)
    angles = token_positions.astype(f32)[:, None] * frequency[None, :]
    angles = jnp.concatenate([angles, angles], axis=-1)
    return (jnp.cos(angles)[:, None, :], jnp.sin(angles)[:, None, :])


def swiglu(gate_act, up_act):
    return jax.nn.silu(gate_act) * up_act


def forward_dot(left_side, right_side):
    return jnp.dot(left_side, right_side, preferred_element_type=f32)


def outer_sum(left_side, right_side):
    return lax.dot_general(
        left_side, right_side, (((0,), (0,)), ((), ())), preferred_element_type=f32
    )


def back_dot(left_side, right_side):
    return lax.dot_general(
        left_side, right_side, (((1,), (1,)), ((), ())), preferred_element_type=f32
    )


def score_block(query_low, key_low, allowed, score_scale):
    scores = (
        jnp.einsum("tkgd,skd->kgts", query_low, key_low, preferred_element_type=f32)
        * score_scale
    )
    return jnp.where(allowed[None, None], scores, masked_score)


MESH = pl.DeviceIdType.MESH
any_space = pl.BlockSpec(memory_space=pl.ANY)
in_vmem = pl.BlockSpec(memory_space=pltpu.VMEM)


def nt_dot(left_side, right_side):
    return lax.dot_general(
        left_side, right_side, (((1,), (1,)), ((), ())), preferred_element_type=f32
    )


def fetch(source, target, sem):
    copy = pltpu.make_async_copy(source, target, sem)
    copy.start()
    return copy


class Spot:
    def __init__(self, wide):
        self.line = wide // 2
        self.w = lax.axis_index("wide")
        self.n = lax.axis_index("narrow")
        self.spot = lax.div(self.w, 2)
        self.side = lax.rem(self.w, 2)
        self.core = lax.rem(self.n, 2)
        self.chip = lax.div(self.n, 2)
        self.to_core = {"narrow": self.n + 1 - 2 * self.core}
        self.to_chip = {"narrow": self.n + 2 - 4 * self.chip}
        self.to_side = {"wide": self.w + 1 - 2 * self.side}
        self.to_up = {"wide": self.w + 2}
        self.to_down = {"wide": self.w - 2}

    def greet(self, wide_too):
        barrier = pltpu.get_barrier_semaphore()

        def tell(who):
            pl.semaphore_signal(barrier, inc=1, device_id=who, device_id_type=MESH)

        tell(self.to_core)
        tell(self.to_chip)
        if wide_too:
            tell(self.to_side)
            pl.when(self.spot > 0)(lambda: tell(self.to_down))
            pl.when(self.spot < self.line - 1)(lambda: tell(self.to_up))
        peers = 2
        if wide_too:
            ends = (self.spot == 0).astype(jnp.int32) + (self.spot == self.line - 1).astype(jnp.int32)
            peers = 5 - ends
        pl.semaphore_wait(barrier, peers)


def remote(source, target, send, recv, who):
    return pltpu.make_async_remote_copy(
        src_ref=source, dst_ref=target, send_sem=send, recv_sem=recv,
        device_id=who, device_id_type=MESH,
    )


class WideSum:
    ahead = 4

    @staticmethod
    def lands(tiles, line, rows, cols):
        return [
            jax.ShapeDtypeStruct((tiles, line, 2, rows, cols), f32),
            jax.ShapeDtypeStruct((tiles, line, rows, cols), f32),
            jax.ShapeDtypeStruct((tiles, line, rows, cols), f32),
            jax.ShapeDtypeStruct((tiles, line, rows, cols), f32),
            jax.ShapeDtypeStruct((tiles, rows, cols), f32),
        ]

    @staticmethod
    def sems(tiles):
        dma = pltpu.SemaphoreType.DMA
        return [dma((tiles,)), dma((tiles,)), dma((2,)), dma((tiles,)), dma((2,)), dma((tiles,)), dma((6,))]

    @staticmethod
    def buffers(line, rows, cols):
        tile = (line, rows, cols)
        return [
            pltpu.VMEM(tile, f32),
            pltpu.VMEM(tile, f32),
            pltpu.VMEM((line + 3,) + tile, f32),
            pltpu.VMEM((2, line - 1, rows, cols), f32),
            pltpu.VMEM((2, line - 1, rows, cols), f32),
            pltpu.VMEM((line - 1, rows, cols), f32),
            pltpu.VMEM((line - 1, rows, cols), f32),
            pltpu.VMEM((3, rows, cols), f32),
        ]

    def __init__(self, me, lands, sems):
        self.me = me
        self.parts, self.y_land, self.up_land, self.down_land, self.result = lands
        (self.y_send, self.y_recv, self.up_send, self.up_recv,
         self.down_send, self.down_recv, self.local) = sems
        self.tiles, self.line = self.parts.shape[0], me.line

    def y_copy(self, tile):
        return remote(
            self.parts.at[tile, :, 1 - self.me.side], self.y_land.at[tile],
            self.y_send.at[tile], self.y_recv.at[tile], self.me.to_side,
        )

    def up_copy(self, tile, count):
        slot = lax.rem(tile, 2)
        return remote(
            self.up_buf.at[slot, 0:count], self.up_land.at[tile, 0:count],
            self.up_send.at[slot], self.up_recv.at[tile], self.me.to_up,
        )

    def down_copy(self, tile, count):
        slot = lax.rem(tile, 2)
        return remote(
            self.down_buf.at[slot, 0:count], self.down_land.at[tile, 0:count],
            self.down_send.at[slot], self.down_recv.at[tile], self.me.to_down,
        )

    def await_up(self, tile, count):
        land = self.up_land.at[tile, 0:count]
        remote(land, land, self.up_send.at[0], self.up_recv.at[tile], self.me.to_up).wait_recv()

    def await_down(self, tile, count):
        land = self.down_land.at[tile, 0:count]
        remote(
            land, land, self.down_send.at[0], self.down_recv.at[tile], self.me.to_down
        ).wait_recv()

    @property
    def slots(self):
        return self.tiles + self.line + 2

    def use(self, buffers):
        (self.own, self.got, self.ring, self.up_buf, self.down_buf,
         self.up_load, self.down_load, self.last) = buffers

    def step(self, s):
        me, line, tiles = self.me, self.line, self.tiles
        depth = self.ring.shape[0]

        @pl.when(s + self.ahead < tiles)
        def _():
            self.y_copy(s + self.ahead).start()

        @pl.when(s < tiles)
        def _():
            self.y_copy(s).wait()
            a = fetch(self.parts.at[s, :, me.side], self.own, self.local.at[0])
            b = fetch(self.y_land.at[s], self.got, self.local.at[1])
            a.wait()
            b.wait()
            self.ring[lax.rem(s, depth)] = self.own[...] + self.got[...]

        for k in range(line - 1):
            tile, count = s - 1 - k, line - 1 - k

            @pl.when((me.spot == k) & (tile >= 0) & (tile < tiles))
            def _(k=k, tile=tile, count=count):
                slot, held = lax.rem(tile, 2), lax.rem(tile, depth)

                @pl.when(tile >= 2)
                def _():
                    self.up_copy(tile, count).wait_send()

                if k > 0:
                    self.await_up(tile, count + 1)
                    fetch(
                        self.up_land.at[tile, 1 : count + 1], self.up_load.at[0:count],
                        self.local.at[2],
                    ).wait()
                    self.up_buf[slot, 0:count] = (
                        self.ring[held, k + 1 : line] + self.up_load[0:count]
                    )
                else:
                    self.up_buf[slot, 0:count] = self.ring[held, k + 1 : line]
                self.up_copy(tile, count).start()

        for k in range(1, line):
            tile, count = s - 1 - (line - 1 - k), k

            @pl.when((me.spot == k) & (tile >= 0) & (tile < tiles))
            def _(k=k, tile=tile, count=count):
                slot, held = lax.rem(tile, 2), lax.rem(tile, depth)

                @pl.when(tile >= 2)
                def _():
                    self.down_copy(tile, count).wait_send()

                if k < line - 1:
                    self.await_down(tile, count + 1)
                    fetch(
                        self.down_land.at[tile, 0:count], self.down_load.at[0:count],
                        self.local.at[3],
                    ).wait()
                    self.down_buf[slot, 0:count] = (
                        self.ring[held, 0:count] + self.down_load[0:count]
                    )
                else:
                    self.down_buf[slot, 0:count] = self.ring[held, 0:count]
                self.down_copy(tile, count).start()

        tile = s - 1 - line

        @pl.when((tile >= 0) & (tile < tiles))
        def _():
            held = lax.rem(tile, depth)
            self.last[2] = self.ring[held, me.spot]

            @pl.when(me.spot == line - 1)
            def _():
                self.await_up(tile, 1)

            @pl.when(me.spot == 0)
            def _():
                self.await_down(tile, 1)

            @pl.when(me.spot > 0)
            def _():
                fetch(self.up_land.at[tile, 0], self.last.at[0], self.local.at[4]).wait()
                self.last[2] = self.last[2] + self.last[0]

            @pl.when(me.spot < line - 1)
            def _():
                fetch(self.down_land.at[tile, me.spot], self.last.at[1], self.local.at[5]).wait()
                self.last[2] = self.last[2] + self.last[1]

            fetch(self.last.at[2], self.result.at[tile], self.local.at[4]).wait()

    def finish(self):
        me, line = self.me, self.line
        for k in range(line - 1):
            @pl.when(me.spot == k)
            def _(k=k):
                for tile in range(max(0, self.tiles - 2), self.tiles):
                    self.up_copy(tile, line - 1 - k).wait_send()

        for k in range(1, line):
            @pl.when(me.spot == k)
            def _(k=k):
                for tile in range(max(0, self.tiles - 2), self.tiles):
                    self.down_copy(tile, k).wait_send()


class NarrowSum:
    @staticmethod
    def lands(chunks, quarter, width):
        return [
            jax.ShapeDtypeStruct((chunks, 2, quarter, width), f32),
            jax.ShapeDtypeStruct((chunks, quarter, width), f32),
            jax.ShapeDtypeStruct((chunks, quarter, width), f32),
            jax.ShapeDtypeStruct((chunks, 2, quarter, width), f32),
        ]

    @staticmethod
    def sems(chunks):
        dma = pltpu.SemaphoreType.DMA
        return [dma((chunks,)) for _ in range(8)] + [dma((5,))]

    @staticmethod
    def buffers(quarter, width):
        return [
            pltpu.VMEM((2, 2, 2, quarter, width), f32),
            pltpu.VMEM((2, quarter, width), f32),
            pltpu.VMEM((2, 2, quarter, width), f32),
            pltpu.VMEM((quarter, width), f32),
            pltpu.VMEM((2, quarter, width), f32),
            pltpu.VMEM((2, 2, quarter, width), f32),
            pltpu.VMEM((2, quarter, width), f32),
            pltpu.VMEM((2, 2, quarter, width), bf16),
        ]

    def __init__(self, me, lands, sems, out):
        self.me, self.out = me, out
        self.core_land, self.chip_land, self.back_land, self.last_land = lands
        (self.s0, self.r0, self.s1, self.r1, self.s2, self.r2, self.s3, self.r3, self.local) = sems
        self.chunks = self.chip_land.shape[0]

    def use(self, buffers):
        (self.part, self.core_load, self.half, self.chip_load,
         self.done, self.pair, self.last_load, self.low) = buffers

    def copies(self, stage, c):
        me, slot = self.me, lax.rem(c, 2)
        if stage == 0:
            return remote(self.part.at[slot, 1 - me.core], self.core_land.at[c],
                          self.s0.at[c], self.r0.at[c], me.to_core)
        if stage == 1:
            return remote(self.half.at[slot, 1 - me.chip], self.chip_land.at[c],
                          self.s1.at[c], self.r1.at[c], me.to_chip)
        if stage == 2:
            return remote(self.done.at[slot], self.back_land.at[c],
                          self.s2.at[c], self.r2.at[c], me.to_chip)
        return remote(self.pair.at[slot], self.last_land.at[c],
                      self.s3.at[c], self.r3.at[c], me.to_core)

    @property
    def slots(self):
        return self.chunks + 4

    def step(self, s, produce, work, lower):
        me = self.me

        def stage(number, body):
            c = s - number

            @pl.when((c >= 0) & (c < self.chunks))
            def _():
                if number > 0:
                    self.copies(number - 1, c).wait()
                body(c, lax.rem(c, 2))
                if number < 4:
                    self.copies(number, c).start()

        def four(c, slot):
            fetch(self.last_land.at[c], self.last_load, self.local.at[3]).wait()
            self.low[me.core] = lower(self.pair[slot])
            self.low[1 - me.core] = lower(self.last_load[...])
            fetch(self.low, self.out(c), self.local.at[4]).wait()

        def three(c, slot):
            fetch(self.back_land.at[c], self.pair.at[slot, 1 - me.chip], self.local.at[2]).wait()
            self.pair[slot, me.chip] = self.done[slot]

        def two(c, slot):
            fetch(self.chip_land.at[c], self.chip_load, self.local.at[1]).wait()
            self.done[slot] = work(c, self.half[slot, me.chip] + self.chip_load[...])

        def one(c, slot):
            fetch(self.core_land.at[c], self.core_load, self.local.at[0]).wait()
            self.half[slot] = self.part[slot, me.core] + self.core_load[...]

        def zero(c, slot):
            produce(c, self.part.at[slot])

        stage(4, four)
        stage(3, three)
        stage(2, two)
        stage(1, one)
        stage(0, zero)


def take(refs, count):
    return refs[:count], refs[count:]


def store_part(part, value, columns):
    half, quarter = 2, value.shape[0] // 4
    part[:, :, :, columns] = value.reshape(half, 2, quarter, value.shape[1])


def attend_out_kernel(wide, chunks, *refs):
    (context, w_output, tokens, gain), refs = take(refs, 4)
    (mlp_in, hidden_out), refs = take(refs, 2)
    lands, refs = take(refs, 4)
    sems, refs = take(refs, 9)
    buffers, refs = take(refs, 8)
    token_load, hidden_buf, sem = refs
    me = Spot(wide)
    me.greet(False)
    summing = NarrowSum(me, lands, sems, lambda c: mlp_in.at[c])
    summing.use(buffers)
    rows = context.shape[0] // chunks
    width = w_output.shape[1]
    step = min(512, width)

    def produce(c, part):
        left = context[pl.ds(pl.multiple_of(c * rows, rows), rows), :]
        for at in range(0, width, step):
            store_part(part, forward_dot(left, w_output[:, at : at + step]), slice(at, at + step))

    def work(c, total):
        fetch(tokens.at[c, me.core, me.chip], token_load, sem.at[0]).wait()
        hidden = token_load[...].astype(f32) + total
        hidden_buf[...] = hidden
        fetch(hidden_buf, hidden_out.at[c], sem.at[1]).wait()
        return hidden * inverse_rms(hidden)

    def lower(value):
        return (value * gain[...]).astype(bf16)

    def body(s, carry):
        summing.step(s, produce, work, lower)
        return carry

    lax.fori_loop(0, summing.slots, body, 0)


def norm_back(pulled, unit, scale, gain):
    scaled = pulled * gain
    return scale * (scaled - unit * jnp.mean(scaled * unit, axis=-1, keepdims=True))


def outer_tile(left_t, right, stage):
    line, _, rows, _ = stage.shape
    group = max(1, 512 // (2 * rows))
    while line % group:
        group -= 1

    def body(m, carry):
        at = pl.multiple_of(m * group * 2 * rows, group * 2 * rows)
        value = forward_dot(left_t[pl.ds(at, group * 2 * rows), :], right)
        stage[pl.ds(m * group, group)] = value.reshape((group, 2, rows, value.shape[1]))
        return carry

    lax.fori_loop(0, line // group, body, 0)


def mlp_kernel(wide, chunks, *refs):
    (mlp_in, mlp_in_t, cot, cot_t, cot_parts, hidden, w_gate, w_up, w_down, gain), refs = take(refs, 10)
    (output, attn_low, grad_hidden, gain_part), refs = take(refs, 4)
    wide_lands, refs = take(refs, 5)
    lands, refs = take(refs, 4)
    wide_sems, refs = take(refs, 7)
    sems, refs = take(refs, 9)
    acts, gain_sum, sem, w_sem, store_sem = refs
    me = Spot(wide)
    me.greet(True)
    tokens, width = mlp_in.shape
    hidden_units = w_gate.shape[1]
    cols = wide_lands[0].shape[-1]
    blocks = hidden_units // cols
    line, side_rows = wide_lands[0].shape[1], wide_lands[0].shape[3]
    total = WideSum(me, wide_lands, wide_sems)
    half = tokens // 2

    def compute(xs, xt, cs, ct, gate_w, up_w, down_w, staged):
        for at, (a, b) in enumerate(((mlp_in, xs), (mlp_in_t, xt), (cot, cs), (cot_t, ct))):
            fetch(a, b, sem.at[at])

        def weights(b, slot):
            at = pl.ds(pl.multiple_of(b * cols, cols), cols)
            return (
                pltpu.make_async_copy(w_gate.at[:, at], gate_w.at[slot], w_sem.at[slot, 0]),
                pltpu.make_async_copy(w_up.at[:, at], up_w.at[slot], w_sem.at[slot, 1]),
                pltpu.make_async_copy(w_down.at[at, :], down_w.at[slot], w_sem.at[slot, 2]),
            )

        for copy in weights(0, 0):
            copy.start()
        for at, (a, b) in enumerate(((mlp_in, xs), (mlp_in_t, xt), (cot, cs), (cot_t, ct))):
            pltpu.make_async_copy(a, b, sem.at[at]).wait()

        def store(tile):
            slot = lax.rem(tile, 2)
            return pltpu.make_async_copy(staged.at[slot], total.parts.at[tile], store_sem.at[slot])

        def block(b, carry):
            slot = lax.rem(b, 2)
            for copy in weights(b, slot):
                copy.wait()

            @pl.when(b + 1 < blocks)
            def _():
                for copy in weights(b + 1, 1 - slot):
                    copy.start()

            at = pl.ds(pl.multiple_of(b * cols, cols), cols)

            def rows(m, carry):
                own = pl.ds(pl.multiple_of(m * half, half), half)
                gate = forward_dot(xs[own, :], gate_w[slot])
                up = forward_dot(xs[own, :], up_w[slot])
                back = nt_dot(cs[own, :], down_w[slot])
                sig = 1.0 / (1.0 + jnp.exp(-gate))
                silu = gate * sig
                acts[0, own, at] = (silu * up).astype(bf16)
                acts[1, own, at] = (back * up * sig * (1.0 + gate * (1.0 - sig))).astype(bf16)
                acts[2, own, at] = (back * silu).astype(bf16)
                return carry

            lax.fori_loop(0, 2, rows, 0)
            for j in range(3):
                tile = 3 * b + j

                @pl.when(tile >= 2)
                def _(tile=tile):
                    store(tile - 2).wait()

                    @pl.when(tile - 2 < total.ahead)
                    def _():
                        total.y_copy(tile - 2).start()

                outer_tile(ct if j == 0 else xt, acts[j, :, at], staged.at[lax.rem(tile, 2)])
                store(tile).start()
            return carry

        lax.fori_loop(0, blocks, block, 0)
        for tile in range(total.tiles - 2, total.tiles):
            store(tile).wait()
            if tile < total.ahead:
                total.y_copy(tile).start()

    pl.run_scoped(
        compute,
        pltpu.VMEM(mlp_in.shape, bf16),
        pltpu.VMEM(mlp_in_t.shape, bf16),
        pltpu.VMEM(mlp_in.shape, bf16),
        pltpu.VMEM(mlp_in_t.shape, bf16),
        pltpu.VMEM((2, width, cols), bf16),
        pltpu.VMEM((2, width, cols), bf16),
        pltpu.VMEM((2, cols, width), bf16),
        pltpu.VMEM((2, line, 2, side_rows, cols), f32),
    )

    def pass_on(*held):
        wide_buffers, held = take(held, 8)
        buffers, held = take(held, 8)
        gate_w, up_w, down_w, hidden_load, cot_load, out_buf = held
        total.use(wide_buffers)
        step = gate_w.shape[1]
        rows = tokens // chunks

        def out(c):
            return both.at[c]

        both = output
        summing = NarrowSum(me, lands, sems, out)
        summing.use(buffers)
        gain_sum[...] = jnp.zeros_like(gain_sum)

        def produce(c, part):
            @pl.when(c < chunks)
            def _():
                own = pl.ds(pl.multiple_of(c * rows, rows), rows)

                def copies(at, slot):
                    cut = pl.ds(at * step, step)
                    return (
                        pltpu.make_async_copy(w_gate.at[cut, :], gate_w.at[slot], w_sem.at[slot, 0]),
                        pltpu.make_async_copy(w_up.at[cut, :], up_w.at[slot], w_sem.at[slot, 1]),
                    )

                count = width // step
                for copy in copies(0, 0):
                    copy.start()
                for at in range(count):
                    if at + 1 < count:
                        for copy in copies(at + 1, (at + 1) % 2):
                            copy.start()
                    for copy in copies(at, at % 2):
                        copy.wait()
                    value = nt_dot(acts[1, own, :], gate_w[at % 2])
                    value = value + nt_dot(acts[2, own, :], up_w[at % 2])
                    store_part(part, value, slice(at * step, (at + 1) * step))

            @pl.when(c >= chunks)
            def _():
                own = pl.ds(pl.multiple_of((c - chunks) * rows, rows), rows)

                def copy(at, slot):
                    cut = pl.ds(at * step, step)
                    return pltpu.make_async_copy(w_down.at[:, cut], down_w.at[slot], w_sem.at[slot, 2])

                count = width // step
                copy(0, 0).start()
                for at in range(count):
                    if at + 1 < count:
                        copy(at + 1, (at + 1) % 2).start()
                    copy(at, at % 2).wait()
                    value = forward_dot(acts[0, own, :], down_w[at % 2])
                    store_part(part, value, slice(at * step, (at + 1) * step))

        def work(c, pulled):
            chunk = lax.rem(c, chunks)
            a = fetch(hidden.at[chunk], hidden_load, sem.at[0])
            b = fetch(cot_parts.at[chunk, me.core, me.chip], cot_load, sem.at[1])
            a.wait()
            b.wait()

            @pl.when(c < chunks)
            def _():
                mid = hidden_load[...]
                scale = inverse_rms(mid)
                unit = mid * scale
                gain_sum[...] += jnp.sum(pulled * unit, axis=0, keepdims=True)
                grad = cot_load[...].astype(f32) + norm_back(pulled, unit, scale, gain[...])
                out_buf[...] = grad
                fetch(out_buf, grad_hidden.at[chunk], sem.at[2]).wait()

            @pl.when(c >= chunks)
            def _():
                out_buf[...] = hidden_load[...] + pulled

            return out_buf[...]

        def lower(value):
            return value.astype(bf16)

        def body(s, carry):
            pl.when(s < total.slots)(lambda: total.step(s))
            pl.when(s < summing.slots)(lambda: summing.step(s, produce, work, lower))
            return carry

        lax.fori_loop(0, max(total.slots, summing.slots), body, 0)
        total.finish()

    quarter = hidden.shape[1]
    step = min(256, width)
    pl.run_scoped(
        pass_on,
        *WideSum.buffers(line, side_rows, cols),
        *NarrowSum.buffers(quarter, width),
        pltpu.VMEM((2, step, hidden_units), bf16),
        pltpu.VMEM((2, step, hidden_units), bf16),
        pltpu.VMEM((2, hidden_units, step), bf16),
        pltpu.VMEM((quarter, width), f32),
        pltpu.VMEM((quarter, width), bf16),
        pltpu.VMEM((quarter, width), f32),
    )
    fetch(gain_sum, gain_part, sem.at[0]).wait()


def attn_grad_kernel(wide, chunks, *refs):
    (low_t, context, normed_t, grad_heads, weights, tokens, grad_hidden, gain), refs = take(refs, 8)
    (grad_tokens, gain_part), refs = take(refs, 2)
    wide_lands, refs = take(refs, 5)
    lands, refs = take(refs, 4)
    wide_sems, refs = take(refs, 7)
    sems, refs = take(refs, 9)
    gain_sum, sem, store_sem = refs
    me = Spot(wide)
    me.greet(True)
    width, count = low_t.shape
    cols = wide_lands[0].shape[-1]
    line, side_rows = wide_lands[0].shape[1], wide_lands[0].shape[3]
    total = WideSum(me, wide_lands, wide_sems)
    out_tiles = context.shape[1] // cols

    def compute(lt, nt, ctx, heads, staged):
        pairs = ((low_t, lt), (normed_t, nt), (context, ctx), (grad_heads, heads))
        for at, (a, b) in enumerate(pairs):
            fetch(a, b, sem.at[at])
        for at, (a, b) in enumerate(pairs):
            pltpu.make_async_copy(a, b, sem.at[at]).wait()

        def store(tile):
            slot = lax.rem(tile, 2)
            return pltpu.make_async_copy(staged.at[slot], total.parts.at[tile], store_sem.at[slot])

        def one(tile, left, right, at):
            @pl.when(tile >= 2)
            def _():
                store(tile - 2).wait()

                @pl.when(tile - 2 < total.ahead)
                def _():
                    total.y_copy(tile - 2).start()

            cut = pl.ds(pl.multiple_of(at * cols, cols), cols)
            outer_tile(left, right[:, cut], staged.at[lax.rem(tile, 2)])
            store(tile).start()

        def first(t, carry):
            one(t, lt, ctx, t)
            return carry

        def second(t, carry):
            one(t, nt, heads, t - out_tiles)
            return carry

        lax.fori_loop(0, out_tiles, first, 0)
        lax.fori_loop(out_tiles, total.tiles, second, 0)
        for tile in range(total.tiles - 2, total.tiles):
            store(tile).wait()
            if tile < total.ahead:
                total.y_copy(tile).start()

    pl.run_scoped(
        compute,
        pltpu.VMEM(low_t.shape, bf16),
        pltpu.VMEM(normed_t.shape, bf16),
        pltpu.VMEM(context.shape, bf16),
        pltpu.VMEM(grad_heads.shape, bf16),
        pltpu.VMEM((2, line, 2, side_rows, cols), f32),
    )

    def pass_on(*held):
        wide_buffers, held = take(held, 8)
        buffers, held = take(held, 8)
        heads, w_all, hidden_load, token_load = held
        total.use(wide_buffers)
        rows = count // chunks
        step = min(512, width)
        a = fetch(grad_heads, heads, sem.at[0])
        b = fetch(weights, w_all, sem.at[1])
        summing = NarrowSum(me, lands, sems, lambda c: grad_tokens.at[c])
        summing.use(buffers)
        gain_sum[...] = jnp.zeros_like(gain_sum)
        a.wait()
        b.wait()

        def produce(c, part):
            left = heads[pl.ds(pl.multiple_of(c * rows, rows), rows), :]
            for at in range(0, width, step):
                store_part(part, nt_dot(left, w_all[at : at + step, :]), slice(at, at + step))

        def work(c, pulled):
            a = fetch(grad_hidden.at[c], hidden_load, sem.at[0])
            b = fetch(tokens.at[c, me.core, me.chip], token_load, sem.at[1])
            a.wait()
            b.wait()
            mid = token_load[...].astype(f32)
            scale = inverse_rms(mid)
            unit = mid * scale
            gain_sum[...] += jnp.sum(pulled * unit, axis=0, keepdims=True)
            return hidden_load[...] + norm_back(pulled, unit, scale, gain[...])

        def lower(value):
            return value.astype(bf16)

        def body(s, carry):
            pl.when(s < total.slots)(lambda: total.step(s))
            pl.when(s < summing.slots)(lambda: summing.step(s, produce, work, lower))
            return carry

        lax.fori_loop(0, max(total.slots, summing.slots), body, 0)
        total.finish()

    quarter = grad_hidden.shape[1]
    pl.run_scoped(
        pass_on,
        *WideSum.buffers(line, side_rows, cols),
        *NarrowSum.buffers(quarter, width),
        pltpu.VMEM(grad_heads.shape, bf16),
        pltpu.VMEM(weights.shape, bf16),
        pltpu.VMEM((quarter, width), f32),
        pltpu.VMEM((quarter, width), bf16),
    )
    fetch(gain_sum, gain_part, sem.at[0]).wait()


def call(kernel, collective_id, out_shape, in_specs, out_specs, scratch, arrays, limit):
    return pl.pallas_call(
        kernel,
        out_shape=out_shape,
        in_specs=in_specs,
        out_specs=out_specs,
        scratch_shapes=scratch,
        compiler_params=pltpu.CompilerParams(
            collective_id=collective_id, has_side_effects=True, vmem_limit_bytes=limit
        ),
    )(*arrays)


def swap_cores(values):
    return lax.ppermute(values, "narrow", [(0, 1), (1, 0), (2, 3), (3, 2)])


def swap_chips(values):
    return lax.ppermute(values, "narrow", [(0, 2), (2, 0), (1, 3), (3, 1)])


def per_device(
    wide,
    tokens,
    seq_lengths,
    attn_gain,
    w_query,
    key_weight,
    value_weight,
    query_gain,
    key_norm_gain,
    w_output,
    mlp_gain,
    w_gate,
    w_up,
    w_down,
    cotangent,
):
    token_count, model_width = tokens.shape
    head_dim = query_gain.shape[0]
    kv_heads = key_weight.shape[1] // head_dim
    q_heads = w_query.shape[1] // head_dim
    group_width = q_heads // kv_heads
    score_scale = head_dim ** (-0.5)
    line = wide // 2
    side_rows = model_width // wide
    first_chunks, chunks = 8, 8
    dma = pltpu.SemaphoreType.DMA
    limit = 60 * 1024 * 1024

    segment_index, token_positions = layout(seq_lengths, token_count)
    segment_index = segment_index.reshape(-1)
    token_positions = token_positions.reshape(-1)
    allowed = (segment_index[:, None] == segment_index[None, :]) & (
        token_positions[:, None] >= token_positions[None, :]
    )
    cosine_table, sine_table = tables(token_positions, head_dim)

    def prepare(raw_heads, gain):
        return rotate_pairs(root_mean_scale(raw_heads, gain), cosine_table, sine_table)

    def parts_of(values, count):
        return values.reshape(count, 2, 2, token_count // count // 4, model_width)

    tokens32 = tokens.astype(f32)
    normed = (tokens32 * inverse_rms(tokens32) * attn_gain).astype(bf16)
    query_proj = forward_dot(normed, w_query)
    key_projected = forward_dot(normed, key_weight)
    value_low = (
        forward_dot(normed, value_weight).astype(bf16).reshape(token_count, kv_heads, head_dim)
    )
    query32, query_pull = jax.vjp(
        prepare, query_proj.reshape(token_count, q_heads, head_dim), query_gain
    )
    key32, key_pull = jax.vjp(
        prepare, key_projected.reshape(token_count, kv_heads, head_dim), key_norm_gain
    )
    query_low = query32.astype(bf16).reshape(token_count, kv_heads, group_width, head_dim)
    key_low = key32.astype(bf16)
    scores = score_block(query_low, key_low, allowed, score_scale)
    top_score = jnp.max(scores, axis=-1, keepdims=True)
    expd = jnp.exp(scores - top_score)
    row_total = jnp.sum(expd, axis=-1, keepdims=True)
    probs_low = (expd / row_total).astype(bf16)
    log_total = top_score + jnp.log(row_total)
    mixed_heads = jnp.einsum("kgts,skd->tkgd", probs_low, value_low, preferred_element_type=f32)
    context = mixed_heads.reshape(token_count, q_heads * head_dim).astype(bf16)

    quarter = token_count // first_chunks // 4
    outs = call(
        lambda *refs: attend_out_kernel(wide, first_chunks, *refs),
        1,
        [
            jax.ShapeDtypeStruct((first_chunks, 2, 2, quarter, model_width), bf16),
            jax.ShapeDtypeStruct((first_chunks, quarter, model_width), f32),
            *NarrowSum.lands(first_chunks, quarter, model_width),
        ],
        [in_vmem, in_vmem, any_space, in_vmem],
        [any_space] * 6,
        [
            *NarrowSum.sems(first_chunks),
            *NarrowSum.buffers(quarter, model_width),
            pltpu.VMEM((quarter, model_width), bf16),
            pltpu.VMEM((quarter, model_width), f32),
            dma((2,)),
        ],
        (context, w_output, parts_of(tokens, first_chunks), mlp_gain[None]),
        limit,
    )
    mlp_in = outs[0].reshape(token_count, model_width)
    hidden = outs[1]

    quarter = token_count // chunks // 4
    cols = min(256, w_gate.shape[1])
    order = first_chunks // chunks
    rows_held = token_count // first_chunks // 4

    def regroup(values):
        return (
            values.reshape(chunks, order, 2, 2, rows_held, model_width)
            .transpose(0, 2, 3, 1, 4, 5)
            .reshape(chunks, 2, 2, quarter, model_width)
        )

    def restore(values):
        return (
            values.reshape(chunks, 2, 2, order, rows_held, model_width)
            .transpose(0, 3, 1, 2, 4, 5)
            .reshape(token_count, model_width)
        )

    cot_parts = regroup(cotangent)
    token_parts = regroup(tokens)
    mlp_rows = regroup(mlp_in).reshape(token_count, model_width)
    cot_rows = cot_parts.reshape(token_count, model_width)
    tiles = 3 * (w_gate.shape[1] // cols)
    outs = call(
        lambda *refs: mlp_kernel(wide, chunks, *refs),
        2,
        [
            jax.ShapeDtypeStruct((2 * chunks, 2, 2, quarter, model_width), bf16),
            jax.ShapeDtypeStruct((8, 128), bf16),
            jax.ShapeDtypeStruct((chunks, quarter, model_width), f32),
            jax.ShapeDtypeStruct((1, model_width), f32),
            *WideSum.lands(tiles, line, side_rows, cols),
            *NarrowSum.lands(2 * chunks, quarter, model_width),
        ],
        [any_space] * 9 + [in_vmem],
        [any_space] * 13,
        [
            *WideSum.sems(tiles),
            *NarrowSum.sems(2 * chunks),
            pltpu.VMEM((3, token_count, w_gate.shape[1]), bf16),
            pltpu.VMEM((1, model_width), f32),
            dma((4,)),
            dma((2, 3)),
            dma((2,)),
        ],
        (
            mlp_rows,
            mlp_rows.T,
            cot_rows,
            cot_rows.T,
            cot_parts,
            hidden.reshape(chunks, quarter, model_width),
            w_gate,
            w_up,
            w_down,
            mlp_gain[None],
        ),
        limit,
    )
    attn_rows = outs[0][:chunks]
    output = restore(outs[0][chunks:])
    grad_hidden, mlp_gain_part, mlp_tiles = outs[2], outs[3][0], outs[8]
    attn_low = restore(attn_rows)

    grad_context = (
        back_dot(attn_low, w_output)
        .astype(bf16)
        .reshape(token_count, kv_heads, group_width, head_dim)
    )
    again = score_block(query_low, key_low, allowed, score_scale)
    probs = jnp.exp(again - log_total)
    again_low = probs.astype(bf16)
    grad_value = jnp.einsum("kgts,tkgd->skd", again_low, grad_context, preferred_element_type=f32)
    grad_probs = jnp.einsum("tkgd,skd->kgts", grad_context, value_low, preferred_element_type=f32)
    grad_scores = probs * (grad_probs - jnp.sum(probs * grad_probs, axis=-1, keepdims=True))
    scores_low = grad_scores.astype(bf16)
    grad_query_heads = (
        jnp.einsum("kgts,skd->tkgd", scores_low, key_low, preferred_element_type=f32) * score_scale
    )
    grad_key_heads = (
        jnp.einsum("kgts,tkgd->skd", scores_low, query_low, preferred_element_type=f32)
        * score_scale
    )
    grad_query32, query_gain_part = query_pull(
        grad_query_heads.reshape(token_count, q_heads, head_dim)
    )
    grad_key32, key_gain_part = key_pull(grad_key_heads)
    grad_query_proj = grad_query32.reshape(token_count, q_heads * head_dim).astype(bf16)
    grad_key_proj = grad_key32.reshape(token_count, kv_heads * head_dim).astype(bf16)
    grad_value_low = grad_value.reshape(token_count, kv_heads * head_dim).astype(bf16)
    grad_heads = jnp.concatenate([grad_query_proj, grad_key_proj, grad_value_low], axis=1)
    head_weights = jnp.concatenate([w_query, key_weight, value_weight], axis=1)

    def regroup_heads(values):
        return (
            values.reshape(chunks, order, 2, 2, rows_held, -1)
            .transpose(0, 2, 3, 1, 4, 5)
            .reshape(token_count, -1)
        )

    tiles = (context.shape[1] + grad_heads.shape[1]) // cols
    outs = call(
        lambda *refs: attn_grad_kernel(wide, chunks, *refs),
        3,
        [
            jax.ShapeDtypeStruct((chunks, 2, 2, quarter, model_width), bf16),
            jax.ShapeDtypeStruct((1, model_width), f32),
            *WideSum.lands(tiles, line, side_rows, cols),
            *NarrowSum.lands(chunks, quarter, model_width),
        ],
        [any_space] * 7 + [in_vmem],
        [any_space] * 11,
        [
            *WideSum.sems(tiles),
            *NarrowSum.sems(chunks),
            pltpu.VMEM((1, model_width), f32),
            dma((4,)),
            dma((2,)),
        ],
        (
            attn_rows.reshape(token_count, model_width).T,
            regroup_heads(context),
            regroup(normed).reshape(token_count, model_width).T,
            regroup_heads(grad_heads),
            head_weights,
            token_parts,
            grad_hidden,
            attn_gain[None],
        ),
        limit,
    )
    grad_tokens = restore(outs[0])
    attn_gain_part, attn_tiles = outs[1][0], outs[6]

    blocks = w_gate.shape[1] // cols
    mlp_tiles = mlp_tiles.reshape(blocks, 3, side_rows, cols)
    shard_down = mlp_tiles[:, 0].transpose(0, 2, 1).reshape(blocks * cols, side_rows)
    shard_gate = mlp_tiles[:, 1].transpose(1, 0, 2).reshape(side_rows, blocks * cols)
    shard_up = mlp_tiles[:, 2].transpose(1, 0, 2).reshape(side_rows, blocks * cols)
    out_tiles = context.shape[1] // cols
    shard_output = attn_tiles[:out_tiles].transpose(0, 2, 1).reshape(context.shape[1], side_rows)
    shard_heads = attn_tiles[out_tiles:].transpose(1, 0, 2).reshape(side_rows, -1)
    query_width, kv_width = w_query.shape[1], key_weight.shape[1]
    shard_query = shard_heads[:, :query_width]
    shard_key = shard_heads[:, query_width : query_width + kv_width]
    shard_value = shard_heads[:, query_width + kv_width :]

    gains = jnp.concatenate(
        [
            v.reshape(wide, -1)
            for v in (attn_gain_part, mlp_gain_part, query_gain_part, key_gain_part)
        ],
        axis=1,
    )
    gains = lax.psum(gains, ("wide", "narrow"))
    gains = lax.dynamic_index_in_dim(gains, lax.axis_index("wide"), 0, keepdims=False)
    wide_width, head_width = model_width // wide, head_dim // wide
    shard_attn_gain = gains[:wide_width]
    shard_mlp_gain = gains[wide_width : 2 * wide_width]
    shard_query_gain = gains[2 * wide_width : 2 * wide_width + head_width]
    shard_key_gain = gains[2 * wide_width + head_width :]
    return (
        output,
        grad_tokens,
        shard_attn_gain,
        shard_query,
        shard_key,
        shard_value,
        shard_query_gain,
        shard_key_gain,
        shard_output,
        shard_mlp_gain,
        shard_gate,
        shard_up,
        shard_down,
    )


def solution(mesh):
    def run(*arrays):
        return per_device(mesh.shape["wide"], *arrays)

    return jax.shard_map(
        run,
        mesh=mesh,
        in_specs=(
            P("wide", None),
            P("wide", None),
            P(),
            P(None, "narrow"),
            P(None, "narrow"),
            P(None, "narrow"),
            P(),
            P(),
            P("narrow", None),
            P(),
            P(None, "narrow"),
            P(None, "narrow"),
            P("narrow", None),
            P("wide", None),
        ),
        out_specs=(
            P("wide", None),
            P("wide", None),
            P("wide"),
            P("wide", "narrow"),
            P("wide", "narrow"),
            P("wide", "narrow"),
            P("wide"),
            P("wide"),
            P("narrow", "wide"),
            P("wide"),
            P("wide", "narrow"),
            P("wide", "narrow"),
            P("narrow", "wide"),
        ),
        check_vma=False,
    )
```

time: 1780 us -> 1080 us (0.61)
  waiting for transfers between devices: 1410 us -> 0 us
  Pallas kernels: 0 us -> 830 us
  matrix products: 201 us -> 58.1 us
  local copies, waits for them, and re-layouts: 10.8 us -> 71.9 us
  other arithmetic: 84.1 us -> 44.8 us
    reduce_scatter x7 -> x0, waiting for transfers between devices: 889 us -> none  [the longest x1 212 us: per_device(): lax.psum_scatter(grad_w_down, 'wide', scatter_dimension=1, tiled=True)]
    pallas_call x0 -> x3, Pallas kernels: none -> 830 us  [call(): pl.pallas_call(kernel, out_shape=out_shape, in_specs=in_specs, out_specs=...]
    psum x3 -> x0, waiting for transfers between devices: 520 us -> none  [the longest x1 223 us: per_device(): mlp_branch = lax.psum(forward_dot(inner_act, w_down), 'narrow')]
    dot_general x15 -> x4, matrix products: 118 us -> 17.2 us  [the longest x3 9.24 us: forward_dot(): return jnp.dot(left_side, right_side, preferred_element_type=f32)]
    dot_general x7 -> x1, matrix products: 52.1 us -> 3.36 us  [back_dot(): lax.dot_general(left_side, right_side, (((1,), (1,)), ((), ())), preferre...]
    psum x1, blocking collectives: 6.45 us -> 50.3 us  [per_device(): gains = lax.psum(gains, ('wide', 'narrow'))]
    unnamed x1 -> x0, blocking collectives: 37.6 us -> none
    unnamed x129 -> x100, local copies, waits for them, and re-layouts: 10.8 us -> 36.8 us
  transfers between devices with their start and end apart: 10 -> 0, of which waited for: 10 -> 0; matrix products, arithmetic and copies ran while one was open for 6% -> 0% of each run, Pallas kernels for 0% -> 0%
where the time goes in v1:
time: 1080 us; the launch traced here: 1060 us
  Pallas kernels  830 us (77%)
  local copies, waits for them, and re-layouts  71.9 us (7%)
  matrix products  58.1 us (5%)
  blocking collectives  50.3 us (5%)
  other arithmetic  44.8 us (4%)
    pallas_call x3, Pallas kernels, call(): pl.pallas_call(kernel, out_shape=out_shape, in_specs=in_specs, out_specs=...  830 us
    psum x1, blocking collectives, per_device(): gains = lax.psum(gains, ('wide', 'narrow'))  50.3 us
    unnamed x100, local copies, waits for them, and re-layouts  36.8 us

profile of v1, /device:TPU:0, one launch (start us, length us, event | category | flops | bytes accessed | tf_op | source)
XLA Modules:
  0.0 1057.2 jit_solution(42909909205308581)
XLA Ops:
  0.6 6.4 copy.117
  7.0 3.3 fusion.5
  10.5 4.1 multiply_reduce_fusion.2
  17.1 2.7 broadcast_multiply_fusion.2
  19.8 2.5 fusion.14
  26.5 8.0 fusion.45
  34.5 8.1 fusion.3
  42.6 3.7 convolution_convert_fusion.1
  46.3 8.8 fusion.17
  55.1 2.3 copy.157.refs_0_.refs_1_
  57.3 125.5 %shard_map.237 = (bf16[8,2,2,32,2048]{4,3,2,1,0:T(8,128)(2,1)}, f32[8,32,2048]{2,1,0:T(8,128)}, f32[8,2,32,2048]{3,2,1,0:T(8,128)}, f32[8,32,2048]{2,1,0:T(8,128...) custom-call(bf16[1024,512]{1,0:T(8,128)(2,1)} %copy.157.refs_0_.refs_1_, bf16[512,2048]{1,0:T(8,128)(2,1)} %refs_1_.1, ...), custom_call_target="tpu_custom_call" | custom-call | tf_op jit(solution)/shard_map/pallas_call | solution.py:811
  182.8 6.4 copy.122
  189.2 6.4 copy.123
  195.6 486.9 %shard_map.238 = (bf16[16,2,2,32,2048]{4,3,2,1,0:T(8,128)(2,1)}, bf16[8,128]{1,0:T(8,128)(2,1)}, f32[8,32,2048]{2,1,0:T(8,128)}, f32[1,2048]{1,0:T(1,128)}, f32[...) custom-call(bf16[1024,2048]{1,0:T(8,128)(2,1)} %bitcast.143, ...), custom_call_target="tpu_custom_call" | custom-call | tf_op jit(solution)/shard_map/pallas_call | solution.py:811
  682.6 5.6 fusion.40
  688.3 3.4 convolution_convert_fusion
  695.1 11.2 %fusion = (f32[2,2,1024]{2,1,0:T(2,128)}, f32[2,1024,1024,2]{2,1,3,0:T(8,128)}) fusion(f32[2,2,1024,1024]{2,3,1,0:T(8,128)S(1)} %bitcast.132, f32[2,2,1024]{2,1,0:T(2,128)} %log_add_fusion, bf16[1024,2,128,1]{0,2,3,1:T(8,128)(2,1)} %bitcast.163, bf16[1024,2,2,128]{0,3,2,1:T(8,128)(2,1)} %bitcast.156), kind=kOutput, calls=%fused_computation.2 | convolution fusion | flops 1086320640 | bytes 35160064 | tf_op jit(solution)/shard_map/tkgd,skd->kgts/dot_general | solution.py:996
  706.3 8.4 fusion.2
  716.0 1.9 copy-done
  721.6 1.7 copy.160
  723.4 6.7 broadcast_multiply_fusion
  731.5 9.5 fusion.21
  743.9 6.4 copy.124
  750.4 4.3 fusion.33.refs_2_
  754.6 2.3 pad_maximum_fusion.refs_4_
  757.0 218.1 %shard_map.239 = (bf16[8,2,2,32,2048]{4,3,2,1,0:T(8,128)(2,1)}, f32[1,2048]{1,0:T(1,128)}, f32[6,4,2,256,256]{4,3,2,1,0:T(8,128)}, f32[6,4,256,256]{3,2,1,0:T(8,...) custom-call(bf16[2048,1024]{1,0:T(8,128)(2,1)} %bitcast.139, ...), custom_call_target="tpu_custom_call" | custom-call | tf_op jit(solution)/shard_map/pallas_call | solution.py:811
  977.9 50.3 %psum.7 = f32[8,544]{1,0:T(8,128)S(1)} all-reduce(f32[8,544]{1,0:T(8,128)S(1)} %pad_maximum_fusion.3), channel_id=1, replica_groups=mesh['wide'=8,'narrow'=4] {'wide','narrow'}, use_global_device_ids=true, to_apply=%region_13.14 | all-reduce | flops 4352 | bytes 34816 | tf_op jit(solution)/shard_map/psum | solution.py:1077
  1035.9 4.0 slice_bitcast_fusion
  1039.9 3.0 copy.163
  1042.9 3.0 copy.141
  1047.5 3.0 copy.142
  1052.2 4.8 copy.166
  (143 shorter events, 33.1 us)
Async XLA Ops:
  7.0 3.4 copy-start.1
  7.0 3.4 copy-start.28
  10.5 32.1 %copy-start.32 = (f32[1024]{0:T(1024)}, f32[1024]{0:T(1024)S(1)}, u32[]{:S(2)}) copy-start(f32[1024]{0:T(1024)S(1)} %add_rsqrt_fusion) | copy-start | bytes 12292
  10.5 4.1 copy-start.35
  17.1 5.2 copy-start.2
  17.1 5.2 copy-start.18
  19.8 4.4 copy-start.6
  22.3 4.1 copy-start.9
  25.2 9.2 copy-start.14
  34.4 11.9 %copy-start.24 = (f32[2,2,1024]{2,1,0:T(2,128)}, f32[2,2,1024]{2,1,0:T(2,128)S(1)}, u32[]{:S(2)}) copy-start(f32[2,2,1024]{2,1,0:T(2,128)S(1)} %get-tuple-element.105) | copy-start | bytes 49156
  34.4 8.1 copy-start.16
  42.6 3.7 copy-start.26
  46.3 8.8 copy-start.20
  682.5 5.7 copy-start.12
  682.6 9.7 slice-start
  682.6 9.9 slice-start.1
  688.2 3.4 copy-start.5
  688.2 3.4 copy-start.25
  688.2 3.4 copy-start.27
  688.2 5.6 slice-start.2
  688.3 6.8 slice-start.3
  706.3 8.4 copy-start.15
  723.3 6.9 copy-start.4
  723.3 6.9 copy-start.11
  723.3 6.9 copy-start.38
  743.9 6.4 copy-start.29
  743.9 6.4 copy-start.33
  750.3 4.3 copy-start.13
  750.3 4.3 copy-start.17
  750.3 4.3 copy-start.19
  757.0 220.0 %copy-start.39 = (f32[128]{0:T(128)S(1)}, f32[128]{0:T(128)}, u32[]{:S(2)}) copy-start(f32[128]{0:T(128)} %get-tuple-element.70) | copy-start | bytes 1540
  757.0 220.1 %copy-start.34 = (f32[1,2048]{1,0:T(1,128)S(1)}, f32[1,2048]{1,0:T(1,128)}, u32[]{:S(2)}) copy-start(f32[1,2048]{1,0:T(1,128)} %get-tuple-element.28) | copy-start | bytes 24580
  (13 other events, 24.1 us)

commit v2 on v1

v2 whole, which is shorter than its diff:
```python
import functools

import jax
import jax.numpy as jnp
from jax import lax
from jax.experimental import pallas as pl
from jax.experimental.pallas import tpu as pltpu
from jax.sharding import PartitionSpec as P

norm_eps = 1e-06
rope_base = 1000000.0
masked_score = -1e30
bf16 = jnp.bfloat16
f32 = jnp.float32


def inverse_rms(values):
    return lax.rsqrt(jnp.mean(values * values, axis=-1, keepdims=True) + norm_eps)


def layout(seq_lengths, row_len):
    seq_ends = jnp.cumsum(seq_lengths, axis=-1)
    starts = seq_ends - seq_lengths
    places = jnp.arange(row_len, dtype=jnp.int32)
    segment_index = jnp.sum(
        (places[None, :, None] >= seq_ends[:, None, :]).astype(jnp.int32), axis=-1
    )
    belongs = (
        segment_index[:, :, None]
        == jnp.arange(seq_lengths.shape[-1], dtype=jnp.int32)[None, None, :]
    )
    seq_start = jnp.sum(jnp.where(belongs, starts[:, None, :], 0), axis=-1)
    return (segment_index, places[None, :] - seq_start)


def tables(token_positions, head_dim):
    half_width = head_dim // 2
    frequency = rope_base ** (-2.0 * jnp.arange(half_width, dtype=f32) / head_dim)
    angles = token_positions.astype(f32)[:, None] * frequency[None, :]
    angles = jnp.concatenate([angles, angles], axis=-1)
    return (jnp.cos(angles)[:, None, :], jnp.sin(angles)[:, None, :])


def forward_dot(left_side, right_side):
    return jnp.dot(left_side, right_side, preferred_element_type=f32)


MESH = pl.DeviceIdType.MESH
any_space = pl.BlockSpec(memory_space=pl.ANY)
in_vmem = pl.BlockSpec(memory_space=pltpu.VMEM)


def nt_dot(left_side, right_side):
    return lax.dot_general(
        left_side, right_side, (((1,), (1,)), ((), ())), preferred_element_type=f32
    )


def fetch(source, target, sem):
    copy = pltpu.make_async_copy(source, target, sem)
    copy.start()
    return copy


class Spot:
    def __init__(self, wide):
        self.line = wide // 2
        self.w = lax.axis_index("wide")
        self.n = lax.axis_index("narrow")
        self.spot = lax.div(self.w, 2)
        self.side = lax.rem(self.w, 2)
        self.core = lax.rem(self.n, 2)
        self.chip = lax.div(self.n, 2)
        self.to_core = {"narrow": self.n + 1 - 2 * self.core}
        self.to_chip = {"narrow": self.n + 2 - 4 * self.chip}
        self.to_side = {"wide": self.w + 1 - 2 * self.side}
        self.to_up = {"wide": self.w + 2}
        self.to_down = {"wide": self.w - 2}

    def along(self, distance):
        there = lax.rem(self.spot + distance, self.line)
        return {"wide": there * 2 + self.side}

    def greet(self, wide_too):
        barrier = pltpu.get_barrier_semaphore()

        def tell(who):
            pl.semaphore_signal(barrier, inc=1, device_id=who, device_id_type=MESH)

        tell(self.to_core)
        tell(self.to_chip)
        if wide_too:
            tell(self.to_side)
            for distance in range(1, self.line):
                tell(self.along(distance))
        pl.semaphore_wait(barrier, 2 + self.line if wide_too else 2)


def remote(source, target, send, recv, who):
    return pltpu.make_async_remote_copy(
        src_ref=source, dst_ref=target, send_sem=send, recv_sem=recv,
        device_id=who, device_id_type=MESH,
    )


class WideSum:
    ahead = 4

    @staticmethod
    def lands(tiles, line, rows, cols):
        return [
            jax.ShapeDtypeStruct((tiles, line, 2, rows, cols), f32),
            jax.ShapeDtypeStruct((tiles, line, rows, cols), f32),
            jax.ShapeDtypeStruct((tiles, line, rows, cols), f32),
            jax.ShapeDtypeStruct((tiles, line, rows, cols), f32),
        ]

    @staticmethod
    def sems(tiles):
        dma = pltpu.SemaphoreType.DMA
        return [dma((tiles,)), dma((tiles,)), dma((2,)), dma((tiles,)), dma((2,)), dma((tiles,)), dma((6,))]

    @staticmethod
    def buffers(line, rows, cols):
        tile = (line, rows, cols)
        return [
            pltpu.VMEM(tile, f32),
            pltpu.VMEM(tile, f32),
            pltpu.VMEM((line + 3,) + tile, f32),
            pltpu.VMEM((2, line - 1, rows, cols), f32),
            pltpu.VMEM((2, line - 1, rows, cols), f32),
            pltpu.VMEM((line - 1, rows, cols), f32),
            pltpu.VMEM((line - 1, rows, cols), f32),
            pltpu.VMEM((3, rows, cols), f32),
        ]

    def __init__(self, me, lands, sems):
        self.me = me
        self.parts, self.y_land, self.up_land, self.down_land = lands
        (self.y_send, self.y_recv, self.up_send, self.up_recv,
         self.down_send, self.down_recv, self.local) = sems
        self.tiles, self.line = self.parts.shape[0], me.line

    def y_copy(self, tile):
        return remote(
            self.parts.at[tile, :, 1 - self.me.side], self.y_land.at[tile],
            self.y_send.at[tile], self.y_recv.at[tile], self.me.to_side,
        )

    def up_copy(self, tile, count):
        slot = lax.rem(tile, 2)
        return remote(
            self.up_buf.at[slot, 0:count], self.up_land.at[tile, 0:count],
            self.up_send.at[slot], self.up_recv.at[tile], self.me.to_up,
        )

    def down_copy(self, tile, count):
        slot = lax.rem(tile, 2)
        return remote(
            self.down_buf.at[slot, 0:count], self.down_land.at[tile, 0:count],
            self.down_send.at[slot], self.down_recv.at[tile], self.me.to_down,
        )

    def await_up(self, tile, count):
        land = self.up_land.at[tile, 0:count]
        remote(land, land, self.up_send.at[0], self.up_recv.at[tile], self.me.to_up).wait_recv()

    def await_down(self, tile, count):
        land = self.down_land.at[tile, 0:count]
        remote(
            land, land, self.down_send.at[0], self.down_recv.at[tile], self.me.to_down
        ).wait_recv()

    @property
    def slots(self):
        return self.tiles + self.line + 2

    def use(self, buffers):
        (self.own, self.got, self.ring, self.up_buf, self.down_buf,
         self.up_load, self.down_load, self.last) = buffers

    def step(self, s, emit):
        me, line, tiles = self.me, self.line, self.tiles
        depth = self.ring.shape[0]

        @pl.when(s + self.ahead < tiles)
        def _():
            self.y_copy(s + self.ahead).start()

        @pl.when(s < tiles)
        def _():
            self.y_copy(s).wait()
            a = fetch(self.parts.at[s, :, me.side], self.own, self.local.at[0])
            b = fetch(self.y_land.at[s], self.got, self.local.at[1])
            a.wait()
            b.wait()
            self.ring[lax.rem(s, depth)] = self.own[...] + self.got[...]

        for k in range(line - 1):
            tile, count = s - 1 - k, line - 1 - k

            @pl.when((me.spot == k) & (tile >= 0) & (tile < tiles))
            def _(k=k, tile=tile, count=count):
                slot, held = lax.rem(tile, 2), lax.rem(tile, depth)

                @pl.when(tile >= 2)
                def _():
                    self.up_copy(tile, count).wait_send()

                if k > 0:
                    self.await_up(tile, count + 1)
                    fetch(
                        self.up_land.at[tile, 1 : count + 1], self.up_load.at[0:count],
                        self.local.at[2],
                    ).wait()
                    self.up_buf[slot, 0:count] = (
                        self.ring[held, k + 1 : line] + self.up_load[0:count]
                    )
                else:
                    self.up_buf[slot, 0:count] = self.ring[held, k + 1 : line]
                self.up_copy(tile, count).start()

        for k in range(1, line):
            tile, count = s - 1 - (line - 1 - k), k

            @pl.when((me.spot == k) & (tile >= 0) & (tile < tiles))
            def _(k=k, tile=tile, count=count):
                slot, held = lax.rem(tile, 2), lax.rem(tile, depth)

                @pl.when(tile >= 2)
                def _():
                    self.down_copy(tile, count).wait_send()

                if k < line - 1:
                    self.await_down(tile, count + 1)
                    fetch(
                        self.down_land.at[tile, 0:count], self.down_load.at[0:count],
                        self.local.at[3],
                    ).wait()
                    self.down_buf[slot, 0:count] = (
                        self.ring[held, 0:count] + self.down_load[0:count]
                    )
                else:
                    self.down_buf[slot, 0:count] = self.ring[held, 0:count]
                self.down_copy(tile, count).start()

        tile = s - 1 - line

        @pl.when((tile >= 0) & (tile < tiles))
        def _():
            held = lax.rem(tile, depth)
            self.last[2] = self.ring[held, me.spot]

            @pl.when(me.spot == line - 1)
            def _():
                self.await_up(tile, 1)

            @pl.when(me.spot == 0)
            def _():
                self.await_down(tile, 1)

            @pl.when(me.spot > 0)
            def _():
                fetch(self.up_land.at[tile, 0], self.last.at[0], self.local.at[4]).wait()
                self.last[2] = self.last[2] + self.last[0]

            @pl.when(me.spot < line - 1)
            def _():
                fetch(self.down_land.at[tile, me.spot], self.last.at[1], self.local.at[5]).wait()
                self.last[2] = self.last[2] + self.last[1]

            emit(tile, self.last.at[2])

    def finish(self):
        me, line = self.me, self.line
        for k in range(line - 1):
            @pl.when(me.spot == k)
            def _(k=k):
                for tile in range(max(0, self.tiles - 2), self.tiles):
                    self.up_copy(tile, line - 1 - k).wait_send()

        for k in range(1, line):
            @pl.when(me.spot == k)
            def _(k=k):
                for tile in range(max(0, self.tiles - 2), self.tiles):
                    self.down_copy(tile, k).wait_send()


class NarrowSum:
    @staticmethod
    def lands(chunks, quarter, width):
        return [
            jax.ShapeDtypeStruct((chunks, 2, quarter, width), f32),
            jax.ShapeDtypeStruct((chunks, quarter, width), f32),
            jax.ShapeDtypeStruct((chunks, quarter, width), f32),
            jax.ShapeDtypeStruct((chunks, 2, quarter, width), f32),
        ]

    @staticmethod
    def sems(chunks):
        dma = pltpu.SemaphoreType.DMA
        return [dma((chunks,)) for _ in range(8)] + [dma((5,))]

    @staticmethod
    def buffers(quarter, width):
        return [
            pltpu.VMEM((2, 2, 2, quarter, width), f32),
            pltpu.VMEM((2, quarter, width), f32),
            pltpu.VMEM((2, 2, quarter, width), f32),
            pltpu.VMEM((quarter, width), f32),
            pltpu.VMEM((2, quarter, width), f32),
            pltpu.VMEM((2, 2, quarter, width), f32),
            pltpu.VMEM((2, quarter, width), f32),
            pltpu.VMEM((2, 2, quarter, width), bf16),
        ]

    def __init__(self, me, lands, sems):
        self.me = me
        self.core_land, self.chip_land, self.back_land, self.last_land = lands
        (self.s0, self.r0, self.s1, self.r1, self.s2, self.r2, self.s3, self.r3, self.local) = sems
        self.chunks = self.chip_land.shape[0]

    def use(self, buffers):
        (self.part, self.core_load, self.half, self.chip_load,
         self.done, self.pair, self.last_load, self.low) = buffers

    def copies(self, stage, c):
        me, slot = self.me, lax.rem(c, 2)
        if stage == 0:
            return remote(self.part.at[slot, 1 - me.core], self.core_land.at[c],
                          self.s0.at[c], self.r0.at[c], me.to_core)
        if stage == 1:
            return remote(self.half.at[slot, 1 - me.chip], self.chip_land.at[c],
                          self.s1.at[c], self.r1.at[c], me.to_chip)
        if stage == 2:
            return remote(self.done.at[slot], self.back_land.at[c],
                          self.s2.at[c], self.r2.at[c], me.to_chip)
        return remote(self.pair.at[slot], self.last_land.at[c],
                      self.s3.at[c], self.r3.at[c], me.to_core)

    @property
    def slots(self):
        return self.chunks + 4

    def step(self, s, produce, work, lower, emit):
        me = self.me

        def stage(number, body):
            c = s - number

            @pl.when((c >= 0) & (c < self.chunks))
            def _():
                if number > 0:
                    self.copies(number - 1, c).wait()
                body(c, lax.rem(c, 2))
                if number < 4:
                    self.copies(number, c).start()

        def four(c, slot):
            fetch(self.last_land.at[c], self.last_load, self.local.at[3]).wait()
            self.low[me.core] = lower(self.pair[slot])
            self.low[1 - me.core] = lower(self.last_load[...])
            emit(c, self.low)

        def three(c, slot):
            fetch(self.back_land.at[c], self.pair.at[slot, 1 - me.chip], self.local.at[2]).wait()
            self.pair[slot, me.chip] = self.done[slot]

        def two(c, slot):
            fetch(self.chip_land.at[c], self.chip_load, self.local.at[1]).wait()
            self.done[slot] = work(c, self.half[slot, me.chip] + self.chip_load[...])

        def one(c, slot):
            fetch(self.core_land.at[c], self.core_load, self.local.at[0]).wait()
            self.half[slot] = self.part[slot, me.core] + self.core_load[...]

        def zero(c, slot):
            produce(c, self.part.at[slot])

        stage(4, four)
        stage(3, three)
        stage(2, two)
        stage(1, one)
        stage(0, zero)


def take(refs, count):
    return refs[:count], refs[count:]


def store_part(part, value, columns):
    half, quarter = 2, value.shape[0] // 4
    part[:, :, :, columns] = value.reshape(half, 2, quarter, value.shape[1])


def norm_back(pulled, unit, scale, gain):
    scaled = pulled * gain
    return scale * (scaled - unit * jnp.mean(scaled * unit, axis=-1, keepdims=True))


def half_turn(values):
    return pltpu.roll(values, values.shape[-1] // 2, values.ndim - 1)


def allowed_pairs(keys, rows, starts):
    count = rows.stop - rows.start
    key = lax.broadcasted_iota(jnp.int32, (keys, count), 0)
    query = lax.broadcasted_iota(jnp.int32, (keys, count), 1) + rows.start
    return (key <= query) & (key >= starts)


def attend_kernel(wide, chunks, *refs):
    (tokens, cot, w_query, w_key, w_value, w_output, attn_gain, mlp_gain, query_gain, key_gain,
     cosine, sine, starts), refs = take(refs, 13)
    (mlp_in, mlp_in_t, cot_t, normed_t, hidden_out, q_out, k_out, v_out, q_raw_out, k_raw_out,
     context_out, lse_out), refs = take(refs, 12)
    lands, refs = take(refs, 4)
    sems, refs = take(refs, 9)
    buffers, refs = take(refs, 8)
    (hidden_buf, q_low, k_low, v_low, v_t, q_raw, k_raw, context, lse, normed, normed_turn,
     cot_load, cot_turn, low_turn, sem, out_sem) = refs
    me = Spot(wide)
    me.greet(False)
    summing = NarrowSum(me, lands, sems)
    summing.use(buffers)
    token_count, width = tokens.shape
    rows = token_count // chunks
    quarter = rows // 4
    block = normed.shape[0]
    per_block = block // rows
    head = query_gain.shape[1]
    q_heads = w_query.shape[1] // head
    group = q_heads // (w_key.shape[1] // head)
    scale = head ** (-0.5)
    step = min(512, width)
    kept = (
        (q_low, q_out), (k_low, k_out), (v_low, v_out), (q_raw, q_raw_out), (k_raw, k_raw_out),
        (context, context_out), (lse, lse_out),
    )

    def attend(i):
        own = slice(i * block, (i + 1) * block)
        keys = (i + 1) * block
        x = tokens[own, :].astype(f32)
        normed[...] = (x * inverse_rms(x) * attn_gain[...]).astype(bf16)
        cos, sin = cosine[own, :], sine[own, :]

        def heads_of(raw, low, gain):
            for h in range(raw.shape[1] // head):
                cut = slice(h * head, (h + 1) * head)
                u = raw[own, cut]
                y = u * inverse_rms(u) * gain[...]
                low[own, cut] = (y * cos + half_turn(y) * sin).astype(bf16)

        q_raw[own, :] = forward_dot(normed[...], w_query[...])
        k_raw[own, :] = forward_dot(normed[...], w_key[...])
        value = forward_dot(normed[...], w_value[...])
        v_low[own, :] = value.astype(bf16)
        v_t[:, own] = value.T.astype(bf16)
        heads_of(q_raw, q_low, query_gain)
        heads_of(k_raw, k_low, key_gain)
        allowed = allowed_pairs(keys, own, starts[:, own])
        for h in range(q_heads):
            cut, kv = slice(h * head, (h + 1) * head), h // group
            kv_cut = slice(kv * head, (kv + 1) * head)
            scores = nt_dot(k_low[0:keys, kv_cut], q_low[own, cut]) * scale
            scores = jnp.where(allowed, scores, masked_score)
            top = jnp.max(scores, axis=0, keepdims=True)
            expd = jnp.exp(scores - top)
            total = jnp.sum(expd, axis=0, keepdims=True)
            probs = (expd / total).astype(bf16)
            lse[h : h + 1, own] = top + jnp.log(total)
            mixed = forward_dot(v_t[kv_cut, 0:keys], probs)
            context[own, cut] = mixed.T.astype(bf16)

    def produce(c, part):
        for i in range(token_count // block):
            pl.when(c == i * per_block)(functools.partial(attend, i))
        left = context[pl.ds(pl.multiple_of(c * rows, rows), rows), :]
        for at in range(0, width, step):
            store_part(part, forward_dot(left, w_output[:, at : at + step]), slice(at, at + step))

    def work(c, total):
        at = pl.multiple_of(c * rows + me.core * 2 * quarter + me.chip * quarter, quarter)
        hidden = tokens[pl.ds(at, quarter), :].astype(f32) + total
        hidden_buf[...] = hidden
        fetch(hidden_buf, hidden_out.at[c], sem.at[1]).wait()
        return hidden * inverse_rms(hidden)

    def lower(value):
        return (value * mlp_gain[...]).astype(bf16)

    def emit(c, low):
        a = fetch(low, mlp_in.at[c], sem.at[0])
        low_turn[...] = low[...].reshape(rows, width).T
        at = pl.ds(pl.multiple_of(c * rows, rows), rows)
        fetch(low_turn, mlp_in_t.at[:, at], sem.at[1]).wait()
        a.wait()

    def turn_rows(s):
        at = pl.ds(pl.multiple_of(s * rows, rows), rows)
        fetch(cot.at[at, :], cot_load, sem.at[0]).wait()
        cot_turn[...] = cot_load[...].T
        a = fetch(cot_turn, cot_t.at[:, at], sem.at[1])

        @pl.when(lax.rem(s, per_block) == 0)
        def _():
            normed_turn[...] = normed[...].T
            wide_at = pl.ds(pl.multiple_of(s * rows, block), block)
            fetch(normed_turn, normed_t.at[:, wide_at], sem.at[0]).wait()

        a.wait()

    def body(s, carry):
        summing.step(s, produce, work, lower, emit)
        pl.when(s < chunks)(lambda: turn_rows(s))

        @pl.when(s == chunks - 1)
        def _():
            for at, (a, b) in enumerate(kept):
                fetch(a, b, out_sem.at[at])

        return carry

    lax.fori_loop(0, summing.slots, body, 0)
    for at, (a, b) in enumerate(kept):
        pltpu.make_async_copy(a, b, out_sem.at[at]).wait()


def outer_tile(left_t, right, stage):
    line, _, rows, _ = stage.shape
    group = max(1, 512 // (2 * rows))
    while line % group:
        group -= 1

    def body(m, carry):
        at = pl.multiple_of(m * group * 2 * rows, group * 2 * rows)
        value = forward_dot(left_t[pl.ds(at, group * 2 * rows), :], right)
        stage[pl.ds(m * group, group)] = value.reshape((group, 2, rows, value.shape[1]))
        return carry

    lax.fori_loop(0, line // group, body, 0)


class SmallSum:
    def __init__(self, me, value, lands, sends, recvs):
        self.me, self.value, self.lands, self.sends, self.recvs = me, value, lands, sends, recvs

    def copy(self, k):
        me = self.me
        who = (me.to_core, me.to_chip, me.to_side)[k] if k < 3 else me.along(k - 2)
        return remote(self.value, self.lands.at[k], self.sends.at[k], self.recvs.at[k], who)

    def step(self, at):
        last = 2 + self.me.line
        stages = [[0], [1], [2], list(range(3, last)), []]
        for number, copies in enumerate(stages):
            @pl.when(at == number)
            def _(number=number, copies=copies):
                if number > 0:
                    for k in stages[number - 1]:
                        self.copy(k).wait()
                    for k in stages[number - 1]:
                        self.value[...] = self.value[...] + self.lands[k]
                for k in copies:
                    self.copy(k).start()


def main_kernel(wide, chunks, *refs):
    (mlp_in, mlp_in_t, cot, cot_t, normed_t, hidden, q_in, k_in, v_in, q_raw, k_raw, context,
     lse_in, tokens, w_gate, w_up, w_down, w_output, w_query, w_key, w_value, cosine, sine,
     starts, attn_gain, mlp_gain, query_gain, key_gain), refs = take(refs, 28)
    (output, grad_tokens, grad_query, grad_key, grad_value, grad_output, grad_gate, grad_up,
     grad_down, gains_out, grad_hidden), refs = take(refs, 11)
    wide_lands, refs = take(refs, 4)
    lands, refs = take(refs, 4)
    wide_sems, refs = take(refs, 7)
    sems, refs = take(refs, 9)
    acts, gains, gain_lands, gain_send, gain_recv, sem, w_sem, store_sem = refs
    me = Spot(wide)
    me.greet(True)
    token_count, width = mlp_in.shape
    hidden_units = w_gate.shape[1]
    tiles, line, _, side_rows, cols = wide_lands[0].shape
    blocks = hidden_units // cols
    mlp_tiles = 3 * blocks
    query_width, kv_width = w_query.shape[1], w_key.shape[1]
    all_heads = query_width + 2 * kv_width
    head = query_gain.shape[1]
    q_heads = query_width // head
    group = q_heads // (kv_width // head)
    scale = head ** (-0.5)
    out_tiles = query_width // cols
    total = WideSum(me, wide_lands, wide_sems)
    half = token_count // 2
    rows = token_count // chunks
    quarter = rows // 4

    def compute(xs, xt, cs, ct, gate_w, up_w, down_w, staged):
        pairs = ((mlp_in, xs), (cot, cs), (cot_t, ct), (mlp_in_t, xt))
        for at, (a, b) in enumerate(pairs):
            fetch(a, b, sem.at[at])

        def weights(b, slot):
            at = pl.ds(pl.multiple_of(b * cols, cols), cols)
            return (
                pltpu.make_async_copy(w_gate.at[:, at], gate_w.at[slot], w_sem.at[slot, 0]),
                pltpu.make_async_copy(w_up.at[:, at], up_w.at[slot], w_sem.at[slot, 1]),
                pltpu.make_async_copy(w_down.at[at, :], down_w.at[slot], w_sem.at[slot, 2]),
            )

        for copy in weights(0, 0):
            copy.start()
        for at, (a, b) in enumerate(pairs):
            pltpu.make_async_copy(a, b, sem.at[at]).wait()

        def store(tile):
            slot = lax.rem(tile, 2)
            return pltpu.make_async_copy(staged.at[slot], total.parts.at[tile], store_sem.at[slot])

        def block(b, carry):
            slot = lax.rem(b, 2)
            for copy in weights(b, slot):
                copy.wait()

            @pl.when(b + 1 < blocks)
            def _():
                for copy in weights(b + 1, 1 - slot):
                    copy.start()

            at = pl.ds(pl.multiple_of(b * cols, cols), cols)

            def some(m, carry):
                own = pl.ds(pl.multiple_of(m * half, half), half)
                gate = forward_dot(xs[own, :], gate_w[slot])
                up = forward_dot(xs[own, :], up_w[slot])
                back = nt_dot(cs[own, :], down_w[slot])
                sig = 1.0 / (1.0 + jnp.exp(-gate))
                silu = gate * sig
                acts[0, own, at] = (silu * up).astype(bf16)
                acts[1, own, at] = (back * up * sig * (1.0 + gate * (1.0 - sig))).astype(bf16)
                acts[2, own, at] = (back * silu).astype(bf16)
                return carry

            lax.fori_loop(0, 2, some, 0)
            for j in range(3):
                tile = 3 * b + j

                @pl.when(tile >= 2)
                def _(tile=tile):
                    store(tile - 2).wait()

                    @pl.when(tile - 2 < total.ahead)
                    def _():
                        total.y_copy(tile - 2).start()

                outer_tile(ct if j == 0 else xt, acts[j, :, at], staged.at[lax.rem(tile, 2)])
                store(tile).start()
            return carry

        lax.fori_loop(0, blocks, block, 0)
        for tile in range(mlp_tiles - 2, mlp_tiles):
            store(tile).wait()

    pl.run_scoped(
        compute,
        pltpu.VMEM(mlp_in.shape, bf16),
        pltpu.VMEM(mlp_in_t.shape, bf16),
        pltpu.VMEM(mlp_in.shape, bf16),
        pltpu.VMEM(mlp_in_t.shape, bf16),
        pltpu.VMEM((2, width, cols), bf16),
        pltpu.VMEM((2, width, cols), bf16),
        pltpu.VMEM((2, cols, width), bf16),
        pltpu.VMEM((2, line, 2, side_rows, cols), f32),
    )

    def pass_on(*held):
        wide_buffers, held = take(held, 8)
        buffers, held = take(held, 8)
        (gate_w, up_w, down_w, hidden_load, token_load, out_buf, out_w, left_t, staged, q_low,
         k_low, v_low, k_t, d_context, right, lse, cos, sin, raw, d_query, d_key, d_value,
         heads, turned) = held
        total.use(wide_buffers)
        summing = NarrowSum(me, lands, sems)
        summing.use(buffers)
        small = SmallSum(me, gains, gain_lands, gain_send, gain_recv)
        gains[...] = jnp.zeros_like(gains)
        gain_at = (
            slice(0, width), slice(width, 2 * width), slice(2 * width, 2 * width + head),
            slice(2 * width + head, 2 * width + 2 * head),
        )
        loads = ((w_output, out_w), (q_in, q_low), (k_in, k_low), (v_in, v_low), (lse_in, lse),
                 (cosine, cos), (sine, sin))
        for a, b in loads:
            fetch(a, b, sem.at[0]).wait()
        k_t[...] = k_low[...].T
        step = gate_w.shape[1]
        first_attend = chunks + 4
        first_heads = first_attend + q_heads

        def stream(copies, use):
            count = width // step
            for copy in copies(0, 0):
                copy.start()
            for at in range(count):
                if at + 1 < count:
                    for copy in copies(at + 1, (at + 1) % 2):
                        copy.start()
                for copy in copies(at, at % 2):
                    copy.wait()
                use(at % 2, slice(at * step, (at + 1) * step))

        def produce(c, part):
            chunk = lax.rem(c, chunks)
            own = pl.ds(pl.multiple_of(chunk * rows, rows), rows)
            kind = lax.div(c, chunks)

            @pl.when(kind == 0)
            def _():
                def copies(at, slot):
                    cut = pl.ds(at * step, step)
                    gate = gate_w.at[slot, :, 0:hidden_units]
                    return (
                        pltpu.make_async_copy(w_gate.at[cut, :], gate, w_sem.at[slot, 0]),
                        pltpu.make_async_copy(w_up.at[cut, :], up_w.at[slot], w_sem.at[slot, 1]),
                    )

                def use(slot, cut):
                    value = nt_dot(acts[1, own, :], gate_w[slot, :, 0:hidden_units])
                    store_part(part, value + nt_dot(acts[2, own, :], up_w[slot]), cut)

                stream(copies, use)

            @pl.when(kind == 1)
            def _():
                def copies(at, slot):
                    cut = pl.ds(at * step, step)
                    return (
                        pltpu.make_async_copy(w_down.at[:, cut], down_w.at[slot], w_sem.at[slot, 2]),
                    )

                def use(slot, cut):
                    store_part(part, forward_dot(acts[0, own, :], down_w[slot]), cut)

                stream(copies, use)

            @pl.when(kind == 2)
            def _():
                def copies(at, slot):
                    cut, start, found = pl.ds(at * step, step), 0, []
                    for j, w in enumerate((w_query, w_key, w_value)):
                        there = gate_w.at[slot, :, start : start + w.shape[1]]
                        found.append(pltpu.make_async_copy(w.at[cut, :], there, w_sem.at[slot, j]))
                        start += w.shape[1]
                    return found

                def use(slot, cut):
                    store_part(part, nt_dot(heads[own, :], gate_w[slot, :, 0:all_heads]), cut)

                stream(copies, use)

        def work(c, pulled):
            chunk = lax.rem(c, chunks)
            kind = lax.div(c, chunks)

            @pl.when(kind == 0)
            def _():
                a = fetch(hidden.at[chunk], hidden_load, sem.at[0])
                b = fetch(cot.at[own_rows(chunk), :], token_load, sem.at[1])
                a.wait()
                b.wait()
                mid = hidden_load[...]
                inverse = inverse_rms(mid)
                unit = mid * inverse
                gains[:, gain_at[1]] += jnp.sum(pulled * unit, axis=0, keepdims=True)
                back = norm_back(pulled, unit, inverse, mlp_gain[...])
                out_buf[...] = token_load[...].astype(f32) + back
                fetch(out_buf, grad_hidden.at[chunk], sem.at[0]).wait()

            @pl.when(kind == 1)
            def _():
                fetch(hidden.at[chunk], hidden_load, sem.at[0]).wait()
                out_buf[...] = hidden_load[...] + pulled

            @pl.when(kind == 2)
            def _():
                a = fetch(grad_hidden.at[chunk], hidden_load, sem.at[0])
                b = fetch(tokens.at[own_rows(chunk), :], token_load, sem.at[1])
                a.wait()
                b.wait()
                mid = token_load[...].astype(f32)
                inverse = inverse_rms(mid)
                unit = mid * inverse
                gains[:, gain_at[0]] += jnp.sum(pulled * unit, axis=0, keepdims=True)
                out_buf[...] = hidden_load[...] + norm_back(pulled, unit, inverse, attn_gain[...])

            return out_buf[...]

        def own_rows(chunk):
            at = chunk * rows + me.core * 2 * quarter + me.chip * quarter
            return pl.ds(pl.multiple_of(at, quarter), quarter)

        def lower(value):
            return value.astype(bf16)

        def emit_rows(c, low):
            chunk = lax.rem(c, chunks)
            kind = lax.div(c, chunks)

            @pl.when(kind == 0)
            def _():
                own = pl.ds(pl.multiple_of(chunk * rows, rows), rows)
                value = low[...].reshape(rows, width)
                d_context[own, :] = nt_dot(value, out_w[...]).astype(bf16)
                left_t[:, own] = value.T

            @pl.when(kind == 1)
            def _():
                fetch(low, output.at[chunk], sem.at[0]).wait()

            @pl.when(kind == 2)
            def _():
                fetch(low, grad_tokens.at[chunk], sem.at[0]).wait()

        def put(tile, right_value):
            outer_tile(left_t, right_value, staged)
            fetch(staged, total.parts.at[tile], store_sem.at[0]).wait()

        def rope_norm_back(grad, raw_value, gain, at):
            scaled = grad * cos[...] - half_turn(grad) * sin[...]
            inverse = inverse_rms(raw_value)
            unit = raw_value * inverse
            gains[:, at] += jnp.sum(scaled * unit, axis=0, keepdims=True)
            return norm_back(scaled, unit, inverse, gain[...])

        def attend_back(h):
            kv = lax.div(h, group)
            cut = pl.ds(pl.multiple_of(h * head, head), head)
            kv_cut = pl.ds(pl.multiple_of(kv * head, head), head)

            @pl.when(lax.rem(h, group) == 0)
            def _():
                d_key[...] = jnp.zeros_like(d_key)
                d_value[...] = jnp.zeros_like(d_value)

            load = fetch(q_raw.at[:, cut], raw, sem.at[0])
            size = min(256, token_count)
            for i in range(token_count // size):
                own, keys = slice(i * size, (i + 1) * size), (i + 1) * size
                q, dc = q_low[own, cut], d_context[own, cut]
                scores = nt_dot(k_low[0:keys, kv_cut], q) * scale
                expd = jnp.exp(scores - lse[pl.ds(h, 1), own])
                probs = jnp.where(allowed_pairs(keys, own, starts[:, own]), expd, 0.0)
                d_value[0:keys, :] += forward_dot(probs.astype(bf16), dc)
                d_probs = nt_dot(v_low[0:keys, kv_cut], dc)
                mean = jnp.sum(probs * d_probs, axis=0, keepdims=True)
                d_scores = (probs * (d_probs - mean)).astype(bf16)
                d_key[0:keys, :] += forward_dot(d_scores, q)
                d_query[own, :] = forward_dot(k_t[kv_cut, 0:keys], d_scores).T
            load.wait()
            heads[:, cut] = rope_norm_back(
                d_query[...] * scale, raw[...], query_gain, gain_at[2]
            ).astype(bf16)

            @pl.when(lax.rem(h, group) == group - 1)
            def _():
                fetch(k_raw.at[:, kv_cut], raw, sem.at[0]).wait()
                there = pl.ds(pl.multiple_of(query_width + kv * head, head), head)
                heads[:, there] = rope_norm_back(
                    d_key[...] * scale, raw[...], key_gain, gain_at[3]
                ).astype(bf16)
                there = pl.ds(pl.multiple_of(query_width + kv_width + kv * head, head), head)
                heads[:, there] = d_value[...].astype(bf16)

        def emit_tile(tile, value):
            def part(first, count, target, turn, every=1, offset=0):
                inside = (tile >= first) & (tile < first + count)
                at = tile - first
                if every > 1:
                    inside = inside & (lax.rem(at, every) == offset)
                    at = lax.div(at, every)

                @pl.when(inside)
                def _():
                    cut = pl.ds(pl.multiple_of(at * cols, cols), cols)
                    if turn:
                        turned[...] = value[...].T
                        fetch(turned, target.at[cut, :], sem.at[0]).wait()
                    else:
                        fetch(value, target.at[:, cut], sem.at[0]).wait()

            part(0, mlp_tiles, grad_down, True, 3, 0)
            part(0, mlp_tiles, grad_gate, False, 3, 1)
            part(0, mlp_tiles, grad_up, False, 3, 2)
            at = mlp_tiles
            part(at, out_tiles, grad_output, True)
            at += out_tiles
            part(at, query_width // cols, grad_query, False)
            at += query_width // cols
            part(at, kv_width // cols, grad_key, False)
            at += kv_width // cols
            part(at, kv_width // cols, grad_value, False)

        small_at = summing.slots - 1

        def body(s, carry):
            @pl.when(s == first_attend)
            def _():
                for t in range(out_tiles):
                    cut = slice(t * cols, (t + 1) * cols)
                    fetch(context.at[:, cut], right, sem.at[0]).wait()
                    put(mlp_tiles + t, right[...])

            @pl.when((s >= first_attend) & (s < first_heads))
            def _():
                attend_back(s - first_attend)

            @pl.when(s == first_heads)
            def _():
                fetch(normed_t, left_t, sem.at[0]).wait()

                def one(t, carry):
                    put(mlp_tiles + out_tiles + t, heads[:, pl.ds(pl.multiple_of(t * cols, cols), cols)])
                    return carry

                lax.fori_loop(0, all_heads // cols, one, 0)

            pl.when(s < total.slots)(lambda: total.step(s, emit_tile))
            pl.when(s < summing.slots)(
                lambda: summing.step(s, produce, work, lower, emit_rows)
            )
            pl.when(s >= small_at)(lambda: small.step(s - small_at))
            return carry

        lax.fori_loop(0, max(total.slots, small_at + 5), body, 0)
        total.finish()

    step = min(256, width)
    pl.run_scoped(
        pass_on,
        *WideSum.buffers(line, side_rows, cols),
        *NarrowSum.buffers(quarter, width),
        pltpu.VMEM((2, step, max(hidden_units, all_heads)), bf16),
        pltpu.VMEM((2, step, hidden_units), bf16),
        pltpu.VMEM((2, hidden_units, step), bf16),
        pltpu.VMEM((quarter, width), f32),
        pltpu.VMEM((quarter, width), bf16),
        pltpu.VMEM((quarter, width), f32),
        pltpu.VMEM(w_output.shape, bf16),
        pltpu.VMEM(normed_t.shape, bf16),
        pltpu.VMEM((line, 2, side_rows, cols), f32),
        pltpu.VMEM(q_in.shape, bf16),
        pltpu.VMEM(k_in.shape, bf16),
        pltpu.VMEM(v_in.shape, bf16),
        pltpu.VMEM((kv_width, token_count), bf16),
        pltpu.VMEM(q_in.shape, bf16),
        pltpu.VMEM((token_count, cols), bf16),
        pltpu.VMEM(lse_in.shape, f32),
        pltpu.VMEM(cosine.shape, f32),
        pltpu.VMEM(sine.shape, f32),
        pltpu.VMEM((token_count, head), f32),
        pltpu.VMEM((token_count, head), f32),
        pltpu.VMEM((token_count, head), f32),
        pltpu.VMEM((token_count, head), f32),
        pltpu.VMEM((token_count, all_heads), bf16),
        pltpu.VMEM((cols, side_rows), f32),
    )
    fetch(gains, gains_out, sem.at[0]).wait()


def call(kernel, collective_id, out_shape, in_specs, out_specs, scratch, arrays):
    return pl.pallas_call(
        kernel,
        out_shape=out_shape,
        in_specs=in_specs,
        out_specs=out_specs,
        scratch_shapes=scratch,
        compiler_params=pltpu.CompilerParams(
            collective_id=collective_id,
            has_side_effects=True,
            vmem_limit_bytes=62 * 1024 * 1024,
        ),
    )(*arrays)


def per_device(
    wide,
    tokens,
    seq_lengths,
    attn_gain,
    w_query,
    key_weight,
    value_weight,
    query_gain,
    key_norm_gain,
    w_output,
    mlp_gain,
    w_gate,
    w_up,
    w_down,
    cotangent,
):
    token_count, width = tokens.shape
    head_dim = query_gain.shape[0]
    query_width, kv_width = w_query.shape[1], key_weight.shape[1]
    hidden_units = w_gate.shape[1]
    all_heads = query_width + 2 * kv_width
    line = wide // 2
    side_rows = width // wide
    chunks = 8
    rows = token_count // chunks
    quarter = rows // 4
    block = min(256, token_count)
    dma = pltpu.SemaphoreType.DMA
    shape = jax.ShapeDtypeStruct

    segment_index, token_positions = layout(seq_lengths, token_count)
    token_positions = token_positions.reshape(-1)
    starts = (jnp.arange(token_count, dtype=jnp.int32) - token_positions)[None]
    cosine, sine = tables(token_positions, head_dim)
    cosine = cosine.reshape(token_count, head_dim)
    sign = jnp.where(jnp.arange(head_dim) < head_dim // 2, -1.0, 1.0).astype(f32)
    sine = sine.reshape(token_count, head_dim) * sign
    q_heads = query_width // head_dim

    kept = [
        shape((token_count, query_width), bf16),
        shape((token_count, kv_width), bf16),
        shape((token_count, kv_width), bf16),
        shape((token_count, query_width), f32),
        shape((token_count, kv_width), f32),
        shape((token_count, query_width), bf16),
        shape((q_heads, token_count), f32),
    ]
    vmem = [pltpu.VMEM(k.shape, k.dtype) for k in kept]
    outs = call(
        lambda *refs: attend_kernel(wide, chunks, *refs),
        1,
        [
            shape((chunks, 2, 2, quarter, width), bf16),
            shape((width, token_count), bf16),
            shape((width, token_count), bf16),
            shape((width, token_count), bf16),
            shape((chunks, quarter, width), f32),
            *kept,
            *NarrowSum.lands(chunks, quarter, width),
        ],
        [in_vmem, any_space] + [in_vmem] * 11,
        [any_space] * 16,
        [
            *NarrowSum.sems(chunks),
            *NarrowSum.buffers(quarter, width),
            pltpu.VMEM((quarter, width), f32),
            *vmem[:3],
            pltpu.VMEM((kv_width, token_count), bf16),
            *vmem[3:],
            pltpu.VMEM((block, width), bf16),
            pltpu.VMEM((width, block), bf16),
            pltpu.VMEM((rows, width), bf16),
            pltpu.VMEM((width, rows), bf16),
            pltpu.VMEM((width, rows), bf16),
            dma((2,)),
            dma((7,)),
        ],
        (
            tokens, cotangent, w_query, key_weight, value_weight, w_output, attn_gain[None],
            mlp_gain[None], query_gain[None], key_norm_gain[None], cosine, sine, starts,
        ),
    )
    (mlp_in, mlp_in_t, cot_t, normed_t, hidden, q_low, k_low, v_low, q_raw, k_raw, context,
     lse) = outs[:12]

    cols = min(256 if line <= 4 else 128, hidden_units // 6)
    tiles = (3 * hidden_units + query_width + all_heads) // cols
    gain_width = 2 * width + 2 * head_dim
    outs = call(
        lambda *refs: main_kernel(wide, chunks, *refs),
        2,
        [
            shape((chunks, 2, 2, quarter, width), bf16),
            shape((chunks, 2, 2, quarter, width), bf16),
            shape((side_rows, query_width), f32),
            shape((side_rows, kv_width), f32),
            shape((side_rows, kv_width), f32),
            shape((query_width, side_rows), f32),
            shape((side_rows, hidden_units), f32),
            shape((side_rows, hidden_units), f32),
            shape((hidden_units, side_rows), f32),
            shape((1, gain_width), f32),
            shape((chunks, quarter, width), f32),
            *WideSum.lands(tiles, line, side_rows, cols),
            *NarrowSum.lands(3 * chunks, quarter, width),
        ],
        [any_space] * 23 + [in_vmem] * 5,
        [any_space] * 19,
        [
            *WideSum.sems(tiles),
            *NarrowSum.sems(3 * chunks),
            pltpu.VMEM((3, token_count, hidden_units), bf16),
            pltpu.VMEM((1, gain_width), f32),
            pltpu.VMEM((2 + line, 1, gain_width), f32),
            dma((2 + line,)),
            dma((2 + line,)),
            dma((4,)),
            dma((2, 3)),
            dma((2,)),
        ],
        (
            mlp_in.reshape(token_count, width), mlp_in_t, cotangent, cot_t, normed_t, hidden,
            q_low, k_low, v_low, q_raw, k_raw, context, lse, tokens, w_gate, w_up, w_down,
            w_output, w_query, key_weight, value_weight, cosine, sine, starts, attn_gain[None],
            mlp_gain[None], query_gain[None], key_norm_gain[None],
        ),
    )
    (output, grad_tokens, shard_query, shard_key, shard_value, shard_output, shard_gate,
     shard_up, shard_down, gains) = outs[:10]
    gains = gains[0]
    at = lax.axis_index("wide")
    head_part = head_dim // wide

    def own(start, size):
        return lax.dynamic_slice_in_dim(gains, start + at * size, size)

    return (
        output.reshape(token_count, width),
        grad_tokens.reshape(token_count, width),
        own(0, side_rows),
        shard_query,
        shard_key,
        shard_value,
        own(2 * width, head_part),
        own(2 * width + head_dim, head_part),
        shard_output,
        own(width, side_rows),
        shard_gate,
        shard_up,
        shard_down,
    )


def solution(mesh):
    def run(*arrays):
        return per_device(mesh.shape["wide"], *arrays)

    return jax.shard_map(
        run,
        mesh=mesh,
        in_specs=(
            P("wide", None),
            P("wide", None),
            P(),
            P(None, "narrow"),
            P(None, "narrow"),
            P(None, "narrow"),
            P(),
            P(),
            P("narrow", None),
            P(),
            P(None, "narrow"),
            P(None, "narrow"),
            P("narrow", None),
            P("wide", None),
        ),
        out_specs=(
            P("wide", None),
            P("wide", None),
            P("wide"),
            P("wide", "narrow"),
            P("wide", "narrow"),
            P("wide", "narrow"),
            P("wide"),
            P("wide"),
            P("narrow", "wide"),
            P("wide"),
            P("wide", "narrow"),
            P("wide", "narrow"),
            P("narrow", "wide"),
        ),
        check_vma=False,
    )
```

time: 1080 us -> 804 us (0.74)
  Pallas kernels: 830 us -> 768 us
  matrix products: 58.1 us -> 0 us
  local copies, waits for them, and re-layouts: 71.9 us -> 16 us
  blocking collectives: 50.3 us -> 0 us
  other arithmetic: 44.8 us -> 5.37 us
    pallas_call x3 -> x2, Pallas kernels: 830 us -> 768 us  [call(): pl.pallas_call(kernel, out_shape=out_shape, in_specs=in_specs, out_specs=...]
    dot_general x10 -> x0, matrix products: 58.1 us -> none  [the longest x1 11.2 us: per_device(): jnp.einsum('tkgd,skd->kgts', grad_context, value_low, preferred_element_t...]
    psum x1 -> x0, blocking collectives: 50.3 us -> none  [per_device(): gains = lax.psum(gains, ('wide', 'narrow'))]
    unnamed x100 -> x25, local copies, waits for them, and re-layouts: 36.8 us -> 13.5 us
    reduce_sum x4 -> x0, other arithmetic: 13.3 us -> none  [the longest x1 8.1 us: per_device(): row_total = jnp.sum(expd, axis=-1, keepdims=True)]
    convert_element_type x5 -> x0, other arithmetic: 13.2 us -> none  [the longest x1 8.38 us: per_device(): scores_low = grad_scores.astype(bf16)]
where the time goes in v2:
time: 804 us; the launch traced here: 790 us
  Pallas kernels  768 us (96%)
  local copies, waits for them, and re-layouts  16 us (2%)
    pallas_call x2, Pallas kernels, call(): pl.pallas_call(kernel, out_shape=out_shape, in_specs=in_specs, out_specs=...  768 us

profile of v2, /device:TPU:0, one launch (start us, length us, event | category | flops | bytes accessed | tf_op | source)
XLA Modules:
  0.0 789.7 jit_solution(8670642008854072834)
XLA Ops:
  0.6 0.8 reduce_window_sum.11
  1.5 0.1 convert_reduce_fusion
  1.6 0.7 subtract_bitcast_fusion
  2.2 0.1 select_reduce_fusion
  2.3 0.2 broadcast_multiply_fusion
  2.6 2.9 sine_multiply_fusion
  5.4 0.6 subtract_subtract_fusion.refs_12_.refs_23_
  6.0 131.7 %shard_map.237 = (bf16[8,2,2,32,2048]{4,3,2,1,0:T(8,128)(2,1)}, bf16[2048,1024]{1,0:T(8,128)(2,1)}, bf16[2048,1024]{1,0:T(8,128)(2,1)}, bf16[2048,1024]{1,0:T(8,...) custom-call(bf16[1024,2048]{1,0:T(8,128)(2,1)} %refs_13_.1, ...), custom_call_target="tpu_custom_call" | custom-call | tf_op jit(solution)/shard_map/pallas_call | solution.py:972
  137.8 635.9 %shard_map.238 = (bf16[8,2,2,32,2048]{4,3,2,1,0:T(8,128)(2,1)}, bf16[8,2,2,32,2048]{4,3,2,1,0:T(8,128)(2,1)}, f32[256,512]{1,0:T(8,128)}, f32[256,256]{1,0:T(8,1...) custom-call(bf16[1024,2048]{1,0:T(8,128)(2,1)} %bitcast.17, ...), custom_call_target="tpu_custom_call" | custom-call | tf_op jit(solution)/shard_map/pallas_call | solution.py:972
  773.7 1.3 constant_dynamic-slice_fusion.3
  774.9 1.2 fusion.2
  776.2 0.0 copy-start
  776.2 4.9 copy.36
  781.1 0.0 copy-done
  781.1 0.0 copy-start.5
  781.1 0.0 copy-start.4
  781.2 0.0 copy-start.3
  781.2 2.1 copy.37
  783.3 0.0 copy-done.5
  783.3 0.8 copy.38
  784.1 0.0 copy-done.7
  784.1 0.7 copy.39
  784.8 0.0 copy-done.6
  784.8 0.7 copy.40
  785.5 0.0 copy-done.4
  785.5 0.8 copy.41
  786.3 0.0 copy-done.3
  786.3 1.1 copy.42
  787.5 0.0 copy-done.2
  787.5 1.1 copy.43
  788.6 0.0 copy-done.1
  788.6 1.1 copy.44
  (7 shorter events, 0.0 us)
Async XLA Ops:
  776.2 4.9 copy-start
  781.1 2.2 copy-start.5
  781.1 3.0 copy-start.7
  781.1 3.7 copy-start.6
  781.1 4.4 copy-start.4
  781.2 5.2 copy-start.3
  783.3 4.2 copy-start.2
  784.1 4.5 copy-start.1

commit v3 on v2

--- a/solution.py
+++ b/solution.py
@@ -104,278 +104,377 @@
 
 
 class WideSum:
-    ahead = 4
+    group = 6
+    ahead = 3
 
     @staticmethod
-    def lands(tiles, line, rows, cols):
+    def lag(line):
+        return 2 if line <= 4 else 1
+
+    @classmethod
+    def counts(cls, tiles):
+        groups = tiles // cls.group
+        return groups, tiles - groups, tiles + groups
+
+    @classmethod
+    def lands(cls, tiles, line, rows, cols):
+        groups, firsts, items = cls.counts(tiles)
         return [
             jax.ShapeDtypeStruct((tiles, line, 2, rows, cols), f32),
-            jax.ShapeDtypeStruct((tiles, line, rows, cols), f32),
-            jax.ShapeDtypeStruct((tiles, line, rows, cols), f32),
-            jax.ShapeDtypeStruct((tiles, line, rows, cols), f32),
+            jax.ShapeDtypeStruct((firsts, line, rows, cols), f32),
+            jax.ShapeDtypeStruct((items, line - 1, rows, cols), f32),
+            jax.ShapeDtypeStruct((items, line - 1, rows, cols), f32),
+            jax.ShapeDtypeStruct((groups, rows, cols), f32),
         ]
 
-    @staticmethod
-    def sems(tiles):
+    @classmethod
+    def sems(cls, tiles):
         dma = pltpu.SemaphoreType.DMA
-        return [dma((tiles,)), dma((tiles,)), dma((2,)), dma((tiles,)), dma((2,)), dma((tiles,)), dma((6,))]
+        groups, firsts, items = cls.counts(tiles)
+        return [
+            dma((firsts,)), dma((firsts,)), dma((2,)), dma((items,)), dma((2,)), dma((items,)),
+            dma((groups,)), dma((groups,)), dma((7,)),
+        ]
 
     @staticmethod
     def buffers(line, rows, cols):
         tile = (line, rows, cols)
         return [
             pltpu.VMEM(tile, f32),
-            pltpu.VMEM(tile, f32),
-            pltpu.VMEM((line + 3,) + tile, f32),
+            pltpu.VMEM((WideSum.lag(line) * (line - 1) + 1,) + tile, f32),
             pltpu.VMEM((2, line - 1, rows, cols), f32),
             pltpu.VMEM((2, line - 1, rows, cols), f32),
             pltpu.VMEM((line - 1, rows, cols), f32),
             pltpu.VMEM((line - 1, rows, cols), f32),
-            pltpu.VMEM((3, rows, cols), f32),
+            pltpu.VMEM((6, rows, cols), f32),
         ]
 
-    def __init__(self, me, lands, sems):
+    def __init__(self, me, lands, sems, buffers):
         self.me = me
-        self.parts, self.y_land, self.up_land, self.down_land = lands
+        self.parts, self.y_land, self.up_land, self.down_land, self.last_land = lands
         (self.y_send, self.y_recv, self.up_send, self.up_recv,
-         self.down_send, self.down_recv, self.local) = sems
+         self.down_send, self.down_recv, self.last_send, self.last_recv, self.local) = sems
+        (self.got, self.ring, self.up_buf, self.down_buf,
+         self.up_load, self.down_load, self.last) = buffers
         self.tiles, self.line = self.parts.shape[0], me.line
-
-    def y_copy(self, tile):
+        self.groups, self.firsts, self.items = self.counts(self.tiles)
+
+    def tile_of(self, first):
+        each = self.group - 1
+        return lax.div(first, each) * self.group + lax.rem(first, each) + 1
+
+    def begin(self, tile):
+        first = tile - lax.div(tile, self.group) - 1
+
+        @pl.when((lax.rem(tile, self.group) != 0) & (first < self.ahead))
+        def _():
+            self.y_copy(first).start()
+
+    def y_copy(self, first):
         return remote(
-            self.parts.at[tile, :, 1 - self.me.side], self.y_land.at[tile],
-            self.y_send.at[tile], self.y_recv.at[tile], self.me.to_side,
+            self.parts.at[self.tile_of(first), :, 1 - self.me.side], self.y_land.at[first],
+            self.y_send.at[first], self.y_recv.at[first], self.me.to_side,
         )
 
-    def up_copy(self, tile, count):
-        slot = lax.rem(tile, 2)
+    def last_copy(self, group):
         return remote(
-            self.up_buf.at[slot, 0:count], self.up_land.at[tile, 0:count],
-            self.up_send.at[slot], self.up_recv.at[tile], self.me.to_up,
+            self.last.at[3], self.last_land.at[group],
+            self.last_send.at[group], self.last_recv.at[group], self.me.to_side,
         )
 
-    def down_copy(self, tile, count):
-        slot = lax.rem(tile, 2)
+    def up_copy(self, item, count):
+        slot = lax.rem(item, 2)
         return remote(
-            self.down_buf.at[slot, 0:count], self.down_land.at[tile, 0:count],
-            self.down_send.at[slot], self.down_recv.at[tile], self.me.to_down,
+            self.up_buf.at[slot, 0:count], self.up_land.at[item, 0:count],
+            self.up_send.at[slot], self.up_recv.at[item], self.me.to_up,
         )
 
-    def await_up(self, tile, count):
-        land = self.up_land.at[tile, 0:count]
-        remote(land, land, self.up_send.at[0], self.up_recv.at[tile], self.me.to_up).wait_recv()
-
-    def await_down(self, tile, count):
-        land = self.down_land.at[tile, 0:count]
+    def down_copy(self, item, count):
+        slot = lax.rem(item, 2)
+        return remote(
+            self.down_buf.at[slot, 0:count], self.down_land.at[item, 0:count],
+            self.down_send.at[slot], self.down_recv.at[item], self.me.to_down,
+        )
+
+    def await_up(self, item, count):
+        land = self.up_land.at[item, 0:count]
+        remote(land, land, self.up_send.at[0], self.up_recv.at[item], self.me.to_up).wait_recv()
+
+    def await_down(self, item, count):
+        land = self.down_land.at[item, 0:count]
         remote(
-            land, land, self.down_send.at[0], self.down_recv.at[tile], self.me.to_down
+            land, land, self.down_send.at[0], self.down_recv.at[item], self.me.to_down
         ).wait_recv()
 
     @property
     def slots(self):
-        return self.tiles + self.line + 2
-
-    def use(self, buffers):
-        (self.own, self.got, self.ring, self.up_buf, self.down_buf,
-         self.up_load, self.down_load, self.last) = buffers
-
-    def step(self, s, emit):
-        me, line, tiles = self.me, self.line, self.tiles
-        depth = self.ring.shape[0]
-
-        @pl.when(s + self.ahead < tiles)
-        def _():
-            self.y_copy(s + self.ahead).start()
-
-        @pl.when(s < tiles)
-        def _():
-            self.y_copy(s).wait()
-            a = fetch(self.parts.at[s, :, me.side], self.own, self.local.at[0])
-            b = fetch(self.y_land.at[s], self.got, self.local.at[1])
-            a.wait()
-            b.wait()
-            self.ring[lax.rem(s, depth)] = self.own[...] + self.got[...]
+        return self.items + self.lag(self.line) * (self.line - 1)
+
+    def stages(self, s, first, up, down, last):
+        me, line, items = self.me, self.line, self.items
+        lag, span = self.lag(line), self.group + 1
+        pl.when(s < items)(lambda: first(lax.div(s, span), lax.rem(s, span)))
+
+        def at(item, found, body, *more):
+            pl.when(found & (item >= 0) & (item < items))(lambda: body(item, *more))
 
         for k in range(line - 1):
-            tile, count = s - 1 - k, line - 1 - k
-
-            @pl.when((me.spot == k) & (tile >= 0) & (tile < tiles))
-            def _(k=k, tile=tile, count=count):
-                slot, held = lax.rem(tile, 2), lax.rem(tile, depth)
-
-                @pl.when(tile >= 2)
+            at(s - lag * k, me.spot == k, up, k, line - 1 - k)
+        for k in range(1, line):
+            at(s - lag * (line - 1 - k), me.spot == k, down, k, k)
+        at(s - lag * (line - 1), s >= 0, last)
+
+    def fetches(self, s):
+        me, line = self.me, self.line
+        depth, span = self.ring.shape[0], self.group + 1
+
+        def first(at, kind):
+            held = self.ring.at[lax.rem(s, depth)]
+
+            @pl.when(kind < 2)
+            def _():
+                side = jnp.where(kind == 0, 1 - me.side, me.side)
+                fetch(self.parts.at[at * self.group, :, side], held, self.local.at[0])
+
+            @pl.when(kind >= 2)
+            def _():
+                number = at * (self.group - 1) + kind - 2
+
+                @pl.when(number + self.ahead < self.firsts)
                 def _():
-                    self.up_copy(tile, count).wait_send()
-
-                if k > 0:
-                    self.await_up(tile, count + 1)
-                    fetch(
-                        self.up_land.at[tile, 1 : count + 1], self.up_load.at[0:count],
-                        self.local.at[2],
-                    ).wait()
-                    self.up_buf[slot, 0:count] = (
-                        self.ring[held, k + 1 : line] + self.up_load[0:count]
-                    )
-                else:
-                    self.up_buf[slot, 0:count] = self.ring[held, k + 1 : line]
-                self.up_copy(tile, count).start()
-
-        for k in range(1, line):
-            tile, count = s - 1 - (line - 1 - k), k
-
-            @pl.when((me.spot == k) & (tile >= 0) & (tile < tiles))
-            def _(k=k, tile=tile, count=count):
-                slot, held = lax.rem(tile, 2), lax.rem(tile, depth)
-
-                @pl.when(tile >= 2)
-                def _():
-                    self.down_copy(tile, count).wait_send()
-
-                if k < line - 1:
-                    self.await_down(tile, count + 1)
-                    fetch(
-                        self.down_land.at[tile, 0:count], self.down_load.at[0:count],
-                        self.local.at[3],
-                    ).wait()
-                    self.down_buf[slot, 0:count] = (
-                        self.ring[held, 0:count] + self.down_load[0:count]
-                    )
-                else:
-                    self.down_buf[slot, 0:count] = self.ring[held, 0:count]
-                self.down_copy(tile, count).start()
-
-        tile = s - 1 - line
-
-        @pl.when((tile >= 0) & (tile < tiles))
-        def _():
-            held = lax.rem(tile, depth)
-            self.last[2] = self.ring[held, me.spot]
-
+                    self.y_copy(number + self.ahead).start()
+
+                fetch(self.parts.at[self.tile_of(number), :, me.side], held, self.local.at[0])
+                self.y_copy(number).wait()
+                fetch(self.y_land.at[number], self.got, self.local.at[1])
+
+        def up(item, k, count):
+            if k > 0:
+                self.await_up(item, count + 1)
+                fetch(
+                    self.up_land.at[item, 1 : count + 1], self.up_load.at[0:count],
+                    self.local.at[2],
+                )
+
+        def down(item, k, count):
+            if k < line - 1:
+                self.await_down(item, count + 1)
+                fetch(
+                    self.down_land.at[item, 0:count], self.down_load.at[0:count],
+                    self.local.at[3],
+                )
+
+        def last(item):
             @pl.when(me.spot == line - 1)
             def _():
-                self.await_up(tile, 1)
+                self.await_up(item, 1)
 
             @pl.when(me.spot == 0)
             def _():
-                self.await_down(tile, 1)
+                self.await_down(item, 1)
 
             @pl.when(me.spot > 0)
             def _():
-                fetch(self.up_land.at[tile, 0], self.last.at[0], self.local.at[4]).wait()
+                fetch(self.up_land.at[item, 0], self.last.at[0], self.local.at[4])
+
+            @pl.when(me.spot < line - 1)
+            def _():
+                fetch(self.down_land.at[item, me.spot], self.last.at[1], self.local.at[5])
+
+            @pl.when(lax.rem(item, span) == self.group - 2)
+            def _():
+                at = lax.div(item, span)
+                self.last_copy(at).wait()
+                fetch(self.last_land.at[at], self.last.at[5], self.local.at[6])
+
+        self.stages(s, first, up, down, last)
+
+    def loaded(self, target, at):
+        pltpu.make_async_copy(target, target, self.local.at[at]).wait()
+
+    def sums(self, s, emit):
+        me, line = self.me, self.line
+        depth, span = self.ring.shape[0], self.group + 1
+
+        def first(at, kind):
+            held = lax.rem(s, depth)
+            self.loaded(self.ring.at[held], 0)
+
+            @pl.when(kind >= 2)
+            def _():
+                self.loaded(self.got, 1)
+                self.ring[held] = self.ring[held] + self.got[...]
+
+        def up(item, k, count):
+            slot, held = lax.rem(item, 2), lax.rem(item, depth)
+
+            @pl.when(item >= 2)
+            def _():
+                self.up_copy(item, count).wait_send()
+
+            if k > 0:
+                self.loaded(self.up_load.at[0:count], 2)
+                self.up_buf[slot, 0:count] = self.ring[held, k + 1 : line] + self.up_load[0:count]
+            else:
+                self.up_buf[slot, 0:count] = self.ring[held, k + 1 : line]
+            self.up_copy(item, count).start()
+
+        def down(item, k, count):
+            slot, held = lax.rem(item, 2), lax.rem(item, depth)
+
+            @pl.when(item >= 2)
+            def _():
+                self.down_copy(item, count).wait_send()
+
+            if k < line - 1:
+                self.loaded(self.down_load.at[0:count], 3)
+                self.down_buf[slot, 0:count] = self.ring[held, 0:count] + self.down_load[0:count]
+            else:
+                self.down_buf[slot, 0:count] = self.ring[held, 0:count]
+            self.down_copy(item, count).start()
+
+        def last(item):
+            at, kind = lax.div(item, span), lax.rem(item, span)
+            self.last[2] = self.ring[lax.rem(item, depth), me.spot]
+
+            @pl.when(me.spot > 0)
+            def _():
+                self.loaded(self.last.at[0], 4)
                 self.last[2] = self.last[2] + self.last[0]
 
             @pl.when(me.spot < line - 1)
             def _():
-                fetch(self.down_land.at[tile, me.spot], self.last.at[1], self.local.at[5]).wait()
+                self.loaded(self.last.at[1], 5)
                 self.last[2] = self.last[2] + self.last[1]
 
-            emit(tile, self.last.at[2])
+            @pl.when(kind == 0)
+            def _():
+                self.last[3] = self.last[2]
+                self.last_copy(at).start()
+
+            @pl.when(kind == 1)
+            def _():
+                self.last[4] = self.last[2]
+
+            @pl.when(kind > 1)
+            def _():
+                emit(at * self.group + kind - 1, self.last.at[2], 0)
+
+            @pl.when(kind == self.group - 2)
+            def _():
+                self.loaded(self.last.at[5], 6)
+                self.last[4] = self.last[4] + self.last[5]
+                emit(at * self.group, self.last.at[4], 1)
+
+        self.stages(s, first, up, down, last)
+
+    def settle(self, s, emitted):
+        def nothing(*_):
+            pass
+
+        def last(item):
+            kind = lax.rem(item, self.group + 1)
+            pl.when(kind > 1)(lambda: emitted(0))
+            pl.when(kind == self.group - 2)(lambda: emitted(1))
+
+        self.stages(s, nothing, nothing, nothing, last)
+
+    def step(self, s, emit, emitted):
+        self.fetches(s)
+        self.sums(s, emit)
+        self.settle(s, emitted)
 
     def finish(self):
         me, line = self.me, self.line
         for k in range(line - 1):
             @pl.when(me.spot == k)
             def _(k=k):
-                for tile in range(max(0, self.tiles - 2), self.tiles):
-                    self.up_copy(tile, line - 1 - k).wait_send()
+                for item in range(self.items - 2, self.items):
+                    self.up_copy(item, line - 1 - k).wait_send()
 
         for k in range(1, line):
             @pl.when(me.spot == k)
             def _(k=k):
-                for tile in range(max(0, self.tiles - 2), self.tiles):
-                    self.down_copy(tile, k).wait_send()
+                for item in range(self.items - 2, self.items):
+                    self.down_copy(item, k).wait_send()
 
 
 class NarrowSum:
-    @staticmethod
-    def lands(chunks, quarter, width):
-        return [
-            jax.ShapeDtypeStruct((chunks, 2, quarter, width), f32),
-            jax.ShapeDtypeStruct((chunks, quarter, width), f32),
-            jax.ShapeDtypeStruct((chunks, quarter, width), f32),
-            jax.ShapeDtypeStruct((chunks, 2, quarter, width), f32),
-        ]
-
     @staticmethod
     def sems(chunks):
         dma = pltpu.SemaphoreType.DMA
-        return [dma((chunks,)) for _ in range(8)] + [dma((5,))]
+        return [dma((chunks,)) for _ in range(8)]
 
     @staticmethod
     def buffers(quarter, width):
         return [
             pltpu.VMEM((2, 2, 2, quarter, width), f32),
-            pltpu.VMEM((2, quarter, width), f32),
             pltpu.VMEM((2, 2, quarter, width), f32),
-            pltpu.VMEM((quarter, width), f32),
-            pltpu.VMEM((2, quarter, width), f32),
             pltpu.VMEM((2, 2, quarter, width), f32),
             pltpu.VMEM((2, quarter, width), f32),
+            pltpu.VMEM((3, 2, quarter, width), f32),
+            pltpu.VMEM((2, 2, quarter, width), f32),
             pltpu.VMEM((2, 2, quarter, width), bf16),
         ]
 
-    def __init__(self, me, lands, sems):
+    def __init__(self, me, sems, buffers):
         self.me = me
-        self.core_land, self.chip_land, self.back_land, self.last_land = lands
-        (self.s0, self.r0, self.s1, self.r1, self.s2, self.r2, self.s3, self.r3, self.local) = sems
-        self.chunks = self.chip_land.shape[0]
-
-    def use(self, buffers):
-        (self.part, self.core_load, self.half, self.chip_load,
-         self.done, self.pair, self.last_load, self.low) = buffers
+        (self.s0, self.r0, self.s1, self.r1, self.s2, self.r2, self.s3, self.r3) = sems
+        (self.part, self.core_land, self.half, self.chip_land, self.pair, self.last_land,
+         self.low) = buffers
+        self.chunks = self.s0.shape[0]
 
     def copies(self, stage, c):
-        me, slot = self.me, lax.rem(c, 2)
+        me, slot, third = self.me, lax.rem(c, 2), lax.rem(c, 3)
         if stage == 0:
-            return remote(self.part.at[slot, 1 - me.core], self.core_land.at[c],
+            return remote(self.part.at[slot, 1 - me.core], self.core_land.at[slot],
                           self.s0.at[c], self.r0.at[c], me.to_core)
         if stage == 1:
-            return remote(self.half.at[slot, 1 - me.chip], self.chip_land.at[c],
+            return remote(self.half.at[slot, 1 - me.chip], self.chip_land.at[slot],
                           self.s1.at[c], self.r1.at[c], me.to_chip)
         if stage == 2:
-            return remote(self.done.at[slot], self.back_land.at[c],
+            return remote(self.pair.at[third, me.chip], self.pair.at[third, me.chip],
                           self.s2.at[c], self.r2.at[c], me.to_chip)
-        return remote(self.pair.at[slot], self.last_land.at[c],
+        return remote(self.pair.at[third], self.last_land.at[slot],
                       self.s3.at[c], self.r3.at[c], me.to_core)
 
     @property
     def slots(self):
         return self.chunks + 4
 
+    def at_stage(self, s, number, body):
+        c = s - number
+        pl.when((c >= 0) & (c < self.chunks))(lambda: body(c))
+
     def step(self, s, produce, work, lower, emit):
         me = self.me
 
         def stage(number, body):
-            c = s - number
-
-            @pl.when((c >= 0) & (c < self.chunks))
-            def _():
+            def run(c):
                 if number > 0:
                     self.copies(number - 1, c).wait()
-                body(c, lax.rem(c, 2))
+                body(c, lax.rem(c, 2), lax.rem(c, 3))
                 if number < 4:
                     self.copies(number, c).start()
 
-        def four(c, slot):
-            fetch(self.last_land.at[c], self.last_load, self.local.at[3]).wait()
-            self.low[me.core] = lower(self.pair[slot])
-            self.low[1 - me.core] = lower(self.last_load[...])
+            self.at_stage(s, number, run)
+
+        def four(c, slot, third):
+            self.low[me.core] = lower(self.pair[third])
+            self.low[1 - me.core] = lower(self.last_land[slot])
             emit(c, self.low)
 
-        def three(c, slot):
-            fetch(self.back_land.at[c], self.pair.at[slot, 1 - me.chip], self.local.at[2]).wait()
-            self.pair[slot, me.chip] = self.done[slot]
-
-        def two(c, slot):
-            fetch(self.chip_land.at[c], self.chip_load, self.local.at[1]).wait()
-            self.done[slot] = work(c, self.half[slot, me.chip] + self.chip_load[...])
-
-        def one(c, slot):
-            fetch(self.core_land.at[c], self.core_load, self.local.at[0]).wait()
-            self.half[slot] = self.part[slot, me.core] + self.core_load[...]
-
-        def zero(c, slot):
-            produce(c, self.part.at[slot])
+        def three(c, slot, third):
+            pass
+
+        def two(c, slot, third):
+            self.pair[third, me.chip] = work(c, self.half[slot, me.chip] + self.chip_land[slot])
+
+        def one(c, slot, third):
+            self.half[slot] = self.part[slot, me.core] + self.core_land[slot]
+
+        def zero(c, slot, third):
+            pl.when(slot == 0)(lambda: produce(c, self.part))
 
         stage(4, four)
         stage(3, three)
@@ -389,8 +488,7 @@
 
 
 def store_part(part, value, columns):
-    half, quarter = 2, value.shape[0] // 4
-    part[:, :, :, columns] = value.reshape(half, 2, quarter, value.shape[1])
+    part[:, :, :, :, columns] = value.reshape(2, 2, 2, value.shape[0] // 8, value.shape[1])
 
 
 def norm_back(pulled, unit, scale, gain):
@@ -414,15 +512,13 @@
      cosine, sine, starts), refs = take(refs, 13)
     (mlp_in, mlp_in_t, cot_t, normed_t, hidden_out, q_out, k_out, v_out, q_raw_out, k_raw_out,
      context_out, lse_out), refs = take(refs, 12)
-    lands, refs = take(refs, 4)
-    sems, refs = take(refs, 9)
-    buffers, refs = take(refs, 8)
+    sems, refs = take(refs, 8)
+    buffers, refs = take(refs, 7)
     (hidden_buf, q_low, k_low, v_low, v_t, q_raw, k_raw, context, lse, normed, normed_turn,
      cot_load, cot_turn, low_turn, sem, out_sem) = refs
     me = Spot(wide)
     me.greet(False)
-    summing = NarrowSum(me, lands, sems)
-    summing.use(buffers)
+    summing = NarrowSum(me, sems, buffers)
     token_count, width = tokens.shape
     rows = token_count // chunks
     quarter = rows // 4
@@ -476,7 +572,7 @@
     def produce(c, part):
         for i in range(token_count // block):
             pl.when(c == i * per_block)(functools.partial(attend, i))
-        left = context[pl.ds(pl.multiple_of(c * rows, rows), rows), :]
+        left = context[pl.ds(pl.multiple_of(c * rows, 2 * rows), 2 * rows), :]
         for at in range(0, width, step):
             store_part(part, forward_dot(left, w_output[:, at : at + step]), slice(at, at + step))
 
@@ -484,18 +580,29 @@
         at = pl.multiple_of(c * rows + me.core * 2 * quarter + me.chip * quarter, quarter)
         hidden = tokens[pl.ds(at, quarter), :].astype(f32) + total
         hidden_buf[...] = hidden
-        fetch(hidden_buf, hidden_out.at[c], sem.at[1]).wait()
+        fetch(hidden_buf, hidden_out.at[c], sem.at[2])
         return hidden * inverse_rms(hidden)
 
     def lower(value):
         return (value * mlp_gain[...]).astype(bf16)
 
     def emit(c, low):
-        a = fetch(low, mlp_in.at[c], sem.at[0])
+        fetch(low, mlp_in.at[c], sem.at[3])
         low_turn[...] = low[...].reshape(rows, width).T
         at = pl.ds(pl.multiple_of(c * rows, rows), rows)
-        fetch(low_turn, mlp_in_t.at[:, at], sem.at[1]).wait()
-        a.wait()
+        fetch(low_turn, mlp_in_t.at[:, at], sem.at[4])
+
+    def settle(s):
+        def two(c):
+            pltpu.make_async_copy(hidden_buf, hidden_out.at[c], sem.at[2]).wait()
+
+        def four(c):
+            pltpu.make_async_copy(summing.low, mlp_in.at[c], sem.at[3]).wait()
+            at = pl.ds(pl.multiple_of(c * rows, rows), rows)
+            pltpu.make_async_copy(low_turn, mlp_in_t.at[:, at], sem.at[4]).wait()
+
+        summing.at_stage(s, 2, two)
+        summing.at_stage(s, 4, four)
 
     def turn_rows(s):
         at = pl.ds(pl.multiple_of(s * rows, rows), rows)
@@ -520,6 +627,7 @@
             for at, (a, b) in enumerate(kept):
                 fetch(a, b, out_sem.at[at])
 
+        settle(s)
         return carry
 
     lax.fori_loop(0, summing.slots, body, 0)
@@ -572,11 +680,13 @@
      starts, attn_gain, mlp_gain, query_gain, key_gain), refs = take(refs, 28)
     (output, grad_tokens, grad_query, grad_key, grad_value, grad_output, grad_gate, grad_up,
      grad_down, gains_out, grad_hidden), refs = take(refs, 11)
-    wide_lands, refs = take(refs, 4)
-    lands, refs = take(refs, 4)
-    wide_sems, refs = take(refs, 7)
-    sems, refs = take(refs, 9)
-    acts, gains, gain_lands, gain_send, gain_recv, sem, w_sem, store_sem = refs
+    wide_lands, refs = take(refs, 5)
+    wide_sems, refs = take(refs, 9)
+    sems, refs = take(refs, 8)
+    wide_buffers, refs = take(refs, 7)
+    buffers, refs = take(refs, 7)
+    (acts, gains, gain_lands, turned, gain_send, gain_recv, sem, w_sem, store_sem, emit_sem,
+     att_sem) = refs
     me = Spot(wide)
     me.greet(True)
     token_count, width = mlp_in.shape
@@ -591,10 +701,44 @@
     group = q_heads // (kv_width // head)
     scale = head ** (-0.5)
     out_tiles = query_width // cols
-    total = WideSum(me, wide_lands, wide_sems)
+    total = WideSum(me, wide_lands, wide_sems, wide_buffers)
     half = token_count // 2
     rows = token_count // chunks
     quarter = rows // 4
+
+    early = (0, 1, 4)
+
+    def emit_tile(tile, value, number):
+        def part(first, count, target, turn, every=1, offset=0):
+            inside = (tile >= first) & (tile < first + count)
+            at = tile - first
+            if every > 1:
+                inside = inside & (lax.rem(at, every) == offset)
+                at = lax.div(at, every)
+
+            @pl.when(inside)
+            def _():
+                cut = pl.ds(pl.multiple_of(at * cols, cols), cols)
+                if turn:
+                    turned[number] = value[...].T
+                    fetch(turned.at[number], target.at[cut, :], emit_sem.at[number])
+                else:
+                    fetch(value, target.at[:, cut], emit_sem.at[number])
+
+        part(0, mlp_tiles, grad_down, True, 3, 0)
+        part(0, mlp_tiles, grad_gate, False, 3, 1)
+        part(0, mlp_tiles, grad_up, False, 3, 2)
+        at = mlp_tiles
+        part(at, out_tiles, grad_output, True)
+        at += out_tiles
+        part(at, query_width // cols, grad_query, False)
+        at += query_width // cols
+        part(at, kv_width // cols, grad_key, False)
+        at += kv_width // cols
+        part(at, kv_width // cols, grad_value, False)
+
+    def emitted(number):
+        pltpu.make_async_copy(turned.at[number], turned.at[number], emit_sem.at[number]).wait()
 
     def compute(xs, xt, cs, ct, gate_w, up_w, down_w, staged):
         pairs = ((mlp_in, xs), (cot, cs), (cot_t, ct), (mlp_in_t, xt))
@@ -645,22 +789,20 @@
             lax.fori_loop(0, 2, some, 0)
             for j in range(3):
                 tile = 3 * b + j
-
-                @pl.when(tile >= 2)
-                def _(tile=tile):
-                    store(tile - 2).wait()
-
-                    @pl.when(tile - 2 < total.ahead)
-                    def _():
-                        total.y_copy(tile - 2).start()
-
                 outer_tile(ct if j == 0 else xt, acts[j, :, at], staged.at[lax.rem(tile, 2)])
                 store(tile).start()
+
+                @pl.when(tile > 0)
+                def _(tile=tile):
+                    store(tile - 1).wait()
+                    total.begin(tile - 1)
+
+            for number, after in enumerate(early):
+                pl.when(b == after)(lambda: total.step(number, emit_tile, emitted))
             return carry
 
         lax.fori_loop(0, blocks, block, 0)
-        for tile in range(mlp_tiles - 2, mlp_tiles):
-            store(tile).wait()
+        store(mlp_tiles - 1).wait()
 
     pl.run_scoped(
         compute,
@@ -675,14 +817,10 @@
     )
 
     def pass_on(*held):
-        wide_buffers, held = take(held, 8)
-        buffers, held = take(held, 8)
         (gate_w, up_w, down_w, hidden_load, token_load, out_buf, out_w, left_t, staged, q_low,
          k_low, v_low, k_t, d_context, right, lse, cos, sin, raw, d_query, d_key, d_value,
-         heads, turned) = held
-        total.use(wide_buffers)
-        summing = NarrowSum(me, lands, sems)
-        summing.use(buffers)
+         heads) = held
+        summing = NarrowSum(me, sems, buffers)
         small = SmallSum(me, gains, gain_lands, gain_send, gain_recv)
         gains[...] = jnp.zeros_like(gains)
         gain_at = (
@@ -695,7 +833,8 @@
             fetch(a, b, sem.at[0]).wait()
         k_t[...] = k_low[...].T
         step = gate_w.shape[1]
-        first_attend = chunks + 4
+        narrow_from = len(early)
+        first_attend = narrow_from + chunks + 4
         first_heads = first_attend + q_heads
 
         def stream(copies, use):
@@ -712,7 +851,7 @@
 
         def produce(c, part):
             chunk = lax.rem(c, chunks)
-            own = pl.ds(pl.multiple_of(chunk * rows, rows), rows)
+            own = pl.ds(pl.multiple_of(chunk * rows, 2 * rows), 2 * rows)
             kind = lax.div(c, chunks)
 
             @pl.when(kind == 0)
@@ -759,35 +898,46 @@
 
                 stream(copies, use)
 
+        def preload(c):
+            chunk, kind = lax.rem(c, chunks), lax.div(c, chunks)
+
+            @pl.when(kind < 2)
+            def _():
+                fetch(hidden.at[chunk], hidden_load, sem.at[0])
+
+            @pl.when(kind == 0)
+            def _():
+                fetch(cot.at[own_rows(chunk), :], token_load, sem.at[1])
+
+            @pl.when(kind == 2)
+            def _():
+                fetch(grad_hidden.at[chunk], hidden_load, sem.at[0])
+                fetch(tokens.at[own_rows(chunk), :], token_load, sem.at[1])
+
         def work(c, pulled):
-            chunk = lax.rem(c, chunks)
             kind = lax.div(c, chunks)
+            pltpu.make_async_copy(hidden_load, hidden_load, sem.at[0]).wait()
+
+            @pl.when(kind != 1)
+            def _():
+                pltpu.make_async_copy(token_load, token_load, sem.at[1]).wait()
 
             @pl.when(kind == 0)
             def _():
-                a = fetch(hidden.at[chunk], hidden_load, sem.at[0])
-                b = fetch(cot.at[own_rows(chunk), :], token_load, sem.at[1])
-                a.wait()
-                b.wait()
                 mid = hidden_load[...]
                 inverse = inverse_rms(mid)
                 unit = mid * inverse
                 gains[:, gain_at[1]] += jnp.sum(pulled * unit, axis=0, keepdims=True)
                 back = norm_back(pulled, unit, inverse, mlp_gain[...])
                 out_buf[...] = token_load[...].astype(f32) + back
-                fetch(out_buf, grad_hidden.at[chunk], sem.at[0]).wait()
+                fetch(out_buf, grad_hidden.at[lax.rem(c, chunks)], sem.at[2])
 
             @pl.when(kind == 1)
             def _():
-                fetch(hidden.at[chunk], hidden_load, sem.at[0]).wait()
                 out_buf[...] = hidden_load[...] + pulled
 
             @pl.when(kind == 2)
             def _():
-                a = fetch(grad_hidden.at[chunk], hidden_load, sem.at[0])
-                b = fetch(tokens.at[own_rows(chunk), :], token_load, sem.at[1])
-                a.wait()
-                b.wait()
                 mid = token_load[...].astype(f32)
                 inverse = inverse_rms(mid)
                 unit = mid * inverse
@@ -796,6 +946,20 @@
 
             return out_buf[...]
 
+        def settle(s):
+            def two(c):
+                @pl.when(lax.div(c, chunks) == 0)
+                def _():
+                    pltpu.make_async_copy(out_buf, out_buf, sem.at[2]).wait()
+
+            def four(c):
+                @pl.when(lax.div(c, chunks) > 0)
+                def _():
+                    pltpu.make_async_copy(summing.low, summing.low, sem.at[3]).wait()
+
+            summing.at_stage(s, 2, two)
+            summing.at_stage(s, 4, four)
+
         def own_rows(chunk):
             at = chunk * rows + me.core * 2 * quarter + me.chip * quarter
             return pl.ds(pl.multiple_of(at, quarter), quarter)
@@ -816,11 +980,11 @@
 
             @pl.when(kind == 1)
             def _():
-                fetch(low, output.at[chunk], sem.at[0]).wait()
+                fetch(low, output.at[chunk], sem.at[3])
 
             @pl.when(kind == 2)
             def _():
-                fetch(low, grad_tokens.at[chunk], sem.at[0]).wait()
+                fetch(low, grad_tokens.at[chunk], sem.at[3])
 
         def put(tile, right_value):
             outer_tile(left_t, right_value, staged)
@@ -843,7 +1007,7 @@
                 d_key[...] = jnp.zeros_like(d_key)
                 d_value[...] = jnp.zeros_like(d_value)
 
-            load = fetch(q_raw.at[:, cut], raw, sem.at[0])
+            load = fetch(q_raw.at[:, cut], raw, att_sem.at[0])
             size = min(256, token_count)
             for i in range(token_count // size):
                 own, keys = slice(i * size, (i + 1) * size), (i + 1) * size
@@ -864,7 +1028,7 @@
 
             @pl.when(lax.rem(h, group) == group - 1)
             def _():
-                fetch(k_raw.at[:, kv_cut], raw, sem.at[0]).wait()
+                fetch(k_raw.at[:, kv_cut], raw, att_sem.at[0]).wait()
                 there = pl.ds(pl.multiple_of(query_width + kv * head, head), head)
                 heads[:, there] = rope_norm_back(
                     d_key[...] * scale, raw[...], key_gain, gain_at[3]
@@ -872,43 +1036,14 @@
                 there = pl.ds(pl.multiple_of(query_width + kv_width + kv * head, head), head)
                 heads[:, there] = d_value[...].astype(bf16)
 
-        def emit_tile(tile, value):
-            def part(first, count, target, turn, every=1, offset=0):
-                inside = (tile >= first) & (tile < first + count)
-                at = tile - first
-                if every > 1:
-                    inside = inside & (lax.rem(at, every) == offset)
-                    at = lax.div(at, every)
-
-                @pl.when(inside)
-                def _():
-                    cut = pl.ds(pl.multiple_of(at * cols, cols), cols)
-                    if turn:
-                        turned[...] = value[...].T
-                        fetch(turned, target.at[cut, :], sem.at[0]).wait()
-                    else:
-                        fetch(value, target.at[:, cut], sem.at[0]).wait()
-
-            part(0, mlp_tiles, grad_down, True, 3, 0)
-            part(0, mlp_tiles, grad_gate, False, 3, 1)
-            part(0, mlp_tiles, grad_up, False, 3, 2)
-            at = mlp_tiles
-            part(at, out_tiles, grad_output, True)
-            at += out_tiles
-            part(at, query_width // cols, grad_query, False)
-            at += query_width // cols
-            part(at, kv_width // cols, grad_key, False)
-            at += kv_width // cols
-            part(at, kv_width // cols, grad_value, False)
-
-        small_at = summing.slots - 1
+        small_at = narrow_from + summing.slots - 1
 
         def body(s, carry):
             @pl.when(s == first_attend)
             def _():
                 for t in range(out_tiles):
                     cut = slice(t * cols, (t + 1) * cols)
-                    fetch(context.at[:, cut], right, sem.at[0]).wait()
+                    fetch(context.at[:, cut], right, att_sem.at[0]).wait()
                     put(mlp_tiles + t, right[...])
 
             @pl.when((s >= first_attend) & (s < first_heads))
@@ -917,7 +1052,7 @@
 
             @pl.when(s == first_heads)
             def _():
-                fetch(normed_t, left_t, sem.at[0]).wait()
+                fetch(normed_t, left_t, att_sem.at[0]).wait()
 
                 def one(t, carry):
                     put(mlp_tiles + out_tiles + t, heads[:, pl.ds(pl.multiple_of(t * cols, cols), cols)])
@@ -925,21 +1060,21 @@
 
                 lax.fori_loop(0, all_heads // cols, one, 0)
 
-            pl.when(s < total.slots)(lambda: total.step(s, emit_tile))
-            pl.when(s < summing.slots)(
-                lambda: summing.step(s, produce, work, lower, emit_rows)
-            )
+            summing.at_stage(s - narrow_from, 2, preload)
+            total.fetches(s)
+            summing.step(s - narrow_from, produce, work, lower, emit_rows)
+            total.sums(s, emit_tile)
+            total.settle(s, emitted)
+            settle(s - narrow_from)
             pl.when(s >= small_at)(lambda: small.step(s - small_at))
             return carry
 
-        lax.fori_loop(0, max(total.slots, small_at + 5), body, 0)
+        lax.fori_loop(narrow_from, max(total.slots, small_at + 5), body, 0)
         total.finish()
 
     step = min(256, width)
     pl.run_scoped(
         pass_on,
-        *WideSum.buffers(line, side_rows, cols),
-        *NarrowSum.buffers(quarter, width),
         pltpu.VMEM((2, step, max(hidden_units, all_heads)), bf16),
         pltpu.VMEM((2, step, hidden_units), bf16),
         pltpu.VMEM((2, hidden_units, step), bf16),
@@ -963,7 +1098,6 @@
         pltpu.VMEM((token_count, head), f32),
         pltpu.VMEM((token_count, head), f32),
         pltpu.VMEM((token_count, all_heads), bf16),
-        pltpu.VMEM((cols, side_rows), f32),
     )
     fetch(gains, gains_out, sem.at[0]).wait()
 
@@ -1043,10 +1177,9 @@
             shape((width, token_count), bf16),
             shape((chunks, quarter, width), f32),
             *kept,
-            *NarrowSum.lands(chunks, quarter, width),
         ],
         [in_vmem, any_space] + [in_vmem] * 11,
-        [any_space] * 16,
+        [any_space] * 12,
         [
             *NarrowSum.sems(chunks),
             *NarrowSum.buffers(quarter, width),
@@ -1059,7 +1192,7 @@
             pltpu.VMEM((rows, width), bf16),
             pltpu.VMEM((width, rows), bf16),
             pltpu.VMEM((width, rows), bf16),
-            dma((2,)),
+            dma((5,)),
             dma((7,)),
         ],
         (
@@ -1089,21 +1222,25 @@
             shape((1, gain_width), f32),
             shape((chunks, quarter, width), f32),
             *WideSum.lands(tiles, line, side_rows, cols),
-            *NarrowSum.lands(3 * chunks, quarter, width),
         ],
         [any_space] * 23 + [in_vmem] * 5,
-        [any_space] * 19,
+        [any_space] * 16,
         [
             *WideSum.sems(tiles),
             *NarrowSum.sems(3 * chunks),
+            *WideSum.buffers(line, side_rows, cols),
+            *NarrowSum.buffers(quarter, width),
             pltpu.VMEM((3, token_count, hidden_units), bf16),
             pltpu.VMEM((1, gain_width), f32),
             pltpu.VMEM((2 + line, 1, gain_width), f32),
+            pltpu.VMEM((2, cols, side_rows), f32),
             dma((2 + line,)),
             dma((2 + line,)),
             dma((4,)),
             dma((2, 3)),
             dma((2,)),
+            dma((2,)),
+            dma((1,)),
         ],
         (
             mlp_in.reshape(token_count, width), mlp_in_t, cotangent, cot_t, normed_t, hidden,

time: 804 us -> 689 us (0.86); the launches traced: 790 us -> 686 us
  Pallas kernels: 768 us -> 664 us
    pallas_call x2, Pallas kernels: 768 us -> 664 us  [call(): pl.pallas_call(kernel, out_shape=out_shape, in_specs=in_specs, out_specs=...]
where the time goes in v3:
time: 689 us; the launch traced here: 686 us
  Pallas kernels  664 us (96%)
  local copies, waits for them, and re-layouts  16 us (2%)
    pallas_call x2, Pallas kernels, call(): pl.pallas_call(kernel, out_shape=out_shape, in_specs=in_specs, out_specs=...  664 us

profile of v3, /device:TPU:0, one launch (start us, length us, event | category | flops | bytes accessed | tf_op | source)
XLA Modules:
  0.0 685.7 jit_solution(14238798175850133142)
XLA Ops:
  0.6 0.8 reduce_window_sum.11
  1.5 0.1 convert_reduce_fusion
  1.6 0.7 subtract_bitcast_fusion
  2.2 0.1 select_reduce_fusion
  2.3 0.2 broadcast_multiply_fusion
  2.6 2.9 sine_multiply_fusion
  5.4 0.6 subtract_subtract_fusion.refs_12_.refs_23_
  6.0 114.7 %shard_map.237 = (bf16[8,2,2,32,2048]{4,3,2,1,0:T(8,128)(2,1)}, bf16[2048,1024]{1,0:T(8,128)(2,1)}, bf16[2048,1024]{1,0:T(8,128)(2,1)}, bf16[2048,1024]{1,0:T(8,...) custom-call(bf16[1024,2048]{1,0:T(8,128)(2,1)} %refs_13_.1, ...), custom_call_target="tpu_custom_call" | custom-call | tf_op jit(solution)/shard_map/pallas_call | solution.py:1106
  120.7 548.8 %shard_map.238 = (bf16[8,2,2,32,2048]{4,3,2,1,0:T(8,128)(2,1)}, bf16[8,2,2,32,2048]{4,3,2,1,0:T(8,128)(2,1)}, f32[256,512]{1,0:T(8,128)}, f32[256,256]{1,0:T(8,1...) custom-call(bf16[1024,2048]{1,0:T(8,128)(2,1)} %bitcast.17, ...), custom_call_target="tpu_custom_call" | custom-call | tf_op jit(solution)/shard_map/pallas_call | solution.py:1106
  669.6 1.2 constant_dynamic-slice_fusion.3
  670.8 1.3 fusion.2
  672.1 0.0 copy-start
  672.1 4.9 copy.36
  677.0 0.0 copy-done
  677.0 0.0 copy-start.5
  677.1 0.0 copy-start.4
  677.1 0.0 copy-start.3
  677.1 2.1 copy.37
  679.2 0.0 copy-done.5
  679.2 0.8 copy.38
  680.0 0.0 copy-done.7
  680.0 0.7 copy.39
  680.7 0.0 copy-done.6
  680.7 0.7 copy.40
  681.4 0.0 copy-done.4
  681.4 0.8 copy.41
  682.2 0.0 copy-done.3
  682.2 1.1 copy.42
  683.4 0.0 copy-done.2
  683.4 1.1 copy.43
  684.5 0.0 copy-done.1
  684.5 1.1 copy.44
  (7 shorter events, 0.0 us)
Async XLA Ops:
  672.1 4.9 copy-start
  677.0 2.2 copy-start.5
  677.0 3.0 copy-start.7
  677.0 3.7 copy-start.6
  677.1 4.4 copy-start.4
  677.1 5.2 copy-start.3
  679.2 4.2 copy-start.2
  680.0 4.5 copy-start.1

commit v4 on v3

--- a/solution.py
+++ b/solution.py
@@ -81,7 +81,7 @@
         there = lax.rem(self.spot + distance, self.line)
         return {"wide": there * 2 + self.side}
 
-    def greet(self, wide_too):
+    def greet(self, line_too):
         barrier = pltpu.get_barrier_semaphore()
 
         def tell(who):
@@ -89,11 +89,11 @@
 
         tell(self.to_core)
         tell(self.to_chip)
-        if wide_too:
-            tell(self.to_side)
+        tell(self.to_side)
+        if line_too:
             for distance in range(1, self.line):
                 tell(self.along(distance))
-        pl.semaphore_wait(barrier, 2 + self.line if wide_too else 2)
+        pl.semaphore_wait(barrier, 2 + self.line if line_too else 3)
 
 
 def remote(source, target, send, recv, who):
@@ -104,82 +104,122 @@
 
 
 class WideSum:
-    group = 6
     ahead = 3
+    join_after = 5
+    held_back = 0
 
     @staticmethod
     def lag(line):
         return 2 if line <= 4 else 1
 
+    @staticmethod
+    def numbers(counts):
+        early, shared, late = counts
+        firsts, pairs = early - 1 + late, 1 + shared
+        return early + shared + late, firsts, pairs, firsts + 2 * pairs
+
     @classmethod
-    def counts(cls, tiles):
-        groups = tiles // cls.group
-        return groups, tiles - groups, tiles + groups
-
-    @classmethod
-    def lands(cls, tiles, line, rows, cols):
-        groups, firsts, items = cls.counts(tiles)
+    def lands(cls, counts, line, rows, cols):
+        tiles, firsts, pairs, items = cls.numbers(counts)
         return [
             jax.ShapeDtypeStruct((tiles, line, 2, rows, cols), f32),
             jax.ShapeDtypeStruct((firsts, line, rows, cols), f32),
             jax.ShapeDtypeStruct((items, line - 1, rows, cols), f32),
             jax.ShapeDtypeStruct((items, line - 1, rows, cols), f32),
-            jax.ShapeDtypeStruct((groups, rows, cols), f32),
+            jax.ShapeDtypeStruct((pairs, rows, cols), f32),
+            jax.ShapeDtypeStruct((counts[1], line, rows, cols), f32),
+            jax.ShapeDtypeStruct((counts[1], line, rows, cols), f32),
         ]
 
     @classmethod
-    def sems(cls, tiles):
+    def sems(cls, counts):
         dma = pltpu.SemaphoreType.DMA
-        groups, firsts, items = cls.counts(tiles)
+        tiles, firsts, pairs, items = cls.numbers(counts)
         return [
             dma((firsts,)), dma((firsts,)), dma((2,)), dma((items,)), dma((2,)), dma((items,)),
-            dma((groups,)), dma((groups,)), dma((7,)),
+            dma((pairs,)), dma((pairs,)), dma((counts[1],)), dma((counts[1],)), dma((7,)),
         ]
 
-    @staticmethod
-    def buffers(line, rows, cols):
+    @classmethod
+    def buffers(cls, line, rows, cols):
         tile = (line, rows, cols)
         return [
             pltpu.VMEM(tile, f32),
-            pltpu.VMEM((WideSum.lag(line) * (line - 1) + 1,) + tile, f32),
+            pltpu.VMEM((cls.lag(line) * (line - 1) + 1,) + tile, f32),
             pltpu.VMEM((2, line - 1, rows, cols), f32),
             pltpu.VMEM((2, line - 1, rows, cols), f32),
             pltpu.VMEM((line - 1, rows, cols), f32),
             pltpu.VMEM((line - 1, rows, cols), f32),
-            pltpu.VMEM((6, rows, cols), f32),
+            pltpu.VMEM((4, rows, cols), f32),
+            pltpu.VMEM((3, rows, cols), f32),
+            pltpu.VMEM((3, rows, cols), f32),
         ]
 
-    def __init__(self, me, lands, sems, buffers):
-        self.me = me
-        self.parts, self.y_land, self.up_land, self.down_land, self.last_land = lands
-        (self.y_send, self.y_recv, self.up_send, self.up_recv,
-         self.down_send, self.down_recv, self.last_send, self.last_recv, self.local) = sems
-        (self.got, self.ring, self.up_buf, self.down_buf,
-         self.up_load, self.down_load, self.last) = buffers
-        self.tiles, self.line = self.parts.shape[0], me.line
-        self.groups, self.firsts, self.items = self.counts(self.tiles)
-
-    def tile_of(self, first):
-        each = self.group - 1
-        return lax.div(first, each) * self.group + lax.rem(first, each) + 1
+    def __init__(self, me, counts, ready, lands, sems, buffers):
+        self.me, self.line = me, me.line
+        self.early, self.shared, self.late = counts
+        (self.parts, self.y_land, self.up_land, self.down_land, self.last_land, self.give,
+         self.give_land) = lands
+        (self.y_send, self.y_recv, self.up_send, self.up_recv, self.down_send, self.down_recv,
+         self.last_send, self.last_recv, self.give_send, self.give_recv, self.local) = sems
+        (self.got, self.ring, self.up_buf, self.down_buf, self.up_load, self.down_load, self.last,
+         self.leave, self.hold) = buffers
+        self.tiles, self.firsts, self.pairs, self.items = self.numbers(counts)
+        self.shared_from = self.early + 1
+        before = self.shared - self.held_back
+        self.late_from = self.shared_from + 2 * before
+        self.rest_from = self.late_from + self.late
+        used = [(2 + u, False, u) for u in range(self.early - 1)]
+        used += [(self.shared_from + 2 * t, True, t) for t in range(before)]
+        used += [(self.late_from + k, False, self.early - 1 + k) for k in range(self.late)]
+        used += [(self.rest_from + 2 * k, True, before + k) for k in range(self.held_back)]
+        self.sending = []
+        for m in range(self.ahead, len(used)):
+            slot, shared, number = used[m]
+            late = number - (self.early - 1)
+            made = 0 if shared or late < 0 else ready(late)
+            at = max(used[m - self.ahead][0], made)
+            assert at < slot
+            self.sending.append((at, shared, number))
+
+    def item(self, s):
+        rest = s >= self.rest_from
+        among = s - self.shared_from - jnp.where(rest, self.late, 0)
+        start = s < 2
+        paired = start | rest | ((among >= 0) & (s < self.late_from))
+        pair = jnp.where(start, 0, 1 + lax.div(among, 2))
+        half = jnp.where(start, s, lax.rem(among, 2))
+        first = jnp.where(among < 0, s - 2, s - self.late_from + self.early - 1)
+        return paired, pair, half, first
+
+    def pair_tile(self, pair):
+        return jnp.where(pair == 0, 0, self.early - 1 + pair)
+
+    def first_tile(self, first):
+        made = self.early - 1
+        return jnp.where(first < made, first + 1, first + 1 + self.shared)
 
     def begin(self, tile):
-        first = tile - lax.div(tile, self.group) - 1
-
-        @pl.when((lax.rem(tile, self.group) != 0) & (first < self.ahead))
+        @pl.when((tile > 0) & (tile <= self.ahead))
         def _():
-            self.y_copy(first).start()
+            self.y_copy(tile - 1).start()
 
     def y_copy(self, first):
         return remote(
-            self.parts.at[self.tile_of(first), :, 1 - self.me.side], self.y_land.at[first],
+            self.parts.at[self.first_tile(first), :, 1 - self.me.side], self.y_land.at[first],
             self.y_send.at[first], self.y_recv.at[first], self.me.to_side,
         )
 
-    def last_copy(self, group):
+    def give_copy(self, shared):
         return remote(
-            self.last.at[3], self.last_land.at[group],
-            self.last_send.at[group], self.last_recv.at[group], self.me.to_side,
+            self.give.at[shared], self.give_land.at[shared],
+            self.give_send.at[shared], self.give_recv.at[shared], self.me.to_side,
+        )
+
+    def last_copy(self, pair):
+        return remote(
+            self.leave.at[lax.rem(pair, 3)], self.last_land.at[pair],
+            self.last_send.at[pair], self.last_recv.at[pair], self.me.to_side,
         )
 
     def up_copy(self, item, count):
@@ -212,8 +252,8 @@
 
     def stages(self, s, first, up, down, last):
         me, line, items = self.me, self.line, self.items
-        lag, span = self.lag(line), self.group + 1
-        pl.when(s < items)(lambda: first(lax.div(s, span), lax.rem(s, span)))
+        lag = self.lag(line)
+        pl.when(s < items)(lambda: first(*self.item(s)))
 
         def at(item, found, body, *more):
             pl.when(found & (item >= 0) & (item < items))(lambda: body(item, *more))
@@ -224,27 +264,38 @@
             at(s - lag * (line - 1 - k), me.spot == k, down, k, k)
         at(s - lag * (line - 1), s >= 0, last)
 
+    @staticmethod
+    def here(pair, half):
+        return (pair > 0) & (half == 0)
+
+    def joined(self, item):
+        before = item - self.join_after
+        paired, pair, half, _ = self.item(before)
+        now_paired, now_pair, now_half, _ = self.item(item)
+        soon = self.pairs - self.held_back
+        late = now_paired & (now_half == 1) & (now_pair >= soon)
+        joins = late | ((before >= 0) & paired & (half == 0) & (pair < soon))
+        return joins, jnp.where(late, now_pair, pair)
+
     def fetches(self, s):
         me, line = self.me, self.line
-        depth, span = self.ring.shape[0], self.group + 1
-
-        def first(at, kind):
+        depth = self.ring.shape[0]
+        for at, shared, number in self.sending:
+            @pl.when(s == at)
+            def _(shared=shared, number=number):
+                (self.give_copy if shared else self.y_copy)(number).start()
+
+        def first(paired, pair, half, number):
             held = self.ring.at[lax.rem(s, depth)]
 
-            @pl.when(kind < 2)
-            def _():
-                side = jnp.where(kind == 0, 1 - me.side, me.side)
-                fetch(self.parts.at[at * self.group, :, side], held, self.local.at[0])
-
-            @pl.when(kind >= 2)
-            def _():
-                number = at * (self.group - 1) + kind - 2
-
-                @pl.when(number + self.ahead < self.firsts)
-                def _():
-                    self.y_copy(number + self.ahead).start()
-
-                fetch(self.parts.at[self.tile_of(number), :, me.side], held, self.local.at[0])
+            @pl.when(paired & jnp.logical_not(self.here(pair, half)))
+            def _():
+                side = jnp.where(half == 0, 1 - me.side, me.side)
+                fetch(self.parts.at[self.pair_tile(pair), :, side], held, self.local.at[0])
+
+            @pl.when(jnp.logical_not(paired))
+            def _():
+                fetch(self.parts.at[self.first_tile(number), :, me.side], held, self.local.at[0])
                 self.y_copy(number).wait()
                 fetch(self.y_land.at[number], self.got, self.local.at[1])
 
@@ -281,26 +332,30 @@
             def _():
                 fetch(self.down_land.at[item, me.spot], self.last.at[1], self.local.at[5])
 
-            @pl.when(lax.rem(item, span) == self.group - 2)
-            def _():
-                at = lax.div(item, span)
-                self.last_copy(at).wait()
-                fetch(self.last_land.at[at], self.last.at[5], self.local.at[6])
+            joins, pair = self.joined(item)
+
+            @pl.when(joins)
+            def _():
+                self.last_copy(pair).wait()
+                fetch(self.last_land.at[pair], self.last.at[3], self.local.at[6])
 
         self.stages(s, first, up, down, last)
 
     def loaded(self, target, at):
         pltpu.make_async_copy(target, target, self.local.at[at]).wait()
 
-    def sums(self, s, emit):
+    def sums(self, s, emit, emit_shared):
         me, line = self.me, self.line
-        depth, span = self.ring.shape[0], self.group + 1
-
-        def first(at, kind):
+        depth = self.ring.shape[0]
+
+        def first(paired, pair, half, number):
             held = lax.rem(s, depth)
-            self.loaded(self.ring.at[held], 0)
-
-            @pl.when(kind >= 2)
+
+            @pl.when(jnp.logical_not(paired & self.here(pair, half)))
+            def _():
+                self.loaded(self.ring.at[held], 0)
+
+            @pl.when(jnp.logical_not(paired))
             def _():
                 self.loaded(self.got, 1)
                 self.ring[held] = self.ring[held] + self.got[...]
@@ -334,7 +389,7 @@
             self.down_copy(item, count).start()
 
         def last(item):
-            at, kind = lax.div(item, span), lax.rem(item, span)
+            paired, pair, half, number = self.item(item)
             self.last[2] = self.ring[lax.rem(item, depth), me.spot]
 
             @pl.when(me.spot > 0)
@@ -347,24 +402,35 @@
                 self.loaded(self.last.at[1], 5)
                 self.last[2] = self.last[2] + self.last[1]
 
-            @pl.when(kind == 0)
-            def _():
-                self.last[3] = self.last[2]
-                self.last_copy(at).start()
-
-            @pl.when(kind == 1)
-            def _():
-                self.last[4] = self.last[2]
-
-            @pl.when(kind > 1)
-            def _():
-                emit(at * self.group + kind - 1, self.last.at[2], 0)
-
-            @pl.when(kind == self.group - 2)
-            def _():
-                self.loaded(self.last.at[5], 6)
-                self.last[4] = self.last[4] + self.last[5]
-                emit(at * self.group, self.last.at[4], 1)
+            @pl.when(paired & (half == 0))
+            def _():
+                self.leave[lax.rem(pair, 3)] = self.last[2]
+                self.last_copy(pair).start()
+
+            @pl.when(paired & (half == 1))
+            def _():
+                self.hold[lax.rem(pair, 3)] = self.last[2]
+
+            @pl.when(jnp.logical_not(paired))
+            def _():
+                emit(self.first_tile(number), self.last.at[2], 0)
+
+            joins, pair = self.joined(item)
+
+            @pl.when(joins)
+            def _():
+                self.loaded(self.last.at[3], 6)
+                third = lax.rem(pair, 3)
+
+                @pl.when(pair == 0)
+                def _():
+                    self.hold[third] = self.hold[third] + self.last[3]
+                    emit(0, self.hold.at[third], 1)
+
+                @pl.when(pair > 0)
+                def _():
+                    emit_shared(pair - 1, me.side, self.hold.at[third], 1)
+                    emit_shared(pair - 1, 1 - me.side, self.last.at[3], 2)
 
         self.stages(s, first, up, down, last)
 
@@ -373,15 +439,17 @@
             pass
 
         def last(item):
-            kind = lax.rem(item, self.group + 1)
-            pl.when(kind > 1)(lambda: emitted(0))
-            pl.when(kind == self.group - 2)(lambda: emitted(1))
+            paired, _, _, _ = self.item(item)
+            pl.when(jnp.logical_not(paired))(lambda: emitted(0))
+            joins, pair = self.joined(item)
+            pl.when(joins)(lambda: emitted(1))
+            pl.when(joins & (pair > 0))(lambda: emitted(2))
 
         self.stages(s, nothing, nothing, nothing, last)
 
-    def step(self, s, emit, emitted):
+    def step(self, s, emit, emit_shared, emitted):
         self.fetches(s)
-        self.sums(s, emit)
+        self.sums(s, emit, emit_shared)
         self.settle(s, emitted)
 
     def finish(self):
@@ -446,7 +514,7 @@
         c = s - number
         pl.when((c >= 0) & (c < self.chunks))(lambda: body(c))
 
-    def step(self, s, produce, work, lower, emit):
+    def step(self, s, produce, work, lower, emit, beside=None):
         me = self.me
 
         def stage(number, body):
@@ -465,7 +533,8 @@
             emit(c, self.low)
 
         def three(c, slot, third):
-            pass
+            if beside is not None:
+                beside(c, self.pair.at[third])
 
         def two(c, slot, third):
             self.pair[third, me.chip] = work(c, self.half[slot, me.chip] + self.chip_land[slot])
@@ -511,11 +580,11 @@
     (tokens, cot, w_query, w_key, w_value, w_output, attn_gain, mlp_gain, query_gain, key_gain,
      cosine, sine, starts), refs = take(refs, 13)
     (mlp_in, mlp_in_t, cot_t, normed_t, hidden_out, q_out, k_out, v_out, q_raw_out, k_raw_out,
-     context_out, lse_out), refs = take(refs, 12)
+     context_out, lse_out, other_out, rest_out), refs = take(refs, 14)
     sems, refs = take(refs, 8)
     buffers, refs = take(refs, 7)
     (hidden_buf, q_low, k_low, v_low, v_t, q_raw, k_raw, context, lse, normed, normed_turn,
-     cot_load, cot_turn, low_turn, sem, out_sem) = refs
+     cot_load, cot_turn, low_turn, sem, out_sem, give_sem, take_sem) = refs
     me = Spot(wide)
     me.greet(False)
     summing = NarrowSum(me, sems, buffers)
@@ -587,6 +656,14 @@
         return (value * mlp_gain[...]).astype(bf16)
 
     def emit(c, low):
+        @pl.when(c < chunks - 1)
+        def _():
+            beside(c, summing.pair.at[lax.rem(c, 3)]).wait_send()
+
+        @pl.when(c == chunks - 1)
+        def _():
+            pltpu.make_async_copy(summing.pair.at[lax.rem(c, 3)], rest_out, sem.at[5]).wait()
+
         fetch(low, mlp_in.at[c], sem.at[3])
         low_turn[...] = low[...].reshape(rows, width).T
         at = pl.ds(pl.multiple_of(c * rows, rows), rows)
@@ -603,6 +680,18 @@
 
         summing.at_stage(s, 2, two)
         summing.at_stage(s, 4, four)
+
+    def beside(c, half):
+        return remote(half, other_out.at[c], give_sem.at[c], take_sem.at[c], me.to_side)
+
+    def begin_beside(c, half):
+        @pl.when(c < chunks - 1)
+        def _():
+            beside(c, half).start()
+
+        @pl.when(c == chunks - 1)
+        def _():
+            fetch(half, rest_out, sem.at[5])
 
     def turn_rows(s):
         at = pl.ds(pl.multiple_of(s * rows, rows), rows)
@@ -619,7 +708,7 @@
         a.wait()
 
     def body(s, carry):
-        summing.step(s, produce, work, lower, emit)
+        summing.step(s, produce, work, lower, emit, begin_beside)
         pl.when(s < chunks)(lambda: turn_rows(s))
 
         @pl.when(s == chunks - 1)
@@ -633,6 +722,8 @@
     lax.fori_loop(0, summing.slots, body, 0)
     for at, (a, b) in enumerate(kept):
         pltpu.make_async_copy(a, b, out_sem.at[at]).wait()
+    for c in range(chunks - 1):
+        beside(c, summing.pair.at[c % 3]).wait_recv()
 
 
 def outer_tile(left_t, right, stage):
@@ -674,26 +765,28 @@
                     self.copy(k).start()
 
 
-def main_kernel(wide, chunks, *refs):
-    (mlp_in, mlp_in_t, cot, cot_t, normed_t, hidden, q_in, k_in, v_in, q_raw, k_raw, context,
-     lse_in, tokens, w_gate, w_up, w_down, w_output, w_query, w_key, w_value, cosine, sine,
-     starts, attn_gain, mlp_gain, query_gain, key_gain), refs = take(refs, 28)
+def main_kernel(wide, chunks, counts, *refs):
+    (mlp_in, mlp_in_t, cot, cot_t, normed_t, hidden, other, rest, q_in, k_in, v_in, q_raw, k_raw,
+     context, lse_in, tokens, w_gate, w_up, w_down, w_output, w_query, w_key, w_value, cosine, sine,
+     starts, attn_gain, mlp_gain, query_gain, key_gain), refs = take(refs, 30)
     (output, grad_tokens, grad_query, grad_key, grad_value, grad_output, grad_gate, grad_up,
-     grad_down, gains_out, grad_hidden), refs = take(refs, 11)
-    wide_lands, refs = take(refs, 5)
-    wide_sems, refs = take(refs, 9)
+     grad_down, gains_out, grad_hidden, inner_out, other_land, rest_land, rest_core,
+     other_t), refs = take(refs, 16)
+    wide_lands, refs = take(refs, 7)
+    wide_sems, refs = take(refs, 11)
     sems, refs = take(refs, 8)
-    wide_buffers, refs = take(refs, 7)
+    wide_buffers, refs = take(refs, 9)
     buffers, refs = take(refs, 7)
     (acts, gains, gain_lands, turned, gain_send, gain_recv, sem, w_sem, store_sem, emit_sem,
-     att_sem) = refs
+     att_sem, give_sem, other_sem) = refs
     me = Spot(wide)
     me.greet(True)
     token_count, width = mlp_in.shape
     hidden_units = w_gate.shape[1]
     tiles, line, _, side_rows, cols = wide_lands[0].shape
     blocks = hidden_units // cols
-    mlp_tiles = 3 * blocks
+    early_tiles, shared_tiles, late_tiles = counts
+    late_from = early_tiles + shared_tiles
     query_width, kv_width = w_query.shape[1], w_key.shape[1]
     all_heads = query_width + 2 * kv_width
     head = query_gain.shape[1]
@@ -701,52 +794,81 @@
     group = q_heads // (kv_width // head)
     scale = head ** (-0.5)
     out_tiles = query_width // cols
-    total = WideSum(me, wide_lands, wide_sems, wide_buffers)
+    narrow_from, pace = 2, 6
+    first_attend = chunks + 4
+    heads_at_once = 2
+    first_heads = first_attend + q_heads // heads_at_once
+
+    def slot_at(r):
+        return narrow_from + r - r // pace
+
+    total = WideSum(
+        me, counts, lambda late: slot_at(first_attend if late < out_tiles else first_heads),
+        wide_lands, wide_sems, wide_buffers,
+    )
+    other_copy = remote(other, other_land, other_sem.at[0], other_sem.at[1], me.to_core)
+    other_copy.start()
+    rest_side = remote(rest, rest_land, other_sem.at[6], other_sem.at[7], me.to_side)
+    rest_side.start()
+    rest_pass = remote(rest_land, rest_core, other_sem.at[8], other_sem.at[9], me.to_core)
     half = token_count // 2
     rows = token_count // chunks
     quarter = rows // 4
 
-    early = (0, 1, 4)
+    def block_of(t):
+        return lax.rem(t, 2) * (blocks // 2) + lax.div(t, 2)
+
+    def half_of(b):
+        return lax.div(b, blocks // 2)
+
+    def columns(at):
+        return pl.ds(pl.multiple_of(at * cols, cols), cols)
 
     def emit_tile(tile, value, number):
-        def part(first, count, target, turn, every=1, offset=0):
-            inside = (tile >= first) & (tile < first + count)
-            at = tile - first
-            if every > 1:
-                inside = inside & (lax.rem(at, every) == offset)
-                at = lax.div(at, every)
-
-            @pl.when(inside)
-            def _():
-                cut = pl.ds(pl.multiple_of(at * cols, cols), cols)
+        def part(first, count, target, turn, place):
+            @pl.when((tile >= first) & (tile < first + count))
+            def _():
+                cut = columns(place(tile - first))
                 if turn:
                     turned[number] = value[...].T
                     fetch(turned.at[number], target.at[cut, :], emit_sem.at[number])
                 else:
                     fetch(value, target.at[:, cut], emit_sem.at[number])
 
-        part(0, mlp_tiles, grad_down, True, 3, 0)
-        part(0, mlp_tiles, grad_gate, False, 3, 1)
-        part(0, mlp_tiles, grad_up, False, 3, 2)
-        at = mlp_tiles
-        part(at, out_tiles, grad_output, True)
+        def same(at):
+            return at
+
+        part(0, early_tiles, grad_down, True, block_of)
+        at = late_from
+        part(at, out_tiles, grad_output, True, same)
         at += out_tiles
-        part(at, query_width // cols, grad_query, False)
+        part(at, query_width // cols, grad_query, False, same)
         at += query_width // cols
-        part(at, kv_width // cols, grad_key, False)
+        part(at, kv_width // cols, grad_key, False, same)
         at += kv_width // cols
-        part(at, kv_width // cols, grad_value, False)
+        part(at, kv_width // cols, grad_value, False, same)
+
+    def emit_shared(t, side, value, number):
+        cut = columns(side * (blocks // 2) + lax.div(t, 2))
+
+        @pl.when(lax.rem(t, 2) == 0)
+        def _():
+            fetch(value, grad_gate.at[:, cut], emit_sem.at[number])
+
+        @pl.when(lax.rem(t, 2) == 1)
+        def _():
+            fetch(value, grad_up.at[:, cut], emit_sem.at[number])
 
     def emitted(number):
-        pltpu.make_async_copy(turned.at[number], turned.at[number], emit_sem.at[number]).wait()
-
-    def compute(xs, xt, cs, ct, gate_w, up_w, down_w, staged):
-        pairs = ((mlp_in, xs), (cot, cs), (cot_t, ct), (mlp_in_t, xt))
-        for at, (a, b) in enumerate(pairs):
-            fetch(a, b, sem.at[at])
-
-        def weights(b, slot):
-            at = pl.ds(pl.multiple_of(b * cols, cols), cols)
+        pltpu.make_async_copy(turned.at[0], turned.at[0], emit_sem.at[number]).wait()
+
+    def compute(xs, cs, ct, gate_w, up_w, down_w, staged, inner, gives):
+        pairs = ((mlp_in, xs), (cot, cs), (cot_t, ct))
+        for at, (source, target) in enumerate(pairs[:2]):
+            fetch(source, target, sem.at[at])
+
+        def weights(t, slot):
+            at = columns(block_of(t))
             return (
                 pltpu.make_async_copy(w_gate.at[:, at], gate_w.at[slot], w_sem.at[slot, 0]),
                 pltpu.make_async_copy(w_up.at[:, at], up_w.at[slot], w_sem.at[slot, 1]),
@@ -755,24 +877,45 @@
 
         for copy in weights(0, 0):
             copy.start()
-        for at, (a, b) in enumerate(pairs):
-            pltpu.make_async_copy(a, b, sem.at[at]).wait()
+        for at, (source, target) in enumerate(pairs[:2]):
+            pltpu.make_async_copy(source, target, sem.at[at]).wait()
+        fetch(cot_t, ct, sem.at[2])
 
         def store(tile):
             slot = lax.rem(tile, 2)
             return pltpu.make_async_copy(staged.at[slot], total.parts.at[tile], store_sem.at[slot])
 
-        def block(b, carry):
-            slot = lax.rem(b, 2)
-            for copy in weights(b, slot):
+        def store_inner(t):
+            slot = lax.rem(t, 2)
+            target = inner_out.at[:, columns(block_of(t))]
+            return pltpu.make_async_copy(inner.at[slot], target, give_sem.at[2 + slot])
+
+        def store_gives(t):
+            return [
+                pltpu.make_async_copy(
+                    gives.at[j], total.give.at[2 * lax.div(t, 2) + j], give_sem.at[j]
+                )
+                for j in range(2)
+            ]
+
+        def leaves(t):
+            return half_of(block_of(t)) != me.side
+
+        def block(t, carry):
+            slot = lax.rem(t, 2)
+            for copy in weights(t, slot):
                 copy.wait()
 
-            @pl.when(b + 1 < blocks)
-            def _():
-                for copy in weights(b + 1, 1 - slot):
+            @pl.when(t + 1 < blocks)
+            def _():
+                for copy in weights(t + 1, 1 - slot):
                     copy.start()
 
-            at = pl.ds(pl.multiple_of(b * cols, cols), cols)
+            @pl.when(t >= 2)
+            def _():
+                store_inner(t - 2).wait()
+
+            at = columns(block_of(t))
 
             def some(m, carry):
                 own = pl.ds(pl.multiple_of(m * half, half), half)
@@ -781,45 +924,79 @@
                 back = nt_dot(cs[own, :], down_w[slot])
                 sig = 1.0 / (1.0 + jnp.exp(-gate))
                 silu = gate * sig
-                acts[0, own, at] = (silu * up).astype(bf16)
-                acts[1, own, at] = (back * up * sig * (1.0 + gate * (1.0 - sig))).astype(bf16)
-                acts[2, own, at] = (back * silu).astype(bf16)
+                inner[slot, own, :] = (silu * up).astype(bf16)
+                grad_gate_low = (back * up * sig * (1.0 + gate * (1.0 - sig))).astype(bf16)
+                grad_up_low = (back * silu).astype(bf16)
+                acts[0, own, at] = grad_gate_low
+                acts[1, own, at] = grad_up_low
+
+                @pl.when(leaves(t))
+                def _():
+                    lines = line // 2
+                    there = pl.ds(m * lines, lines)
+                    shape = (lines, side_rows, cols)
+                    gives[0, there] = grad_gate_low.astype(f32).reshape(shape)
+                    gives[1, there] = grad_up_low.astype(f32).reshape(shape)
+
                 return carry
 
             lax.fori_loop(0, 2, some, 0)
-            for j in range(3):
-                tile = 3 * b + j
-                outer_tile(ct if j == 0 else xt, acts[j, :, at], staged.at[lax.rem(tile, 2)])
-                store(tile).start()
-
-                @pl.when(tile > 0)
-                def _(tile=tile):
-                    store(tile - 1).wait()
-                    total.begin(tile - 1)
-
-            for number, after in enumerate(early):
-                pl.when(b == after)(lambda: total.step(number, emit_tile, emitted))
+            store_inner(t).start()
+
+            @pl.when(leaves(t))
+            def _():
+                for copy in store_gives(t):
+                    copy.start()
+
+            @pl.when(t == 0)
+            def _():
+                pltpu.make_async_copy(cot_t, ct, sem.at[2]).wait()
+
+            outer_tile(ct, inner[slot], staged.at[slot])
+            store(t).start()
+
+            @pl.when(t == 0)
+            def _():
+                store(t).wait()
+
+            @pl.when(t > 1)
+            def _():
+                store(t - 1).wait()
+                total.begin(t - 1)
+
+            @pl.when(leaves(t))
+            def _():
+                for copy in store_gives(t):
+                    copy.wait()
+
+            for number, after in enumerate((0, 2)):
+                pl.when(t == after)(
+                    lambda number=number: total.step(number, emit_tile, emit_shared, emitted)
+                )
             return carry
 
         lax.fori_loop(0, blocks, block, 0)
-        store(mlp_tiles - 1).wait()
+        store(blocks - 1).wait()
+        store_inner(blocks - 2).wait()
+        store_inner(blocks - 1).wait()
 
     pl.run_scoped(
         compute,
         pltpu.VMEM(mlp_in.shape, bf16),
-        pltpu.VMEM(mlp_in_t.shape, bf16),
         pltpu.VMEM(mlp_in.shape, bf16),
         pltpu.VMEM(mlp_in_t.shape, bf16),
         pltpu.VMEM((2, width, cols), bf16),
         pltpu.VMEM((2, width, cols), bf16),
         pltpu.VMEM((2, cols, width), bf16),
         pltpu.VMEM((2, line, 2, side_rows, cols), f32),
+        pltpu.VMEM((2, token_count, cols), bf16),
+        pltpu.VMEM((2, line, side_rows, cols), f32),
     )
 
     def pass_on(*held):
         (gate_w, up_w, down_w, hidden_load, token_load, out_buf, out_w, left_t, staged, q_low,
          k_low, v_low, k_t, d_context, right, lse, cos, sin, raw, d_query, d_key, d_value,
-         heads) = held
+         heads, inner_load, other_load, other_turn, left_cut) = held
         summing = NarrowSum(me, sems, buffers)
         small = SmallSum(me, gains, gain_lands, gain_send, gain_recv)
         gains[...] = jnp.zeros_like(gains)
@@ -833,9 +1010,6 @@
             fetch(a, b, sem.at[0]).wait()
         k_t[...] = k_low[...].T
         step = gate_w.shape[1]
-        narrow_from = len(early)
-        first_attend = narrow_from + chunks + 4
-        first_heads = first_attend + q_heads
 
         def stream(copies, use):
             count = width // step
@@ -865,13 +1039,15 @@
                     )
 
                 def use(slot, cut):
-                    value = nt_dot(acts[1, own, :], gate_w[slot, :, 0:hidden_units])
-                    store_part(part, value + nt_dot(acts[2, own, :], up_w[slot]), cut)
+                    value = nt_dot(acts[0, own, :], gate_w[slot, :, 0:hidden_units])
+                    store_part(part, value + nt_dot(acts[1, own, :], up_w[slot]), cut)
 
                 stream(copies, use)
 
             @pl.when(kind == 1)
             def _():
+                fetch(inner_out.at[own, :], inner_load, att_sem.at[0]).wait()
+
                 def copies(at, slot):
                     cut = pl.ds(at * step, step)
                     return (
@@ -879,7 +1055,7 @@
                     )
 
                 def use(slot, cut):
-                    store_part(part, forward_dot(acts[0, own, :], down_w[slot]), cut)
+                    store_part(part, forward_dot(inner_load[...], down_w[slot]), cut)
 
                 stream(copies, use)
 
@@ -985,6 +1161,68 @@
             @pl.when(kind == 2)
             def _():
                 fetch(low, grad_tokens.at[chunk], sem.at[3])
+
+        def take_other(c):
+            mine, theirs = other_load.at[me.core], other_load.at[1 - me.core]
+
+            @pl.when(c < chunks - 1)
+            def _():
+                a = fetch(other.at[c], mine, att_sem.at[0])
+                fetch(other_land.at[c], theirs, give_sem.at[0]).wait()
+                a.wait()
+
+            @pl.when(c == chunks - 1)
+            def _():
+                rest_pass.wait()
+                a = fetch(rest_land, mine, att_sem.at[0])
+                fetch(rest_core, theirs, give_sem.at[0]).wait()
+                a.wait()
+
+            value = (other_load[...] * mlp_gain[...][None, None]).astype(bf16)
+            other_turn[...] = value.reshape(rows, width).T
+            at = pl.ds(pl.multiple_of(c * rows, rows), rows)
+            fetch(other_turn, other_t.at[:, at], att_sem.at[0]).wait()
+
+        def put_shared(t, s):
+            total.give_copy(t).wait()
+            load = fetch(total.give_land.at[t], total.got, att_sem.at[0])
+            mine = acts[lax.rem(t, 2), :, columns(me.side * (blocks // 2) + lax.div(t, 2))]
+            group = left_cut.shape[2]
+            count = width // group
+
+            def copies(m, slot):
+                at = pl.ds(pl.multiple_of(m * group, group), group)
+                return (
+                    pltpu.make_async_copy(mlp_in_t.at[at, :], left_cut.at[slot, 0], other_sem.at[2 + slot]),
+                    pltpu.make_async_copy(other_t.at[at, :], left_cut.at[slot, 1], other_sem.at[4 + slot]),
+                )
+
+            for copy in copies(0, 0):
+                copy.start()
+            load.wait()
+            right[...] = total.got[...].reshape(token_count, cols).astype(bf16)
+
+            def one(m, carry):
+                slot = lax.rem(m, 2)
+                for copy in copies(m, slot):
+                    copy.wait()
+
+                @pl.when(m + 1 < count)
+                def _():
+                    for copy in copies(m + 1, 1 - slot):
+                        copy.start()
+
+                value = forward_dot(left_cut[slot, 0], mine) + forward_dot(left_cut[slot, 1], right[...])
+                lines = group // (2 * side_rows)
+                staged[pl.ds(m * lines, lines)] = value.reshape((lines, 2, side_rows, cols))
+                return carry
+
+            lax.fori_loop(0, count, one, 0)
+            fetch(staged, total.parts.at[early_tiles + t], store_sem.at[0])
+            total.ring[lax.rem(s, total.ring.shape[0])] = staged[:, 1 - me.side]
+
+        def shared_stored():
+            pltpu.make_async_copy(staged, total.parts.at[0], store_sem.at[0]).wait()
 
         def put(tile, right_value):
             outer_tile(left_t, right_value, staged)
@@ -1036,40 +1274,83 @@
                 there = pl.ds(pl.multiple_of(query_width + kv_width + kv * head, head), head)
                 heads[:, there] = d_value[...].astype(bf16)
 
-        small_at = narrow_from + summing.slots - 1
-
-        def body(s, carry):
-            @pl.when(s == first_attend)
+        small_at = summing.slots - 1
+        steps = small_at + 5
+        while slot_at(steps) < total.slots:
+            steps += 1
+
+        def shared_at(s):
+            paired, pair, second, _ = total.item(s)
+            return paired & total.here(pair, second) & (s < total.items)
+
+        def settle_all(r):
+            s = narrow_from + r - lax.div(r, pace)
+
+            @pl.when((r >= 0) & (lax.rem(r, pace) != pace - 1))
+            def _():
+                total.settle(s, emitted)
+                pl.when(shared_at(s))(shared_stored)
+
+            settle(r)
+
+        def body(r, carry):
+            s = narrow_from + r - lax.div(r, pace)
+            wide_too = lax.rem(r, pace) != pace - 1
+            settle_all(r - 1)
+
+            @pl.when(r == first_attend)
             def _():
                 for t in range(out_tiles):
                     cut = slice(t * cols, (t + 1) * cols)
                     fetch(context.at[:, cut], right, att_sem.at[0]).wait()
-                    put(mlp_tiles + t, right[...])
-
-            @pl.when((s >= first_attend) & (s < first_heads))
-            def _():
-                attend_back(s - first_attend)
-
-            @pl.when(s == first_heads)
+                    put(late_from + t, right[...])
+
+            @pl.when((r >= first_attend) & (r < first_heads))
+            def _():
+                def one(h, carry):
+                    attend_back((r - first_attend) * heads_at_once + h)
+                    return carry
+
+                lax.fori_loop(0, heads_at_once, one, 0)
+
+            @pl.when(r == first_heads)
             def _():
                 fetch(normed_t, left_t, att_sem.at[0]).wait()
 
                 def one(t, carry):
-                    put(mlp_tiles + out_tiles + t, heads[:, pl.ds(pl.multiple_of(t * cols, cols), cols)])
+                    put(late_from + out_tiles + t, heads[:, columns(t)])
                     return carry
 
                 lax.fori_loop(0, all_heads // cols, one, 0)
 
-            summing.at_stage(s - narrow_from, 2, preload)
-            total.fetches(s)
-            summing.step(s - narrow_from, produce, work, lower, emit_rows)
-            total.sums(s, emit_tile)
-            total.settle(s, emitted)
-            settle(s - narrow_from)
-            pl.when(s >= small_at)(lambda: small.step(s - small_at))
+            @pl.when(r == 0)
+            def _():
+                other_copy.wait()
+                rest_side.wait()
+                rest_pass.start()
+
+            @pl.when(r < chunks // 2)
+            def _():
+                for each in range(2):
+                    take_other(r * 2 + each)
+
+            @pl.when(wide_too & shared_at(s))
+            def _():
+                put_shared(total.item(s)[1] - 1, s)
+
+            summing.at_stage(r, 2, preload)
+            pl.when(wide_too)(lambda: total.fetches(s))
+            summing.step(r, produce, work, lower, emit_rows)
+
+            @pl.when(wide_too)
+            def _():
+                total.sums(s, emit_tile, emit_shared)
+
+            pl.when(r >= small_at)(lambda: small.step(r - small_at))
             return carry
 
-        lax.fori_loop(narrow_from, max(total.slots, small_at + 5), body, 0)
+        lax.fori_loop(0, steps, body, 0)
+        settle_all(steps - 1)
         total.finish()
 
     step = min(256, width)
@@ -1098,6 +1379,10 @@
         pltpu.VMEM((token_count, head), f32),
         pltpu.VMEM((token_count, head), f32),
         pltpu.VMEM((token_count, all_heads), bf16),
+        pltpu.VMEM((2 * rows, hidden_units), bf16),
+        pltpu.VMEM((2, 2, quarter, width), f32),
+        pltpu.VMEM((width, rows), bf16),
+        pltpu.VMEM((2, 2, max(512, 2 * side_rows), token_count), bf16),
     )
     fetch(gains, gains_out, sem.at[0]).wait()
 
@@ -1177,9 +1462,11 @@
             shape((width, token_count), bf16),
             shape((chunks, quarter, width), f32),
             *kept,
+            shape((chunks - 1, 2, quarter, width), f32),
+            shape((2, quarter, width), f32),
         ],
         [in_vmem, any_space] + [in_vmem] * 11,
-        [any_space] * 12,
+        [any_space] * 14,
         [
             *NarrowSum.sems(chunks),
             *NarrowSum.buffers(quarter, width),
@@ -1192,8 +1479,10 @@
             pltpu.VMEM((rows, width), bf16),
             pltpu.VMEM((width, rows), bf16),
             pltpu.VMEM((width, rows), bf16),
-            dma((5,)),
+            dma((6,)),
             dma((7,)),
+            dma((chunks,)),
+            dma((chunks,)),
         ],
         (
             tokens, cotangent, w_query, key_weight, value_weight, w_output, attn_gain[None],
@@ -1201,13 +1490,13 @@
         ),
     )
     (mlp_in, mlp_in_t, cot_t, normed_t, hidden, q_low, k_low, v_low, q_raw, k_raw, context,
-     lse) = outs[:12]
+     lse, other, rest) = outs[:14]
 
     cols = min(256 if line <= 4 else 128, hidden_units // 6)
-    tiles = (3 * hidden_units + query_width + all_heads) // cols
+    counts = (hidden_units // cols, hidden_units // cols, (query_width + all_heads) // cols)
     gain_width = 2 * width + 2 * head_dim
     outs = call(
-        lambda *refs: main_kernel(wide, chunks, *refs),
+        lambda *refs: main_kernel(wide, chunks, counts, *refs),
         2,
         [
             shape((chunks, 2, 2, quarter, width), bf16),
@@ -1221,16 +1510,21 @@
             shape((hidden_units, side_rows), f32),
             shape((1, gain_width), f32),
             shape((chunks, quarter, width), f32),
-            *WideSum.lands(tiles, line, side_rows, cols),
+            shape((token_count, hidden_units), bf16),
+            shape((chunks - 1, 2, quarter, width), f32),
+            shape((2, quarter, width), f32),
+            shape((2, quarter, width), f32),
+            shape((width, token_count), bf16),
+            *WideSum.lands(counts, line, side_rows, cols),
         ],
-        [any_space] * 23 + [in_vmem] * 5,
-        [any_space] * 16,
+        [any_space] * 25 + [in_vmem] * 5,
+        [any_space] * 23,
         [
-            *WideSum.sems(tiles),
+            *WideSum.sems(counts),
             *NarrowSum.sems(3 * chunks),
             *WideSum.buffers(line, side_rows, cols),
             *NarrowSum.buffers(quarter, width),
-            pltpu.VMEM((3, token_count, hidden_units), bf16),
+            pltpu.VMEM((2, token_count, hidden_units), bf16),
             pltpu.VMEM((1, gain_width), f32),
             pltpu.VMEM((2 + line, 1, gain_width), f32),
             pltpu.VMEM((2, cols, side_rows), f32),
@@ -1239,12 +1533,14 @@
             dma((4,)),
             dma((2, 3)),
             dma((2,)),
-            dma((2,)),
+            dma((3,)),
             dma((1,)),
+            dma((4,)),
+            dma((10,)),
         ],
         (
             mlp_in.reshape(token_count, width), mlp_in_t, cotangent, cot_t, normed_t, hidden,
-            q_low, k_low, v_low, q_raw, k_raw, context, lse, tokens, w_gate, w_up, w_down,
+            other, rest, q_low, k_low, v_low, q_raw, k_raw, context, lse, tokens, w_gate, w_up, w_down,
             w_output, w_query, key_weight, value_weight, cosine, sine, starts, attn_gain[None],
             mlp_gain[None], query_gain[None], key_norm_gain[None],
         ),

time: 689 us -> 665 us (0.965)
  Pallas kernels: 664 us -> 639 us
    pallas_call x2, Pallas kernels: 664 us -> 639 us  [call(): pl.pallas_call(kernel, out_shape=out_shape, in_specs=in_specs, out_specs=...]
where the time goes in v4:
time: 665 us; the launch traced here: 661 us
  Pallas kernels  639 us (96%)
  local copies, waits for them, and re-layouts  16 us (2%)
    pallas_call x2, Pallas kernels, call(): pl.pallas_call(kernel, out_shape=out_shape, in_specs=in_specs, out_specs=...  639 us
    unnamed x25, local copies, waits for them, and re-layouts  13.5 us

profile of v4, /device:TPU:0, one launch (start us, length us, event | category | flops | bytes accessed | tf_op | source)
XLA Modules:
  0.0 660.9 jit_solution(5377645857976755823)
XLA Ops:
  0.6 0.8 reduce_window_sum.11
  1.5 0.1 convert_reduce_fusion
  1.6 0.7 subtract_bitcast_fusion
  2.2 0.1 select_reduce_fusion
  2.3 0.2 broadcast_multiply_fusion
  2.6 2.9 sine_multiply_fusion
  5.4 0.6 subtract_subtract_fusion.refs_12_.refs_25_
  6.0 113.6 %shard_map.237 = (bf16[8,2,2,32,2048]{4,3,2,1,0:T(8,128)(2,1)}, bf16[2048,1024]{1,0:T(8,128)(2,1)}, bf16[2048,1024]{1,0:T(8,128)(2,1)}, bf16[2048,1024]{1,0:T(8,...) custom-call(bf16[1024,2048]{1,0:T(8,128)(2,1)} %refs_15_.1, ...), custom_call_target="tpu_custom_call" | custom-call | tf_op jit(solution)/shard_map/pallas_call | solution.py:1391
  119.6 525.2 %shard_map.238 = (bf16[8,2,2,32,2048]{4,3,2,1,0:T(8,128)(2,1)}, bf16[8,2,2,32,2048]{4,3,2,1,0:T(8,128)(2,1)}, f32[256,512]{1,0:T(8,128)}, f32[256,256]{1,0:T(8,1...) custom-call(bf16[1024,2048]{1,0:T(8,128)(2,1)} %bitcast.17, ...), custom_call_target="tpu_custom_call" | custom-call | tf_op jit(solution)/shard_map/pallas_call | solution.py:1391
  644.8 1.3 constant_dynamic-slice_fusion.3
  646.1 1.3 fusion.2
  647.3 0.0 copy-start
  647.3 4.9 copy.36
  652.3 0.0 copy-done
  652.3 0.0 copy-start.5
  652.3 0.0 copy-start.4
  652.3 0.0 copy-start.3
  652.3 2.1 copy.37
  654.4 0.0 copy-done.5
  654.4 0.8 copy.38
  655.2 0.0 copy-done.7
  655.2 0.7 copy.39
  655.9 0.0 copy-done.6
  655.9 0.7 copy.40
  656.7 0.0 copy-done.4
  656.7 0.8 copy.41
  657.4 0.0 copy-done.3
  657.4 1.1 copy.42
  658.6 0.0 copy-done.2
  658.6 1.1 copy.43
  659.7 0.0 copy-done.1
  659.7 1.1 copy.44
  (7 shorter events, 0.0 us)
Async XLA Ops:
  647.3 4.9 copy-start
  652.3 2.2 copy-start.5
  652.3 3.0 copy-start.7
  652.3 3.7 copy-start.6
  652.3 4.4 copy-start.4
  652.3 5.2 copy-start.3
  654.4 4.2 copy-start.2
  655.2 4.5 copy-start.1

commit v5 on v4

--- a/solution.py
+++ b/solution.py
@@ -132,11 +132,12 @@
         ]
 
     @classmethod
-    def sems(cls, counts):
-        dma = pltpu.SemaphoreType.DMA
+    def sems(cls, counts, line):
+        dma, hops = pltpu.SemaphoreType.DMA, line - 1
         tiles, firsts, pairs, items = cls.numbers(counts)
         return [
-            dma((firsts,)), dma((firsts,)), dma((2,)), dma((items,)), dma((2,)), dma((items,)),
+            dma((firsts,)), dma((firsts,)), dma((2, hops)), dma((items, hops)), dma((2, hops)),
+            dma((items, hops)),
             dma((pairs,)), dma((pairs,)), dma((counts[1],)), dma((counts[1],)), dma((7,)),
         ]
 
@@ -222,28 +223,30 @@
             self.last_send.at[pair], self.last_recv.at[pair], self.me.to_side,
         )
 
-    def up_copy(self, item, count):
+    def up_copy(self, item, at):
         slot = lax.rem(item, 2)
         return remote(
-            self.up_buf.at[slot, 0:count], self.up_land.at[item, 0:count],
-            self.up_send.at[slot], self.up_recv.at[item], self.me.to_up,
+            self.up_buf.at[slot, at], self.up_land.at[item, at],
+            self.up_send.at[slot, at], self.up_recv.at[item, at], self.me.to_up,
         )
 
-    def down_copy(self, item, count):
+    def down_copy(self, item, at):
         slot = lax.rem(item, 2)
         return remote(
-            self.down_buf.at[slot, 0:count], self.down_land.at[item, 0:count],
-            self.down_send.at[slot], self.down_recv.at[item], self.me.to_down,
+            self.down_buf.at[slot, at], self.down_land.at[item, at],
+            self.down_send.at[slot, at], self.down_recv.at[item, at], self.me.to_down,
         )
 
-    def await_up(self, item, count):
-        land = self.up_land.at[item, 0:count]
-        remote(land, land, self.up_send.at[0], self.up_recv.at[item], self.me.to_up).wait_recv()
-
-    def await_down(self, item, count):
-        land = self.down_land.at[item, 0:count]
+    def await_up(self, item, at):
+        land = self.up_land.at[item, at]
         remote(
-            land, land, self.down_send.at[0], self.down_recv.at[item], self.me.to_down
+            land, land, self.up_send.at[0, 0], self.up_recv.at[item, at], self.me.to_up
+        ).wait_recv()
+
+    def await_down(self, item, at):
+        land = self.down_land.at[item, at]
+        remote(
+            land, land, self.down_send.at[0, 0], self.down_recv.at[item, at], self.me.to_down
         ).wait_recv()
 
     @property
@@ -300,29 +303,41 @@
                 fetch(self.y_land.at[number], self.got, self.local.at[1])
 
         def up(item, k, count):
-            if k > 0:
-                self.await_up(item, count + 1)
+            if k == 0:
+                return
+
+            @pl.when(item < self.items - 1)
+            def _():
+                for at in range(count + 1):
+                    self.await_up(item, at)
                 fetch(
                     self.up_land.at[item, 1 : count + 1], self.up_load.at[0:count],
                     self.local.at[2],
                 )
 
         def down(item, k, count):
-            if k < line - 1:
-                self.await_down(item, count + 1)
+            if k == line - 1:
+                return
+
+            @pl.when(item < self.items - 1)
+            def _():
+                for at in range(count + 1):
+                    self.await_down(item, at)
                 fetch(
                     self.down_land.at[item, 0:count], self.down_load.at[0:count],
                     self.local.at[3],
                 )
 
         def last(item):
-            @pl.when(me.spot == line - 1)
-            def _():
-                self.await_up(item, 1)
-
-            @pl.when(me.spot == 0)
-            def _():
-                self.await_down(item, 1)
+            final = item == self.items - 1
+
+            @pl.when((me.spot == line - 1) | (final & (me.spot > 0)))
+            def _():
+                self.await_up(item, 0)
+
+            @pl.when((me.spot == 0) | (final & (me.spot < line - 1)))
+            def _():
+                self.await_down(item, me.spot)
 
             @pl.when(me.spot > 0)
             def _():
@@ -362,31 +377,67 @@
 
         def up(item, k, count):
             slot, held = lax.rem(item, 2), lax.rem(item, depth)
+            order = range(count - 1, -1, -1)
 
             @pl.when(item >= 2)
             def _():
-                self.up_copy(item, count).wait_send()
-
-            if k > 0:
+                for at in order:
+                    self.up_copy(item, at).wait_send()
+
+            if k == 0:
+                self.up_buf[slot, 0:count] = self.ring[held, 1:line]
+                for at in order:
+                    self.up_copy(item, at).start()
+                return
+
+            @pl.when(item < self.items - 1)
+            def _():
                 self.loaded(self.up_load.at[0:count], 2)
                 self.up_buf[slot, 0:count] = self.ring[held, k + 1 : line] + self.up_load[0:count]
-            else:
-                self.up_buf[slot, 0:count] = self.ring[held, k + 1 : line]
-            self.up_copy(item, count).start()
+                for at in order:
+                    self.up_copy(item, at).start()
+
+            @pl.when(item == self.items - 1)
+            def _():
+                for at in order:
+                    self.await_up(item, at + 1)
+                    fetch(
+                        self.up_land.at[item, at + 1], self.up_load.at[at], self.local.at[2]
+                    ).wait()
+                    self.up_buf[slot, at] = self.ring[held, k + 1 + at] + self.up_load[at]
+                    self.up_copy(item, at).start()
 
         def down(item, k, count):
             slot, held = lax.rem(item, 2), lax.rem(item, depth)
+            order = range(count)
 
             @pl.when(item >= 2)
             def _():
-                self.down_copy(item, count).wait_send()
-
-            if k < line - 1:
+                for at in order:
+                    self.down_copy(item, at).wait_send()
+
+            if k == line - 1:
+                self.down_buf[slot, 0:count] = self.ring[held, 0:count]
+                for at in order:
+                    self.down_copy(item, at).start()
+                return
+
+            @pl.when(item < self.items - 1)
+            def _():
                 self.loaded(self.down_load.at[0:count], 3)
                 self.down_buf[slot, 0:count] = self.ring[held, 0:count] + self.down_load[0:count]
-            else:
-                self.down_buf[slot, 0:count] = self.ring[held, 0:count]
-            self.down_copy(item, count).start()
+                for at in order:
+                    self.down_copy(item, at).start()
+
+            @pl.when(item == self.items - 1)
+            def _():
+                for at in order:
+                    self.await_down(item, at)
+                    fetch(
+                        self.down_land.at[item, at], self.down_load.at[at], self.local.at[3]
+                    ).wait()
+                    self.down_buf[slot, at] = self.ring[held, at] + self.down_load[at]
+                    self.down_copy(item, at).start()
 
         def last(item):
             paired, pair, half, number = self.item(item)
@@ -458,13 +509,15 @@
             @pl.when(me.spot == k)
             def _(k=k):
                 for item in range(self.items - 2, self.items):
-                    self.up_copy(item, line - 1 - k).wait_send()
+                    for at in range(line - 1 - k):
+                        self.up_copy(item, at).wait_send()
 
         for k in range(1, line):
             @pl.when(me.spot == k)
             def _(k=k):
                 for item in range(self.items - 2, self.items):
-                    self.down_copy(item, k).wait_send()
+                    for at in range(k):
+                        self.down_copy(item, at).wait_send()
 
 
 class NarrowSum:
@@ -1011,68 +1064,71 @@
         k_t[...] = k_low[...].T
         step = gate_w.shape[1]
 
-        def stream(copies, use):
+        def weights_of(kind, at, slot):
+            cut = pl.ds(at * step, step)
+            if kind == 0:
+                gate = gate_w.at[slot, :, 0:hidden_units]
+                return [
+                    pltpu.make_async_copy(w_gate.at[cut, :], gate, w_sem.at[slot, 0]),
+                    pltpu.make_async_copy(w_up.at[cut, :], up_w.at[slot], w_sem.at[slot, 1]),
+                ]
+            if kind == 1:
+                return [
+                    pltpu.make_async_copy(w_down.at[:, cut], down_w.at[slot], w_sem.at[slot, 2])
+                ]
+            start, found = 0, []
+            for j, w in enumerate((w_query, w_key, w_value)):
+                there = gate_w.at[slot, :, start : start + w.shape[1]]
+                found.append(pltpu.make_async_copy(w.at[cut, :], there, w_sem.at[slot, j]))
+                start += w.shape[1]
+            return found
+
+        def of_kind(c, body):
+            kind = lax.div(c, chunks)
+            for number in range(3):
+                pl.when(kind == number)(functools.partial(body, number))
+
+        def chunk_rows(c):
+            at = lax.rem(c, chunks) * rows
+            return pl.ds(pl.multiple_of(at, 2 * rows), 2 * rows)
+
+        def inner_copy(c):
+            return pltpu.make_async_copy(inner_out.at[chunk_rows(c), :], inner_load, sem.at[4])
+
+        def ahead_of_produce(c):
+            def start(kind):
+                if kind == 1:
+                    inner_copy(c).start()
+                for at in range(2):
+                    for copy in weights_of(kind, at, at):
+                        copy.start()
+
+            pl.when(lax.rem(c, 2) == 0)(lambda: of_kind(c, start))
+
+        def produce(c, part):
+            own = chunk_rows(c)
             count = width // step
-            for copy in copies(0, 0):
-                copy.start()
-            for at in range(count):
-                if at + 1 < count:
-                    for copy in copies(at + 1, (at + 1) % 2):
-                        copy.start()
-                for copy in copies(at, at % 2):
-                    copy.wait()
-                use(at % 2, slice(at * step, (at + 1) * step))
-
-        def produce(c, part):
-            chunk = lax.rem(c, chunks)
-            own = pl.ds(pl.multiple_of(chunk * rows, 2 * rows), 2 * rows)
-            kind = lax.div(c, chunks)
-
-            @pl.when(kind == 0)
-            def _():
-                def copies(at, slot):
-                    cut = pl.ds(at * step, step)
-                    gate = gate_w.at[slot, :, 0:hidden_units]
-                    return (
-                        pltpu.make_async_copy(w_gate.at[cut, :], gate, w_sem.at[slot, 0]),
-                        pltpu.make_async_copy(w_up.at[cut, :], up_w.at[slot], w_sem.at[slot, 1]),
-                    )
-
-                def use(slot, cut):
-                    value = nt_dot(acts[0, own, :], gate_w[slot, :, 0:hidden_units])
-                    store_part(part, value + nt_dot(acts[1, own, :], up_w[slot]), cut)
-
-                stream(copies, use)
-
-            @pl.when(kind == 1)
-            def _():
-                fetch(inner_out.at[own, :], inner_load, att_sem.at[0]).wait()
-
-                def copies(at, slot):
-                    cut = pl.ds(at * step, step)
-                    return (
-                        pltpu.make_async_copy(w_down.at[:, cut], down_w.at[slot], w_sem.at[slot, 2]),
-                    )
-
-                def use(slot, cut):
-                    store_part(part, forward_dot(inner_load[...], down_w[slot]), cut)
-
-                stream(copies, use)
-
-            @pl.when(kind == 2)
-            def _():
-                def copies(at, slot):
-                    cut, start, found = pl.ds(at * step, step), 0, []
-                    for j, w in enumerate((w_query, w_key, w_value)):
-                        there = gate_w.at[slot, :, start : start + w.shape[1]]
-                        found.append(pltpu.make_async_copy(w.at[cut, :], there, w_sem.at[slot, j]))
-                        start += w.shape[1]
-                    return found
-
-                def use(slot, cut):
-                    store_part(part, nt_dot(heads[own, :], gate_w[slot, :, 0:all_heads]), cut)
-
-                stream(copies, use)
+
+            def make(kind):
+                if kind == 1:
+                    inner_copy(c).wait()
+                for at in range(count):
+                    slot = at % 2
+                    if 1 <= at < count - 1:
+                        for copy in weights_of(kind, at + 1, 1 - slot):
+                            copy.start()
+                    for copy in weights_of(kind, at, slot):
+                        copy.wait()
+                    if kind == 0:
+                        value = nt_dot(acts[0, own, :], gate_w[slot, :, 0:hidden_units])
+                        value = value + nt_dot(acts[1, own, :], up_w[slot])
+                    elif kind == 1:
+                        value = forward_dot(inner_load[...], down_w[slot])
+                    else:
+                        value = nt_dot(heads[own, :], gate_w[slot, :, 0:all_heads])
+                    store_part(part, value, slice(at * step, (at + 1) * step))
+
+            of_kind(c, make)
 
         def preload(c):
             chunk, kind = lax.rem(c, chunks), lax.div(c, chunks)
@@ -1274,7 +1330,7 @@
                 there = pl.ds(pl.multiple_of(query_width + kv_width + kv * head, head), head)
                 heads[:, there] = d_value[...].astype(bf16)
 
-        small_at = summing.slots - 1
+        small_at = summing.slots - 3
         steps = small_at + 5
         while slot_at(steps) < total.slots:
             steps += 1
@@ -1297,6 +1353,7 @@
             s = narrow_from + r - lax.div(r, pace)
             wide_too = lax.rem(r, pace) != pace - 1
             settle_all(r - 1)
+            summing.at_stage(r, 0, ahead_of_produce)
 
             @pl.when(r == first_attend)
             def _():
@@ -1520,7 +1577,7 @@
         [any_space] * 25 + [in_vmem] * 5,
         [any_space] * 23,
         [
-            *WideSum.sems(counts),
+            *WideSum.sems(counts, line),
             *NarrowSum.sems(3 * chunks),
             *WideSum.buffers(line, side_rows, cols),
             *NarrowSum.buffers(quarter, width),
@@ -1530,7 +1587,7 @@
             pltpu.VMEM((2, cols, side_rows), f32),
             dma((2 + line,)),
             dma((2 + line,)),
-            dma((4,)),
+            dma((5,)),
             dma((2, 3)),
             dma((2,)),
             dma((3,)),

time: 665 us -> 657 us (0.988)
  Pallas kernels: 639 us -> 631 us
    pallas_call x2, Pallas kernels: 639 us -> 631 us  [call(): pl.pallas_call(kernel, out_shape=out_shape, in_specs=in_specs, out_specs=...]
where the time goes in v5:
time: 657 us; the launch traced here: 653 us
  Pallas kernels  631 us (96%)
  local copies, waits for them, and re-layouts  16 us (2%)
    pallas_call x2, Pallas kernels, call(): pl.pallas_call(kernel, out_shape=out_shape, in_specs=in_specs, out_specs=...  631 us
    unnamed x25, local copies, waits for them, and re-layouts  13.5 us

profile of v5, /device:TPU:0, one launch (start us, length us, event | category | flops | bytes accessed | tf_op | source)
XLA Modules:
  0.0 653.0 jit_solution(1687755925785904688)
XLA Ops:
  0.6 0.8 reduce_window_sum.11
  1.5 0.1 convert_reduce_fusion
  1.6 0.7 subtract_bitcast_fusion
  2.2 0.1 select_reduce_fusion
  2.3 0.2 broadcast_multiply_fusion
  2.6 2.9 sine_multiply_fusion
  5.4 0.6 subtract_subtract_fusion.refs_12_.refs_25_
  6.0 113.6 %shard_map.237 = (bf16[8,2,2,32,2048]{4,3,2,1,0:T(8,128)(2,1)}, bf16[2048,1024]{1,0:T(8,128)(2,1)}, bf16[2048,1024]{1,0:T(8,128)(2,1)}, bf16[2048,1024]{1,0:T(8,...) custom-call(bf16[1024,2048]{1,0:T(8,128)(2,1)} %refs_15_.1, ...), custom_call_target="tpu_custom_call" | custom-call | tf_op jit(solution)/shard_map/pallas_call | solution.py:1448
  119.6 517.3 %shard_map.238 = (bf16[8,2,2,32,2048]{4,3,2,1,0:T(8,128)(2,1)}, bf16[8,2,2,32,2048]{4,3,2,1,0:T(8,128)(2,1)}, f32[256,512]{1,0:T(8,128)}, f32[256,256]{1,0:T(8,1...) custom-call(bf16[1024,2048]{1,0:T(8,128)(2,1)} %bitcast.17, ...), custom_call_target="tpu_custom_call" | custom-call | tf_op jit(solution)/shard_map/pallas_call | solution.py:1448
  636.9 1.3 constant_dynamic-slice_fusion.3
  638.2 1.3 fusion.2
  639.4 0.0 copy-start
  639.4 4.9 copy.36
  644.4 0.0 copy-done
  644.4 0.0 copy-start.5
  644.4 0.0 copy-start.4
  644.4 0.0 copy-start.3
  644.4 2.1 copy.37
  646.5 0.0 copy-done.5
  646.5 0.8 copy.38
  647.3 0.0 copy-done.7
  647.3 0.7 copy.39
  648.0 0.0 copy-done.6
  648.1 0.7 copy.40
  648.8 0.0 copy-done.4
  648.8 0.8 copy.41
  649.6 0.0 copy-done.3
  649.6 1.1 copy.42
  650.7 0.0 copy-done.2
  650.7 1.1 copy.43
  651.8 0.0 copy-done.1
  651.8 1.1 copy.44
  (7 shorter events, 0.0 us)
Async XLA Ops:
  639.4 4.9 copy-start
  644.4 2.2 copy-start.5
  644.4 3.0 copy-start.7
  644.4 3.7 copy-start.6
  644.4 4.4 copy-start.4
  644.4 5.2 copy-start.3
  646.5 4.2 copy-start.2
  647.3 4.5 copy-start.1

commit v6 on v5

--- a/solution.py
+++ b/solution.py
@@ -831,7 +831,7 @@
     wide_buffers, refs = take(refs, 9)
     buffers, refs = take(refs, 7)
     (acts, gains, gain_lands, turned, gain_send, gain_recv, sem, w_sem, store_sem, emit_sem,
-     att_sem, give_sem, other_sem) = refs
+     att_sem, give_sem, other_sem, late_sem) = refs
     me = Spot(wide)
     me.greet(True)
     token_count, width = mlp_in.shape
@@ -847,7 +847,7 @@
     group = q_heads // (kv_width // head)
     scale = head ** (-0.5)
     out_tiles = query_width // cols
-    narrow_from, pace = 2, 6
+    narrow_from, pace = 2, 10
     first_attend = chunks + 4
     heads_at_once = 2
     first_heads = first_attend + q_heads // heads_at_once
@@ -1239,33 +1239,35 @@
             at = pl.ds(pl.multiple_of(c * rows, rows), rows)
             fetch(other_turn, other_t.at[:, at], att_sem.at[0]).wait()
 
+        def left_copies(m, slot):
+            group = left_cut.shape[2]
+            at = pl.ds(pl.multiple_of(m * group, group), group)
+            return (
+                pltpu.make_async_copy(mlp_in_t.at[at, :], left_cut.at[slot, 0], other_sem.at[2 + slot]),
+                pltpu.make_async_copy(other_t.at[at, :], left_cut.at[slot, 1], other_sem.at[4 + slot]),
+            )
+
+        def load_shared(t):
+            for copy in left_copies(0, 0):
+                copy.start()
+            total.give_copy(t).wait()
+            fetch(total.give_land.at[t], total.got, att_sem.at[0])
+
         def put_shared(t, s):
-            total.give_copy(t).wait()
-            load = fetch(total.give_land.at[t], total.got, att_sem.at[0])
+            pltpu.make_async_copy(total.got, total.got, att_sem.at[0]).wait()
+            right[...] = total.got[...].reshape(token_count, cols).astype(bf16)
             mine = acts[lax.rem(t, 2), :, columns(me.side * (blocks // 2) + lax.div(t, 2))]
             group = left_cut.shape[2]
             count = width // group
 
-            def copies(m, slot):
-                at = pl.ds(pl.multiple_of(m * group, group), group)
-                return (
-                    pltpu.make_async_copy(mlp_in_t.at[at, :], left_cut.at[slot, 0], other_sem.at[2 + slot]),
-                    pltpu.make_async_copy(other_t.at[at, :], left_cut.at[slot, 1], other_sem.at[4 + slot]),
-                )
-
-            for copy in copies(0, 0):
-                copy.start()
-            load.wait()
-            right[...] = total.got[...].reshape(token_count, cols).astype(bf16)
-
             def one(m, carry):
                 slot = lax.rem(m, 2)
-                for copy in copies(m, slot):
+                for copy in left_copies(m, slot):
                     copy.wait()
 
                 @pl.when(m + 1 < count)
                 def _():
-                    for copy in copies(m + 1, 1 - slot):
+                    for copy in left_copies(m + 1, 1 - slot):
                         copy.start()
 
                 value = forward_dot(left_cut[slot, 0], mine) + forward_dot(left_cut[slot, 1], right[...])
@@ -1355,12 +1357,17 @@
             settle_all(r - 1)
             summing.at_stage(r, 0, ahead_of_produce)
 
+            @pl.when(r == first_attend - 1)
+            def _():
+                fetch(context, heads.at[:, 0:query_width], late_sem.at[0])
+
             @pl.when(r == first_attend)
             def _():
+                held = heads.at[:, 0:query_width]
+                pltpu.make_async_copy(context, held, late_sem.at[0]).wait()
                 for t in range(out_tiles):
-                    cut = slice(t * cols, (t + 1) * cols)
-                    fetch(context.at[:, cut], right, att_sem.at[0]).wait()
-                    put(late_from + t, right[...])
+                    put(late_from + t, heads[:, t * cols : (t + 1) * cols])
+                fetch(normed_t, left_t, late_sem.at[0])
 
             @pl.when((r >= first_attend) & (r < first_heads))
             def _():
@@ -1372,7 +1379,7 @@
 
             @pl.when(r == first_heads)
             def _():
-                fetch(normed_t, left_t, att_sem.at[0]).wait()
+                pltpu.make_async_copy(normed_t, left_t, late_sem.at[0]).wait()
 
                 def one(t, carry):
                     put(late_from + out_tiles + t, heads[:, columns(t)])
@@ -1391,13 +1398,11 @@
                 for each in range(2):
                     take_other(r * 2 + each)
 
-            @pl.when(wide_too & shared_at(s))
-            def _():
-                put_shared(total.item(s)[1] - 1, s)
-
+            pl.when(wide_too & shared_at(s))(lambda: load_shared(total.item(s)[1] - 1))
             summing.at_stage(r, 2, preload)
             pl.when(wide_too)(lambda: total.fetches(s))
             summing.step(r, produce, work, lower, emit_rows)
+            pl.when(wide_too & shared_at(s))(lambda: put_shared(total.item(s)[1] - 1, s))
 
             @pl.when(wide_too)
             def _():
@@ -1594,6 +1599,7 @@
             dma((1,)),
             dma((4,)),
             dma((10,)),
+            dma((1,)),
         ],
         (
             mlp_in.reshape(token_count, width), mlp_in_t, cotangent, cot_t, normed_t, hidden,

time: 657 us -> 641 us (0.976)
  Pallas kernels: 631 us -> 616 us
    pallas_call x2, Pallas kernels: 631 us -> 616 us  [call(): pl.pallas_call(kernel, out_shape=out_shape, in_specs=in_specs, out_specs=...]
where the time goes in v6:
time: 641 us; the launch traced here: 638 us
  Pallas kernels  616 us (96%)
  local copies, waits for them, and re-layouts  16 us (2%)
    pallas_call x2, Pallas kernels, call(): pl.pallas_call(kernel, out_shape=out_shape, in_specs=in_specs, out_specs=...  616 us
    unnamed x25, local copies, waits for them, and re-layouts  13.5 us

profile of v6, /device:TPU:0, one launch (start us, length us, event | category | flops | bytes accessed | tf_op | source)
XLA Modules:
  0.0 637.7 jit_solution(5590166583507933585)
XLA Ops:
  0.6 0.8 reduce_window_sum.11
  1.5 0.1 convert_reduce_fusion
  1.6 0.7 subtract_bitcast_fusion
  2.2 0.1 select_reduce_fusion
  2.3 0.2 broadcast_multiply_fusion
  2.6 2.9 sine_multiply_fusion
  5.4 0.6 subtract_subtract_fusion.refs_12_.refs_25_
  6.0 113.6 %shard_map.237 = (bf16[8,2,2,32,2048]{4,3,2,1,0:T(8,128)(2,1)}, bf16[2048,1024]{1,0:T(8,128)(2,1)}, bf16[2048,1024]{1,0:T(8,128)(2,1)}, bf16[2048,1024]{1,0:T(8,...) custom-call(bf16[1024,2048]{1,0:T(8,128)(2,1)} %refs_15_.1, ...), custom_call_target="tpu_custom_call" | custom-call | tf_op jit(solution)/shard_map/pallas_call | solution.py:1453
  119.6 502.1 %shard_map.238 = (bf16[8,2,2,32,2048]{4,3,2,1,0:T(8,128)(2,1)}, bf16[8,2,2,32,2048]{4,3,2,1,0:T(8,128)(2,1)}, f32[256,512]{1,0:T(8,128)}, f32[256,256]{1,0:T(8,1...) custom-call(bf16[1024,2048]{1,0:T(8,128)(2,1)} %bitcast.17, ...), custom_call_target="tpu_custom_call" | custom-call | tf_op jit(solution)/shard_map/pallas_call | solution.py:1453
  621.7 1.3 constant_dynamic-slice_fusion.3
  622.9 1.3 fusion.2
  624.2 0.0 copy-start
  624.2 4.9 copy.36
  629.1 0.0 copy-done
  629.1 0.0 copy-start.5
  629.1 0.0 copy-start.4
  629.1 0.0 copy-start.3
  629.2 2.1 copy.37
  631.3 0.0 copy-done.5
  631.3 0.8 copy.38
  632.1 0.0 copy-done.7
  632.1 0.7 copy.39
  632.8 0.0 copy-done.6
  632.8 0.7 copy.40
  633.5 0.0 copy-done.4
  633.5 0.8 copy.41
  634.3 0.0 copy-done.3
  634.3 1.1 copy.42
  635.4 0.0 copy-done.2
  635.4 1.1 copy.43
  636.6 0.0 copy-done.1
  636.6 1.1 copy.44
  (7 shorter events, 0.0 us)
Async XLA Ops:
  624.2 4.9 copy-start
  629.1 2.2 copy-start.5
  629.1 3.0 copy-start.7
  629.1 3.7 copy-start.6
  629.1 4.4 copy-start.4
  629.1 5.2 copy-start.3
  631.3 4.2 copy-start.2
  632.1 4.5 copy-start.1

commit v7 on v6

--- a/solution.py
+++ b/solution.py
@@ -567,7 +567,7 @@
         c = s - number
         pl.when((c >= 0) & (c < self.chunks))(lambda: body(c))
 
-    def step(self, s, produce, work, lower, emit, beside=None):
+    def step(self, s, produce, work, lower, emit, beside=None, only=(4, 3, 2, 1, 0)):
         me = self.me
 
         def stage(number, body):
@@ -598,11 +598,8 @@
         def zero(c, slot, third):
             pl.when(slot == 0)(lambda: produce(c, self.part))
 
-        stage(4, four)
-        stage(3, three)
-        stage(2, two)
-        stage(1, one)
-        stage(0, zero)
+        for number in only:
+            stage(number, (zero, one, two, three, four)[number])
 
 
 def take(refs, count):
@@ -1401,13 +1398,14 @@
             pl.when(wide_too & shared_at(s))(lambda: load_shared(total.item(s)[1] - 1))
             summing.at_stage(r, 2, preload)
             pl.when(wide_too)(lambda: total.fetches(s))
-            summing.step(r, produce, work, lower, emit_rows)
+            summing.step(r, produce, work, lower, emit_rows, only=(4, 3, 2, 1))
             pl.when(wide_too & shared_at(s))(lambda: put_shared(total.item(s)[1] - 1, s))
 
             @pl.when(wide_too)
             def _():
                 total.sums(s, emit_tile, emit_shared)
 
+            summing.step(r, produce, work, lower, emit_rows, only=(0,))
             pl.when(r >= small_at)(lambda: small.step(r - small_at))
             return carry
 

time: 641 us -> 640 us (level)
  no operation moved by 1% of the time
where the time goes in v7:
time: 640 us; the launch traced here: 636 us
  Pallas kernels  614 us (96%)
  local copies, waits for them, and re-layouts  16 us (2%)
    pallas_call x2, Pallas kernels, call(): pl.pallas_call(kernel, out_shape=out_shape, in_specs=in_specs, out_specs=...  614 us
    unnamed x25, local copies, waits for them, and re-layouts  13.5 us

profile of v7, /device:TPU:0, one launch (start us, length us, event | category | flops | bytes accessed | tf_op | source)
XLA Modules:
  0.0 636.0 jit_solution(10890095349651044899)
XLA Ops:
  0.6 0.8 reduce_window_sum.11
  1.5 0.1 convert_reduce_fusion
  1.6 0.7 subtract_bitcast_fusion
  2.2 0.1 select_reduce_fusion
  2.3 0.2 broadcast_multiply_fusion
  2.6 2.9 sine_multiply_fusion
  5.4 0.6 subtract_subtract_fusion.refs_12_.refs_25_
  6.0 113.6 %shard_map.237 = (bf16[8,2,2,32,2048]{4,3,2,1,0:T(8,128)(2,1)}, bf16[2048,1024]{1,0:T(8,128)(2,1)}, bf16[2048,1024]{1,0:T(8,128)(2,1)}, bf16[2048,1024]{1,0:T(8,...) custom-call(bf16[1024,2048]{1,0:T(8,128)(2,1)} %refs_15_.1, ...), custom_call_target="tpu_custom_call" | custom-call | tf_op jit(solution)/shard_map/pallas_call | solution.py:1451
  119.6 500.3 %shard_map.238 = (bf16[8,2,2,32,2048]{4,3,2,1,0:T(8,128)(2,1)}, bf16[8,2,2,32,2048]{4,3,2,1,0:T(8,128)(2,1)}, f32[256,512]{1,0:T(8,128)}, f32[256,256]{1,0:T(8,1...) custom-call(bf16[1024,2048]{1,0:T(8,128)(2,1)} %bitcast.17, ...), custom_call_target="tpu_custom_call" | custom-call | tf_op jit(solution)/shard_map/pallas_call | solution.py:1451
  619.9 1.3 constant_dynamic-slice_fusion.3
  621.2 1.3 fusion.2
  622.4 0.0 copy-start
  622.5 4.9 copy.36
  627.4 0.0 copy-done
  627.4 0.0 copy-start.5
  627.4 0.0 copy-start.4
  627.4 0.0 copy-start.3
  627.4 2.1 copy.37
  629.6 0.0 copy-done.5
  629.6 0.8 copy.38
  630.4 0.0 copy-done.7
  630.4 0.7 copy.39
  631.1 0.0 copy-done.6
  631.1 0.7 copy.40
  631.8 0.0 copy-done.4
  631.8 0.8 copy.41
  632.6 0.0 copy-done.3
  632.6 1.1 copy.42
  633.7 0.0 copy-done.2
  633.7 1.1 copy.43
  634.9 0.0 copy-done.1
  634.9 1.1 copy.44
  (7 shorter events, 0.0 us)
Async XLA Ops:
  622.4 4.9 copy-start
  627.4 2.2 copy-start.5
  627.4 3.0 copy-start.7
  627.4 3.7 copy-start.6
  627.4 4.4 copy-start.4
  627.4 5.2 copy-start.3
  629.6 4.2 copy-start.2
  630.4 4.5 copy-start.1
